TPU v7x, 32 devices: a whole 2x2x4 slice. The times are simulated.
32 devices in a mesh: dp: 4 (over y, x), ctx: 2 (over core), head: 4 (over z).
Axes of the slice: x: 2, y: 2, z: 4, core: 2. Of those that a mesh axis runs over, the one named last changes fastest.
Arguments:
- inputs: bfloat16 [4, 256, 4096], P('dp', 'ctx', 'head'), may hold values from -6 to 6
- step_rate: float32 [4, 256, 4096], P('dp', 'ctx', 'head'), may hold values from 0 to 12
- key_rows: bfloat16 [4, 256, 16], P('dp', 'ctx'), may hold values from -5 to 5
- query_rows: bfloat16 [4, 256, 16], P('dp', 'ctx'), may hold values from -1.5 to 1.5
- grad_out: bfloat16 [4, 256, 4096], P('dp', 'ctx', 'head'), may hold values from -6 to 6
Outputs:
- grad_inputs: bfloat16 [4, 256, 4096], P('dp', ('ctx', 'head'))
- grad_rate: bfloat16 [4, 256, 4096], P('dp', ('ctx', 'head'))
- grad_keys: float32 [4, 256, 16], P('dp', ('ctx', 'head'))
- grad_queries: float32 [4, 256, 16], P('dp', ('ctx', 'head'))
All inputs are finite; a program needn't handle non-finite values.
Results may differ from a plain program's by a relative error of at most 0.0018.
Values may be sent and summed in bfloat16 or wider, within the bound.
No kernel may reach another device: no remote copies, remote signals or barrier semaphores. Data moves between devices by JAX's collectives and lax.ppermute only.
A program may use at most 64 MiB of HBM per device.

v0:
```python
import functools

import jax
import jax.numpy as jnp
from jax import lax
from jax.experimental import pallas as pl
from jax.experimental.pallas import tpu as pltpu
from jax.sharding import PartitionSpec as P

BLOCK = 16
LANES = 128
SUB = 8
UNROLL = 8
CHUNKS = 1
VMEM_LIMIT = 20 * 1024 * 1024


def affine(earlier, subsequent):
    return (earlier[0] * subsequent[0], subsequent[0] * earlier[1] + subsequent[1])


def prefix(array, axis, identity, reverse):
    size, position = (lax.axis_size(axis), lax.axis_index(axis))
    everything = jax.tree.map(lambda part: lax.all_gather(part, axis), array)
    start = jax.tree.map(
        lambda part, zero: jnp.broadcast_to(jnp.asarray(zero, part.dtype), part.shape),
        array,
        identity,
    )

    def hop(k, before):
        at = size - 1 - k if reverse else k
        reached = at > position if reverse else at < position
        new = affine(before, jax.tree.map(lambda part: part[at], everything))
        return jax.tree.map(lambda a, b: jnp.where(reached, a, b), new, before)

    return lax.fori_loop(0, size, hop, start)


def group_summary(inputs, step_rate, key_rows, query_rows, grad_out):
    tokens, channels = inputs.shape[1:]
    state_dim = key_rows.shape[2]
    num_blocks = tokens // BLOCK

    def to_blocks(array_in):
        return array_in[0].astype(jnp.float32).reshape(num_blocks, BLOCK, array_in.shape[2])

    def summarize(carried, block_in):
        x, rate, key_blk, query_blk, grad_blk = block_in
        keys_sq = key_blk * key_blk
        step = rate / (1.0 + rate * jnp.sum(keys_sq, axis=1)[:, None])
        decays = 1.0 - step[:, None, :] * keys_sq[:, :, None]
        drives = (step * x)[:, None, :] * key_blk[:, :, None]
        before = jnp.cumprod(decays, axis=0)
        suffix = jnp.cumprod(decays[::-1], axis=0)[::-1]
        after = jnp.concatenate([suffix[1:], jnp.ones_like(decays[:1])], axis=0)
        total = before[-1]
        end = jnp.sum(drives * after, axis=0)
        back = jnp.sum(grad_blk[:, None, :] * query_blk[:, :, None] * before, axis=0)
        return (
            carried[0] * total,
            total * carried[1] + end,
            carried[2] + carried[0] * back,
        ), None

    zero = jnp.zeros((state_dim, channels), jnp.float32)
    blocked = tuple(map(to_blocks, (inputs, step_rate, key_rows, query_rows, grad_out)))
    return lax.scan(summarize, (jnp.ones_like(zero), zero, zero), blocked)[0]


def columns(matrix, base):
    rows, tokens = matrix.shape
    turned = pltpu.roll(matrix, lax.rem(tokens - base, tokens), 1)
    return [jnp.broadcast_to(turned[:, u : u + 1], (rows, LANES)) for u in range(UNROLL)]


def halves(value):
    return [value[at : at + SUB] for at in range(0, value.shape[0], SUB)]


def row(ref, tile, t):
    return ref[tile, pl.ds(t, SUB, stride=0), :]


def tile_at(j):
    return pl.ds(j * LANES, LANES)


def lane_sums(values):
    ones = jnp.ones((SUB, LANES), jnp.bfloat16)

    def product(part):
        return lax.dot_general(
            ones, part, (((1,), (1,)), ((), ())), preferred_element_type=jnp.float32
        )

    high = values.astype(jnp.bfloat16)
    low = (values - high.astype(jnp.float32)).astype(jnp.bfloat16)
    return product(high) + product(low)


def first_kernel(backwards, has_entry, *refs):
    x_ref, rate_ref, key_ref, query_ref, go_ref = refs[:5]
    entry_ref = refs[5] if has_entry else None
    path_ref, end_ref, rows_ref, step_ref, drive_ref, x32_ref, go32_ref, inverse_ref = refs[
        5 + has_entry :
    ]
    states, tokens = key_ref.shape[1:]
    tiles = x_ref.shape[2] // LANES
    key = key_ref[0].astype(jnp.float32)
    query = query_ref[0].astype(jnp.float32)
    rows_ref[0] = key
    rows_ref[1] = query
    key_norm = jnp.sum(key * key, axis=0, keepdims=True)
    norm = jnp.transpose(jnp.broadcast_to(key_norm, (LANES, tokens)))
    for j in range(tiles):
        rate = rate_ref[0, :, tile_at(j)]
        x = x_ref[0, :, tile_at(j)].astype(jnp.float32)
        inverse = 1.0 / (1.0 + rate * norm)
        step = rate * inverse
        inverse_ref[j, :tokens] = inverse
        step_ref[j, :tokens] = step
        x32_ref[j, :tokens] = x
        drive_ref[j, :tokens] = step * x
        go32_ref[j, :tokens] = go_ref[0, :, tile_at(j)].astype(jnp.float32)

    if has_entry:
        entry = [halves(entry_ref[:, tile_at(j)]) for j in range(tiles)]
    else:
        entry = [[jnp.zeros((SUB, LANES), jnp.float32)] * (states // SUB)] * tiles

    def finish(state):
        for j in range(tiles):
            end_ref[:, tile_at(j)] = jnp.concatenate(state[j], axis=0)

    def run_states():
        def block(b, state):
            base = b * UNROLL
            keys = columns(key, base)
            state = [list(part) for part in state]
            for u in range(UNROLL):
                k = halves(keys[u])
                k2 = [part * part for part in k]
                for j in range(tiles):
                    step = row(step_ref, j, base + u)
                    drive = row(drive_ref, j, base + u)
                    for h in range(len(k)):
                        state[j][h] = (1.0 - step * k2[h]) * state[j][h] + drive * k[h]
                        path_ref[base + u, pl.ds(h * SUB, SUB), tile_at(j)] = state[j][h]
            return state

        finish(lax.fori_loop(0, tokens // UNROLL, block, entry))

    def run_grads():
        def block(i, state):
            base = tokens - UNROLL - i * UNROLL
            keys = columns(key, base)
            queries = columns(query, base)
            state = [list(part) for part in state]
            for u in reversed(range(UNROLL)):
                k2 = [part * part for part in halves(keys[u])]
                q = halves(queries[u])
                for j in range(tiles):
                    step = row(step_ref, j, base + u)
                    go = row(go32_ref, j, base + u)
                    for h in range(len(q)):
                        grad = go * q[h] + state[j][h]
                        path_ref[base + u, pl.ds(h * SUB, SUB), tile_at(j)] = grad
                        state[j][h] = (1.0 - step * k2[h]) * grad
            return state

        finish(lax.fori_loop(0, tokens // UNROLL, block, entry))

    choose(backwards, run_grads, run_states)


def choose(flag, if_set, if_not):
    if flag is None:
        group = lax.axis_index("ctx")
        pl.when(group != 0)(if_set)
        pl.when(group == 0)(if_not)
    else:
        (if_set if flag else if_not)()


def second_kernel(onwards_here, last, heads, has_start, has_before, *refs):
    refs = list(refs)
    entry_ref, path_ref, rows_ref, step_ref, drive_ref, x32_ref, go32_ref, inverse_ref = refs[:8]
    del refs[:8]
    start_ref = refs.pop(0) if has_start else None
    before_ref = refs.pop(0) if has_before else None
    message_ref, sums_ref, dot_ref, weighted_ref, key_part_ref, query_part_ref, norm_ref = refs
    states, tokens = rows_ref.shape[1:]
    tiles = step_ref.shape[0]
    width = tiles * LANES
    key = rows_ref[0]
    query = rows_ref[1]
    pair = range(states // SUB)

    def path_at(t, h, j):
        return path_ref[t, pl.ds(h * SUB, SUB), tile_at(j)]

    def step_through(back, advance):
        def block(i, state):
            base = tokens - UNROLL - i * UNROLL if back else i * UNROLL
            keys = columns(key, base)
            queries = columns(query, base)
            state = [list(part) for part in state]
            for u in reversed(range(UNROLL)) if back else range(UNROLL):
                t = base + u
                k, q = halves(keys[u]), halves(queries[u])
                k2 = [part * part for part in k]
                sums = None
                for j in range(tiles):
                    step, drive, go = (
                        row(ref, j, t) for ref in (step_ref, drive_ref, go32_ref)
                    )
                    dots, weights, terms = [], [], []
                    for h in pair:
                        decay = 1.0 - step * k2[h]
                        grad, here, previous, state[j][h] = advance(
                            t, u, h, j, state[j][h], decay, drive, go, k[h], q[h]
                        )
                        weight = grad * previous
                        dots.append(grad * k[h])
                        weights.append(weight * k2[h])
                        terms += [grad * drive, weight * step, here * go]
                    dot_ref[j, pl.ds(pl.multiple_of(t * SUB, SUB), SUB), :] = sum(dots[1:], dots[0])
                    weighted_ref[j, pl.ds(pl.multiple_of(t * SUB, SUB), SUB), :] = sum(
                        weights[1:], weights[0]
                    )
                    sums = terms if j == 0 else [a + b for a, b in zip(sums, terms)]
                for h in pair:
                    by_drive, by_decay, by_query = sums[3 * h : 3 * h + 3]
                    at = pl.ds(pl.multiple_of(t * states + h * SUB, SUB), SUB)
                    key_part_ref[at, :] = by_drive - (2.0 * k[h]) * by_decay
                    query_part_ref[at, :] = by_query
            return state

        entry = [halves(entry_ref[:, tile_at(j)]) for j in range(tiles)]
        lax.fori_loop(0, tokens // UNROLL, block, entry)

    def backwards(t, u, h, j, state, decay, drive, go, k, q):
        grad = go * q + state
        earlier = path_at(jnp.maximum(t - 1, 0), h, j)
        if u == 0:
            start = start_ref[pl.ds(h * SUB, SUB), tile_at(j)] if has_start else 0.0
            earlier = jnp.where(t == 0, start, earlier)
        return grad, path_at(t, h, j), earlier, decay * grad

    def onwards(t, u, h, j, state, decay, drive, go, k, q):
        here = decay * state + drive * k
        return path_at(t, h, j), here, state, here

    choose(onwards_here, lambda: step_through(False, onwards), lambda: step_through(True, backwards))

    part = tokens // heads
    rows = 2 * SUB

    def finish(i, _):
        base = pl.multiple_of(i * rows, rows)
        to = pl.ds(pl.multiple_of(lax.rem(base, part), rows), rows)
        head = lax.div(base, part)
        norm_sum = None
        for j in range(tiles):
            dot, weighted = (
                sum(ref[j, pl.ds(base * SUB + s, rows, stride=SUB), :] for s in range(SUB))
                for ref in (dot_ref, weighted_ref)
            )
            step, x, inverse = (
                ref[j, pl.ds(base, rows), :] for ref in (step_ref, x32_ref, inverse_ref)
            )
            grad_step = x * dot - weighted
            message_ref[head, to, tile_at(j)] = (step * dot).astype(jnp.bfloat16)
            message_ref[head, to, tile_at(tiles + j)] = (grad_step * inverse * inverse).astype(
                jnp.bfloat16
            )
            term = grad_step * step * step
            norm_sum = term if j == 0 else norm_sum + term
        norm_ref[pl.ds(base, rows), :] = norm_sum
        return _

    lax.fori_loop(0, tokens // rows, finish, 0)
    norm_row = lane_sums(norm_ref[...])[:1]
    for n in range(states):
        at = pl.ds(n, tokens, stride=states)
        sums_ref[n : n + 1, :] = lane_sums(key_part_ref[at, :])[:1]
        sums_ref[states + n : states + n + 1, :] = lane_sums(query_part_ref[at, :])[:1]
    sums_ref[:states] = sums_ref[:states] - 2.0 * key * norm_row
    if has_before:
        sums_ref[...] = sums_ref[...] + before_ref[...]
    if last:
        quarters = 2 * states // SUB
        lane = lax.broadcasted_iota(jnp.int32, (SUB, tokens), 1) // part
        for h in range(heads):
            packed = None
            for i in range(quarters):
                turned = pltpu.roll(sums_ref[SUB * i : SUB * i + SUB], ((i - h) * part) % tokens, 1)
                packed = turned if packed is None else jnp.where(lane == i, turned, packed)
            high = packed.astype(jnp.bfloat16).astype(jnp.float32)
            both = jnp.concatenate([high, packed - high], axis=0).astype(jnp.bfloat16)
            message_ref[h, :rows, pl.ds(2 * width, LANES)] = both
            message_ref[h, rows:, pl.ds(2 * width, LANES)] = jnp.zeros(
                (part - rows, LANES), jnp.bfloat16
            )


def gather_kernel(heads, chunks, *refs):
    messages, (in_ref, rate_ref, key_ref, query_ref) = refs[:chunks], refs[chunks:]
    states, part = key_ref.shape[1:]
    channels = in_ref.shape[2] // heads
    width = channels // chunks
    total = None
    for s in range(heads):
        for c, message in enumerate(messages):
            to = pl.ds(s * channels + c * width, width)
            in_ref[0, :, to] = message[s, :, pl.ds(0, width)]
            rate_ref[0, :, to] = message[s, :, pl.ds(width, width)]
        both = messages[-1][s, :16, pl.ds(2 * width, LANES)].astype(jnp.float32)
        both = both[:8] + both[8:]
        total = both if total is None else total + both
    for i in range(states // 8):
        key_ref[0, 8 * i : 8 * i + 8] = total[:, i * part : (i + 1) * part]
        at = states // 8 + i
        query_ref[0, 8 * i : 8 * i + 8] = total[:, at * part : (at + 1) * part]


def shards(inputs, step_rate, key_rows, query_rows, grad_out):
    _, tokens, channels = inputs.shape
    states = key_rows.shape[2]
    heads = lax.axis_size("head")
    groups = lax.axis_size("ctx")
    width = channels // CHUNKS
    part = tokens // heads
    key_cols = jnp.swapaxes(key_rows, 1, 2)
    query_cols = jnp.swapaxes(query_rows, 1, 2)
    f32 = jnp.float32
    params = pltpu.CompilerParams(vmem_limit_bytes=VMEM_LIMIT)
    whole = pl.BlockSpec(memory_space=pltpu.VMEM)
    plane = pltpu.VMEM((width // LANES, tokens + SUB, LANES), f32)

    def first(c, backwards, entry=None):
        wide = pl.BlockSpec((1, tokens, width), lambda i: (0, 0, c))
        specs = [wide, wide, whole, whole, wide]
        arrays = [inputs, step_rate, key_cols, query_cols, grad_out]
        if entry is not None:
            specs, arrays = specs + [whole], arrays + [entry]
        return pl.pallas_call(
            functools.partial(first_kernel, backwards, entry is not None),
            grid=(1,),
            in_specs=specs,
            out_specs=[whole] * 8,
            out_shape=[
                pltpu.VMEM((tokens, states, width), f32),
                jax.ShapeDtypeStruct((states, width), f32),
                pltpu.VMEM((2, states, tokens), f32),
            ]
            + [plane] * 5,
            compiler_params=params,
        )(*arrays)

    def second(c, onwards_here, entry, carried, start, before):
        last = c == CHUNKS - 1
        wide_message = 2 * width + (LANES if last else 0)
        extra = [a for a in (start, before) if a is not None]
        parts = pltpu.VMEM((width // LANES, (tokens + 1) * SUB, LANES), f32)
        sums = pltpu.VMEM(((tokens + 1) * states, LANES), f32)
        return pl.pallas_call(
            functools.partial(
                second_kernel, onwards_here, last, heads, start is not None, before is not None
            ),
            in_specs=[whole] * (8 + len(extra)),
            out_specs=[whole, whole],
            out_shape=[
                jax.ShapeDtypeStruct((heads, part, wide_message), jnp.bfloat16),
                pltpu.VMEM((2 * states, tokens), f32),
            ],
            scratch_shapes=[parts, parts, sums, sums, pltpu.VMEM((tokens, LANES), f32)],
            compiler_params=params,
        )(entry, *carried, *extra)

    work = []
    if groups == 2:
        here = None
        for c in range(CHUNKS):
            path, end, *carried = first(c, here)
            entry = lax.ppermute(end, "ctx", [(0, 1), (1, 0)])
            work.append((entry, [path] + carried, None))
    else:
        here = False
        product, end, back = group_summary(inputs, step_rate, key_rows, query_rows, grad_out)
        unit = (jnp.ones_like(product), jnp.zeros_like(product))
        starts = prefix((product, end), "ctx", unit, False)[1]
        entries = prefix((product, back), "ctx", unit, True)[1]
        for c in range(CHUNKS):
            at = slice(c * width, (c + 1) * width)
            path, _, *carried = first(c, here, starts[:, at])
            work.append((entries[:, at], [path] + carried, starts[:, at]))

    sums = None
    arrived = []
    for c, (entry, carried, start) in enumerate(work):
        message, sums = second(c, here, entry, carried, start, sums)
        arrived.append(lax.all_to_all(message, "head", split_axis=0, concat_axis=0, tiled=True))

    grad_in, grad_rate, grad_key, grad_query = pl.pallas_call(
        functools.partial(gather_kernel, heads, CHUNKS),
        in_specs=[whole] * CHUNKS,
        out_specs=[whole] * 4,
        out_shape=[
            jax.ShapeDtypeStruct((1, part, heads * channels), jnp.bfloat16),
            jax.ShapeDtypeStruct((1, part, heads * channels), jnp.bfloat16),
            jax.ShapeDtypeStruct((1, states, part), f32),
            jax.ShapeDtypeStruct((1, states, part), f32),
        ],
        compiler_params=params,
    )(*arrived)
    return (grad_in, grad_rate, jnp.swapaxes(grad_key, 1, 2), jnp.swapaxes(grad_query, 1, 2))


def solution(mesh):
    placed = (
        P("dp", "ctx", "head"),
        P("dp", "ctx", "head"),
        P("dp", "ctx", None),
        P("dp", "ctx", None),
        P("dp", "ctx", "head"),
    )
    spread = P("dp", ("ctx", "head"), None)
    return jax.shard_map(
        shards, mesh=mesh, in_specs=placed, out_specs=(spread,) * 4, check_vma=False
    )
```

profile of v0, /device:TPU:0, one launch (start us, length us, event | category | flops | bytes accessed | tf_op | source)
XLA Modules:
  0.0 42.7 jit_solution(817866372869872092)
XLA Ops:
  0.6 0.0 copy-start
  0.6 1.0 %copy-done = f32[1,128,1024]{2,1,0:T(8,128)S(1)} copy-done((f32[1,128,1024]{2,1,0:T(8,128)S(1)}, f32[1,128,1024]{2,1,0:T(8,128)}, u32[]{:S(2)}) %copy-start) | copy-done | bytes 524312
  1.7 0.0 copy-start.1
  1.7 0.9 %copy-done.1 = bf16[1,128,1024]{2,1,0:T(8,128)(2,1)S(1)} copy-done((bf16[1,128,1024]{2,1,0:T(8,128)(2,1)S(1)}, bf16[1,128,1024]{2,1,0:T(8,128)(2,1)}, u32[]{:S(2)}) %copy-start.1) | copy-done | bytes 262168
  2.6 0.0 copy-start.2
  2.6 0.9 %copy-done.2 = bf16[1,128,1024]{2,1,0:T(8,128)(2,1)S(1)} copy-done((bf16[1,128,1024]{2,1,0:T(8,128)(2,1)S(1)}, bf16[1,128,1024]{2,1,0:T(8,128)(2,1)}, u32[]{:S(2)}) %copy-start.2) | copy-done | bytes 262168
  3.6 0.0 copy-start.3
  3.6 0.7 %copy-done.3 = bf16[1,128,16]{1,2,0:T(8,128)(2,1)S(1)} copy-done((bf16[1,128,16]{1,2,0:T(8,128)(2,1)S(1)}, bf16[1,128,16]{1,2,0:T(8,128)(2,1)}, u32[]{:S(2)}) %copy-start.3) | copy-done | bytes 4120
  4.3 0.0 copy-start.4
  4.3 0.7 %copy-done.4 = bf16[1,128,16]{1,2,0:T(8,128)(2,1)S(1)} copy-done((bf16[1,128,16]{1,2,0:T(8,128)(2,1)S(1)}, bf16[1,128,16]{1,2,0:T(8,128)(2,1)}, u32[]{:S(2)}) %copy-start.4) | copy-done | bytes 4120
  5.0 4.1 %shard_map.84 = (f32[128,16,1024]{2,1,0:T(8,128)S(1)}, f32[16,1024]{1,0:T(8,128)S(1)}, f32[2,16,128]{2,1,0:T(8,128)S(1)}, f32[8,136,128]{2,1,0:T(8,128)S(1)}, f3...) custom-call(bf16[1,128,1024]{2,1,0:T(8,128)(2,1)S(1)} %copy-done.1, ...), custom_call_target="tpu_custom_call" | custom-call | tf_op jit(solution)/shard_map/pallas_call | solution.py:348
  9.0 0.5 %collective-permute-start = (f32[16,1024]{1,0:T(8,128)S(1)}, f32[16,1024]{1,0:T(8,128)S(1)}, u32[]{:S(2)}, u32[]{:S(2)}) collective-permute-start(f32[16,1024]{1,0:T(8,128)S(1)} %get-tuple-element.17), channel_id=1, source_target_pairs={{0,4},{4,0},{1,5},{5,1},{2,6},{6,2},{3,7},{7,3},{8,12},{12,8},{9,1... | collective-permute-start | bytes 196616 | tf_op jit(solution)/shard_map/ppermute | solution.py:387
  9.6 0.9 %collective-permute-done.refs_0_ = f32[16,1024]{1,0:T(8,128)S(1)} collective-permute-done((f32[16,1024]{1,0:T(8,128)S(1)}, f32[16,1024]{1,0:T(8,128)S(1)}, u32[]{:S(2)}, u32[]{:S(2)}) %collective-permute-start) | collective-permute-done | bytes 65568 | tf_op jit(solution)/shard_map/ppermute | solution.py:387
  10.5 9.8 %shard_map.85 = (bf16[4,32,2176]{2,1,0:T(8,128)(2,1)S(1)}, f32[32,128]{1,0:T(8,128)}) custom-call(f32[16,1024]{1,0:T(8,128)S(1)} %collective-permute-done.refs_0_, f32[128,16,1024]{2,1,0:T(8,128)S(1)} %get-tuple-element.18.refs_1_, f32[2,16,128]{2,1,0:T(8,128)S(1)} %get-tuple-element.19.refs_2_, f32[8,136,128]{2,1,0:T(8,128)S(1)} %get-tuple-element.20.refs_3_, ...), custom_call_target="tpu_custom_call" | custom-call | tf_op jit(solution)/shard_map/pallas_call | solution.py:368
  20.3 21.6 %all_to_all.5.refs_0_ = bf16[4,32,2176]{2,1,0:T(8,128)(2,1)S(1)} all-to-all(bf16[4,32,2176]{2,1,0:T(8,128)(2,1)S(1)} %get-tuple-element.25), channel_id=1, replica_groups=mesh['dp'=4,'ctx'=2,'head'=4] {'head'}, dimensions={0} | all-to-all | bytes 1114112 | tf_op jit(solution)/shard_map/all_to_all | solution.py:404
  41.9 0.8 %shard_map.86 = (bf16[1,32,4096]{2,1,0:T(8,128)(2,1)}, bf16[1,32,4096]{2,1,0:T(8,128)(2,1)}, f32[1,16,32]{2,1,0:T(8,128)}, f32[1,16,32]{2,1,0:T(8,128)}) custom-call(bf16[4,32,2176]{2,1,0:T(8,128)(2,1)S(1)} %all_to_all.5.refs_0_), custom_call_target="tpu_custom_call" | custom-call | tf_op jit(solution)/shard_map/pallas_call | solution.py:406
Async XLA Ops:
  0.6 1.0 %copy-start = (f32[1,128,1024]{2,1,0:T(8,128)S(1)}, f32[1,128,1024]{2,1,0:T(8,128)}, u32[]{:S(2)}) copy-start(f32[1,128,1024]{2,1,0:T(8,128)} %refs_1_.1) | copy-start | bytes 1572868
  1.7 0.9 %copy-start.1 = (bf16[1,128,1024]{2,1,0:T(8,128)(2,1)S(1)}, bf16[1,128,1024]{2,1,0:T(8,128)(2,1)}, u32[]{:S(2)}) copy-start(bf16[1,128,1024]{2,1,0:T(8,128)(2,1)} %refs_0_.1) | copy-start | bytes 786436
  2.6 0.9 %copy-start.2 = (bf16[1,128,1024]{2,1,0:T(8,128)(2,1)S(1)}, bf16[1,128,1024]{2,1,0:T(8,128)(2,1)}, u32[]{:S(2)}) copy-start(bf16[1,128,1024]{2,1,0:T(8,128)(2,1)} %refs_4_.1) | copy-start | bytes 786436
  3.6 0.7 %copy-start.3 = (bf16[1,128,16]{1,2,0:T(8,128)(2,1)S(1)}, bf16[1,128,16]{1,2,0:T(8,128)(2,1)}, u32[]{:S(2)}) copy-start(bf16[1,128,16]{1,2,0:T(8,128)(2,1)} %param.7) | copy-start | bytes 12292
  4.3 0.7 %copy-start.4 = (bf16[1,128,16]{1,2,0:T(8,128)(2,1)S(1)}, bf16[1,128,16]{1,2,0:T(8,128)(2,1)}, u32[]{:S(2)}) copy-start(bf16[1,128,16]{1,2,0:T(8,128)(2,1)} %param.8) | copy-start | bytes 12292
  9.0 1.4 %collective-permute-start = (f32[16,1024]{1,0:T(8,128)S(1)}, f32[16,1024]{1,0:T(8,128)S(1)}, u32[]{:S(2)}, u32[]{:S(2)}) collective-permute-start(f32[16,1024]{1,0:T(8,128)S(1)} %get-tuple-element.17), channel_id=1, source_target_pairs={{0,4},{4,0},{1,5},{5,1},{2,6},{6,2},{3,7},{7,3},{8,12},{12,8},{9,1... | collective-permute-start | bytes 196616 | tf_op jit(solution)/shard_map/ppermute | solution.py:387
where the time goes:
time: 43 us; the launch traced here: 42.7 us
  blocking collectives  21.6 us (50%)
  Pallas kernels  14.7 us (34%)
  local copies, waits for them, and re-layouts  4.31 us (10%)
  waiting for transfers between devices  0.9 us (2%)
  between operations  0.65 us (2%)
  starting transfers between devices  0.52 us (1%)
    all_to_all x1, blocking collectives, shards(): lax.all_to_all(message, 'head', split_axis=0, concat_axis=0, tiled=True)  21.6 us
    pallas_call x1, Pallas kernels, second(): pl.pallas_call(functools.partial(second_kernel, onwards_here, last, heads...  9.82 us
    unnamed x10, local copies, waits for them, and re-layouts  4.31 us
    pallas_call x1, Pallas kernels, first(): pl.pallas_call(functools.partial(first_kernel, backwards, entry is not No...  4.09 us
    ppermute x1, waiting for transfers between devices, shards(): entry = lax.ppermute(end, 'ctx', [(0, 1), (1, 0)])  0.9 us
  transfers between devices with their start and end apart: 1, of which 1 were waited for; matrix products, arithmetic and copies ran while one was open for 0% of the time, Pallas kernels for 0%

commit v1 on v0

--- a/solution.py
+++ b/solution.py
@@ -11,7 +11,7 @@
 LANES = 128
 SUB = 8
 UNROLL = 8
-CHUNKS = 1
+CHUNKS = 2
 VMEM_LIMIT = 20 * 1024 * 1024
 
 
@@ -68,10 +68,10 @@
     return lax.scan(summarize, (jnp.ones_like(zero), zero, zero), blocked)[0]
 
 
-def columns(matrix, base):
+def spread_columns(matrix, table_ref):
     rows, tokens = matrix.shape
-    turned = pltpu.roll(matrix, lax.rem(tokens - base, tokens), 1)
-    return [jnp.broadcast_to(turned[:, u : u + 1], (rows, LANES)) for u in range(UNROLL)]
+    for t in range(tokens):
+        table_ref[t] = jnp.broadcast_to(matrix[:, t : t + 1], (rows, LANES))
 
 
 def halves(value):
@@ -99,18 +99,20 @@
     return product(high) + product(low)
 
 
-def first_kernel(backwards, has_entry, *refs):
+def first_kernel(backwards, has_entry, has_tables, *refs):
+    refs = list(refs)
     x_ref, rate_ref, key_ref, query_ref, go_ref = refs[:5]
-    entry_ref = refs[5] if has_entry else None
-    path_ref, end_ref, rows_ref, step_ref, drive_ref, x32_ref, go32_ref, inverse_ref = refs[
-        5 + has_entry :
-    ]
+    del refs[:5]
+    entry_ref = refs.pop(0) if has_entry else None
+    given = [refs.pop(0), refs.pop(0)] if has_tables else None
+    path_ref, end_ref, step_ref, drive_ref, x32_ref, go32_ref, inverse_ref = refs[:7]
+    keys_ref, queries_ref = given or refs[7:]
     states, tokens = key_ref.shape[1:]
     tiles = x_ref.shape[2] // LANES
     key = key_ref[0].astype(jnp.float32)
-    query = query_ref[0].astype(jnp.float32)
-    rows_ref[0] = key
-    rows_ref[1] = query
+    if not has_tables:
+        spread_columns(key, keys_ref)
+        spread_columns(query_ref[0].astype(jnp.float32), queries_ref)
     key_norm = jnp.sum(key * key, axis=0, keepdims=True)
     norm = jnp.transpose(jnp.broadcast_to(key_norm, (LANES, tokens)))
     for j in range(tiles):
@@ -136,10 +138,9 @@
     def run_states():
         def block(b, state):
             base = b * UNROLL
-            keys = columns(key, base)
             state = [list(part) for part in state]
             for u in range(UNROLL):
-                k = halves(keys[u])
+                k = halves(keys_ref[base + u])
                 k2 = [part * part for part in k]
                 for j in range(tiles):
                     step = row(step_ref, j, base + u)
@@ -154,12 +155,10 @@
     def run_grads():
         def block(i, state):
             base = tokens - UNROLL - i * UNROLL
-            keys = columns(key, base)
-            queries = columns(query, base)
             state = [list(part) for part in state]
             for u in reversed(range(UNROLL)):
-                k2 = [part * part for part in halves(keys[u])]
-                q = halves(queries[u])
+                k2 = [part * part for part in halves(keys_ref[base + u])]
+                q = halves(queries_ref[base + u])
                 for j in range(tiles):
                     step = row(step_ref, j, base + u)
                     go = row(go32_ref, j, base + u)
@@ -185,16 +184,17 @@
 
 def second_kernel(onwards_here, last, heads, has_start, has_before, *refs):
     refs = list(refs)
-    entry_ref, path_ref, rows_ref, step_ref, drive_ref, x32_ref, go32_ref, inverse_ref = refs[:8]
-    del refs[:8]
+    key_ref, entry_ref, path_ref, step_ref, drive_ref, x32_ref, go32_ref, inverse_ref = refs[:8]
+    keys_ref, queries_ref = refs[8:10]
+    del refs[:10]
     start_ref = refs.pop(0) if has_start else None
     before_ref = refs.pop(0) if has_before else None
-    message_ref, sums_ref, dot_ref, weighted_ref, key_part_ref, query_part_ref, norm_ref = refs
-    states, tokens = rows_ref.shape[1:]
+    message_refs = refs[:heads]
+    sums_ref, dot_ref, weighted_ref, key_part_ref, query_part_ref, norm_ref = refs[heads:]
+    states, tokens = key_ref.shape[1:]
     tiles = step_ref.shape[0]
     width = tiles * LANES
-    key = rows_ref[0]
-    query = rows_ref[1]
+    key = key_ref[0].astype(jnp.float32)
     pair = range(states // SUB)
 
     def path_at(t, h, j):
@@ -203,12 +203,10 @@
     def step_through(back, advance):
         def block(i, state):
             base = tokens - UNROLL - i * UNROLL if back else i * UNROLL
-            keys = columns(key, base)
-            queries = columns(query, base)
             state = [list(part) for part in state]
             for u in reversed(range(UNROLL)) if back else range(UNROLL):
                 t = base + u
-                k, q = halves(keys[u]), halves(queries[u])
+                k, q = halves(keys_ref[t]), halves(queries_ref[t])
                 k2 = [part * part for part in k]
                 sums = None
                 for j in range(tiles):
@@ -256,31 +254,28 @@
 
     part = tokens // heads
     rows = 2 * SUB
-
-    def finish(i, _):
-        base = pl.multiple_of(i * rows, rows)
-        to = pl.ds(pl.multiple_of(lax.rem(base, part), rows), rows)
-        head = lax.div(base, part)
-        norm_sum = None
-        for j in range(tiles):
-            dot, weighted = (
-                sum(ref[j, pl.ds(base * SUB + s, rows, stride=SUB), :] for s in range(SUB))
-                for ref in (dot_ref, weighted_ref)
-            )
-            step, x, inverse = (
-                ref[j, pl.ds(base, rows), :] for ref in (step_ref, x32_ref, inverse_ref)
-            )
-            grad_step = x * dot - weighted
-            message_ref[head, to, tile_at(j)] = (step * dot).astype(jnp.bfloat16)
-            message_ref[head, to, tile_at(tiles + j)] = (grad_step * inverse * inverse).astype(
-                jnp.bfloat16
-            )
-            term = grad_step * step * step
-            norm_sum = term if j == 0 else norm_sum + term
-        norm_ref[pl.ds(base, rows), :] = norm_sum
-        return _
-
-    lax.fori_loop(0, tokens // rows, finish, 0)
+    position = lax.axis_index("head")
+    for d in range(heads):
+        for r in range(part // rows):
+            base = pl.multiple_of((position ^ d) * part + r * rows, rows)
+            to = pl.ds(r * rows, rows)
+            norm_sum = None
+            for j in range(tiles):
+                dot, weighted = (
+                    sum(ref[j, pl.ds(base * SUB + s, rows, stride=SUB), :] for s in range(SUB))
+                    for ref in (dot_ref, weighted_ref)
+                )
+                step, x, inverse = (
+                    ref[j, pl.ds(base, rows), :] for ref in (step_ref, x32_ref, inverse_ref)
+                )
+                grad_step = x * dot - weighted
+                message_refs[d][to, tile_at(j)] = (step * dot).astype(jnp.bfloat16)
+                message_refs[d][to, tile_at(tiles + j)] = (grad_step * inverse * inverse).astype(
+                    jnp.bfloat16
+                )
+                term = grad_step * step * step
+                norm_sum = term if j == 0 else norm_sum + term
+            norm_ref[pl.ds(base, rows), :] = norm_sum
     norm_row = lane_sums(norm_ref[...])[:1]
     for n in range(states):
         at = pl.ds(n, tokens, stride=states)
@@ -292,37 +287,43 @@
     if last:
         quarters = 2 * states // SUB
         lane = lax.broadcasted_iota(jnp.int32, (SUB, tokens), 1) // part
-        for h in range(heads):
+        for d in range(heads):
+            shift = (heads - (position ^ d)) * part
             packed = None
             for i in range(quarters):
-                turned = pltpu.roll(sums_ref[SUB * i : SUB * i + SUB], ((i - h) * part) % tokens, 1)
+                turned = pltpu.roll(
+                    sums_ref[SUB * i : SUB * i + SUB], lax.rem(shift + i * part, tokens), 1
+                )
                 packed = turned if packed is None else jnp.where(lane == i, turned, packed)
             high = packed.astype(jnp.bfloat16).astype(jnp.float32)
             both = jnp.concatenate([high, packed - high], axis=0).astype(jnp.bfloat16)
-            message_ref[h, :rows, pl.ds(2 * width, LANES)] = both
-            message_ref[h, rows:, pl.ds(2 * width, LANES)] = jnp.zeros(
+            message_refs[d][:rows, pl.ds(2 * width, LANES)] = both
+            message_refs[d][rows:, pl.ds(2 * width, LANES)] = jnp.zeros(
                 (part - rows, LANES), jnp.bfloat16
             )
 
 
 def gather_kernel(heads, chunks, *refs):
-    messages, (in_ref, rate_ref, key_ref, query_ref) = refs[:chunks], refs[chunks:]
+    pieces, (in_ref, rate_ref, key_ref, query_ref) = refs[:-4], refs[-4:]
     states, part = key_ref.shape[1:]
     channels = in_ref.shape[2] // heads
     width = channels // chunks
+    position = lax.axis_index("head")
     total = None
-    for s in range(heads):
-        for c, message in enumerate(messages):
-            to = pl.ds(s * channels + c * width, width)
-            in_ref[0, :, to] = message[s, :, pl.ds(0, width)]
-            rate_ref[0, :, to] = message[s, :, pl.ds(width, width)]
-        both = messages[-1][s, :16, pl.ds(2 * width, LANES)].astype(jnp.float32)
-        both = both[:8] + both[8:]
-        total = both if total is None else total + both
-    for i in range(states // 8):
-        key_ref[0, 8 * i : 8 * i + 8] = total[:, i * part : (i + 1) * part]
-        at = states // 8 + i
-        query_ref[0, 8 * i : 8 * i + 8] = total[:, at * part : (at + 1) * part]
+    for c in range(chunks):
+        for d in range(heads):
+            piece = pieces[c * heads + d]
+            at = pl.multiple_of((position ^ d) * channels + c * width, LANES)
+            in_ref[0, :, pl.ds(at, width)] = piece[:, pl.ds(0, width)]
+            rate_ref[0, :, pl.ds(at, width)] = piece[:, pl.ds(width, width)]
+            if c == chunks - 1:
+                both = piece[: 2 * SUB, pl.ds(2 * width, LANES)].astype(jnp.float32)
+                both = both[:SUB] + both[SUB:]
+                total = both if total is None else total + both
+    for i in range(states // SUB):
+        key_ref[0, SUB * i : SUB * i + SUB] = total[:, i * part : (i + 1) * part]
+        at = states // SUB + i
+        query_ref[0, SUB * i : SUB * i + SUB] = total[:, at * part : (at + 1) * part]
 
 
 def shards(inputs, step_rate, key_rows, query_rows, grad_out):
@@ -339,25 +340,29 @@
     whole = pl.BlockSpec(memory_space=pltpu.VMEM)
     plane = pltpu.VMEM((width // LANES, tokens + SUB, LANES), f32)
 
-    def first(c, backwards, entry=None):
+    table = pltpu.VMEM((tokens, states, LANES), f32)
+
+    def first(c, backwards, tables=(), entry=None):
         wide = pl.BlockSpec((1, tokens, width), lambda i: (0, 0, c))
         specs = [wide, wide, whole, whole, wide]
         arrays = [inputs, step_rate, key_cols, query_cols, grad_out]
-        if entry is not None:
-            specs, arrays = specs + [whole], arrays + [entry]
-        return pl.pallas_call(
-            functools.partial(first_kernel, backwards, entry is not None),
+        if c == 0:
+            arrays = [pltpu.with_memory_space_constraint(a, pltpu.HBM) for a in arrays]
+        extra = [*(() if entry is None else (entry,)), *tables]
+        out_shape = [
+            pltpu.VMEM((tokens, states, width), f32),
+            jax.ShapeDtypeStruct((states, width), f32),
+        ]
+        out_shape += [plane] * 5 + [table] * (0 if tables else 2)
+        path, end, *carried = pl.pallas_call(
+            functools.partial(first_kernel, backwards, entry is not None, bool(tables)),
             grid=(1,),
-            in_specs=specs,
-            out_specs=[whole] * 8,
-            out_shape=[
-                pltpu.VMEM((tokens, states, width), f32),
-                jax.ShapeDtypeStruct((states, width), f32),
-                pltpu.VMEM((2, states, tokens), f32),
-            ]
-            + [plane] * 5,
+            in_specs=specs + [whole] * len(extra),
+            out_specs=[whole] * len(out_shape),
+            out_shape=out_shape,
             compiler_params=params,
-        )(*arrays)
+        )(*arrays, *extra)
+        return path, end, carried[:5], tuple(tables) or tuple(carried[5:])
 
     def second(c, onwards_here, entry, carried, start, before):
         last = c == CHUNKS - 1
@@ -365,47 +370,50 @@
         extra = [a for a in (start, before) if a is not None]
         parts = pltpu.VMEM((width // LANES, (tokens + 1) * SUB, LANES), f32)
         sums = pltpu.VMEM(((tokens + 1) * states, LANES), f32)
-        return pl.pallas_call(
+        piece = jax.ShapeDtypeStruct((part, wide_message), jnp.bfloat16)
+        *pieces, sums = pl.pallas_call(
             functools.partial(
                 second_kernel, onwards_here, last, heads, start is not None, before is not None
             ),
-            in_specs=[whole] * (8 + len(extra)),
-            out_specs=[whole, whole],
-            out_shape=[
-                jax.ShapeDtypeStruct((heads, part, wide_message), jnp.bfloat16),
-                pltpu.VMEM((2 * states, tokens), f32),
-            ],
+            in_specs=[whole] * (10 + len(extra)),
+            out_specs=[whole] * (heads + 1),
+            out_shape=[piece] * heads + [pltpu.VMEM((2 * states, tokens), f32)],
             scratch_shapes=[parts, parts, sums, sums, pltpu.VMEM((tokens, LANES), f32)],
             compiler_params=params,
-        )(entry, *carried, *extra)
+        )(key_cols, entry, *carried, *extra)
+        return pieces, sums
 
     work = []
     if groups == 2:
         here = None
+        tables = ()
         for c in range(CHUNKS):
-            path, end, *carried = first(c, here)
+            path, end, carried, tables = first(c, here, tables)
             entry = lax.ppermute(end, "ctx", [(0, 1), (1, 0)])
-            work.append((entry, [path] + carried, None))
+            work.append((entry, [path, *carried, *tables], None))
     else:
         here = False
         product, end, back = group_summary(inputs, step_rate, key_rows, query_rows, grad_out)
         unit = (jnp.ones_like(product), jnp.zeros_like(product))
         starts = prefix((product, end), "ctx", unit, False)[1]
         entries = prefix((product, back), "ctx", unit, True)[1]
+        tables = ()
         for c in range(CHUNKS):
             at = slice(c * width, (c + 1) * width)
-            path, _, *carried = first(c, here, starts[:, at])
-            work.append((entries[:, at], [path] + carried, starts[:, at]))
+            path, _, carried, tables = first(c, here, tables, starts[:, at])
+            work.append((entries[:, at], [path, *carried, *tables], starts[:, at]))
 
     sums = None
     arrived = []
     for c, (entry, carried, start) in enumerate(work):
-        message, sums = second(c, here, entry, carried, start, sums)
-        arrived.append(lax.all_to_all(message, "head", split_axis=0, concat_axis=0, tiled=True))
+        pieces, sums = second(c, here, entry, carried, start, sums)
+        arrived.append(pieces[0])
+        for d in range(1, heads):
+            arrived.append(lax.ppermute(pieces[d], "head", [(s, s ^ d) for s in range(heads)]))
 
     grad_in, grad_rate, grad_key, grad_query = pl.pallas_call(
         functools.partial(gather_kernel, heads, CHUNKS),
-        in_specs=[whole] * CHUNKS,
+        in_specs=[whole] * len(arrived),
         out_specs=[whole] * 4,
         out_shape=[
             jax.ShapeDtypeStruct((1, part, heads * channels), jnp.bfloat16),

time: 43 us -> 36.2 us (0.84)
  blocking collectives: 21.6 us -> 0 us
  starting transfers between devices: 0.52 us -> 10.5 us
  waiting for transfers between devices: 0.9 us -> 10.4 us
  local copies, waits for them, and re-layouts: 4.31 us -> 0.71 us
  Pallas kernels: 14.7 us -> 13.6 us
    all_to_all x1 -> x0, blocking collectives: 21.6 us -> none  [shards(): lax.all_to_all(message, 'head', split_axis=0, concat_axis=0, tiled=True)]
    ppermute x0 -> x6, starting transfers between devices: none -> 9.82 us  [shards(): lax.ppermute(pieces[d], 'head', [(s, s ^ d) for s in range(heads)])]
    ppermute x0 -> x6, waiting for transfers between devices: none -> 8.36 us  [shards(): lax.ppermute(pieces[d], 'head', [(s, s ^ d) for s in range(heads)])]
    unnamed x10 -> x12, local copies, waits for them, and re-layouts: 4.31 us -> 0.71 us
    ppermute x1 -> x2, waiting for transfers between devices: 0.9 us -> 2.05 us  [shards(): entry = lax.ppermute(end, 'ctx', [(0, 1), (1, 0)])]
    pallas_call x1 -> x2, Pallas kernels: 9.82 us -> 9.18 us  [second(): pl.pallas_call(functools.partial(second_kernel, onwards_here, last, heads...]
    pallas_call x1 -> x2, Pallas kernels: 4.09 us -> 3.61 us  [first(): pl.pallas_call(functools.partial(first_kernel, backwards, entry is not No...]
  transfers between devices with their start and end apart: 1 -> 8, of which waited for: 1 -> 3; matrix products, arithmetic and copies ran while one was open for 0% -> 0% of each run, Pallas kernels for 0% -> 16%
where the time goes in v1:
time: 36.2 us; the launch traced here: 36 us
  Pallas kernels  13.6 us (38%)
  starting transfers between devices  10.5 us (29%)
  waiting for transfers between devices  10.4 us (29%)
  between operations  0.72 us (2%)
  local copies, waits for them, and re-layouts  0.71 us (2%)
    ppermute x6, starting transfers between devices, shards(): lax.ppermute(pieces[d], 'head', [(s, s ^ d) for s in range(heads)])  9.82 us
    pallas_call x2, Pallas kernels, second(): pl.pallas_call(functools.partial(second_kernel, onwards_here, last, heads...  9.18 us
    ppermute x6, waiting for transfers between devices, shards(): lax.ppermute(pieces[d], 'head', [(s, s ^ d) for s in range(heads)])  8.36 us
    pallas_call x2, Pallas kernels, first(): pl.pallas_call(functools.partial(first_kernel, backwards, entry is not No...  3.61 us
    ppermute x2, waiting for transfers between devices, shards(): entry = lax.ppermute(end, 'ctx', [(0, 1), (1, 0)])  2.05 us
    pallas_call x1, Pallas kernels, shards(): pl.pallas_call(functools.partial(gather_kernel, heads, CHUNKS), in_specs=...  0.83 us
  transfers between devices with their start and end apart: 8, of which 3 were waited for; matrix products, arithmetic and copies ran while one was open for 0% of the time, Pallas kernels for 16%

profile of v1, /device:TPU:0, one launch (start us, length us, event | category | flops | bytes accessed | tf_op | source)
XLA Modules:
  0.0 36.0 jit_solution(819749908952112709)
XLA Ops:
  0.6 0.0 copy-start
  0.6 0.0 copy-start.1
  0.7 0.0 copy-start.2
  0.7 0.0 copy-start.4
  0.7 0.0 copy-start.5
  0.7 2.6 %shard_map.84 = (f32[128,16,512]{2,1,0:T(8,128)S(1)}, f32[16,512]{1,0:T(8,128)S(1)}, f32[4,136,128]{2,1,0:T(8,128)S(1)}, f32[4,136,128]{2,1,0:T(8,128)S(1)}, f32...) custom-call(bf16[1,128,1024]{2,1,0:T(8,128)(2,1)} %refs_0_.3, ...), custom_call_target="tpu_custom_call" | custom-call | tf_op jit(solution)/shard_map/pallas_call | solution.py:357
  3.3 0.6 %collective-permute-start = (f32[16,512]{1,0:T(8,128)S(1)}, f32[16,512]{1,0:T(8,128)S(1)}, u32[]{:S(2)}, u32[]{:S(2)}) collective-permute-start(f32[16,512]{1,0:T(8,128)S(1)} %get-tuple-element.33), channel_id=1, source_target_pairs={{0,4},{4,0},{1,5},{5,1},{2,6},{6,2},{3,7},{7,3},{8,12},{12,8},{9,1... | collective-permute-start | bytes 98312 | tf_op jit(solution)/shard_map/ppermute | solution.py:392
  3.9 0.9 %collective-permute-done.refs_1_ = f32[16,512]{1,0:T(8,128)S(1)} collective-permute-done((f32[16,512]{1,0:T(8,128)S(1)}, f32[16,512]{1,0:T(8,128)S(1)}, u32[]{:S(2)}, u32[]{:S(2)}) %collective-permute-start) | collective-permute-done | bytes 32800 | tf_op jit(solution)/shard_map/ppermute | solution.py:392
  4.8 0.0 copy-start.3
  4.8 0.7 %copy-done.3 = bf16[1,128,16]{1,2,0:T(8,128)(2,1)S(1)} copy-done((bf16[1,128,16]{1,2,0:T(8,128)(2,1)S(1)}, bf16[1,128,16]{1,2,0:T(8,128)(2,1)}, u32[]{:S(2)}) %copy-start.3) | copy-done | bytes 4120
  5.5 4.3 %shard_map.85 = (bf16[32,1024]{1,0:T(8,128)(2,1)S(1)}, bf16[32,1024]{1,0:T(8,128)(2,1)S(1)}, bf16[32,1024]{1,0:T(8,128)(2,1)S(1)}, bf16[32,1024]{1,0:T(8,128)(2,1)S(1)}, f32[32,128]{1,0:T(8,128)S(1)}) custom-call(bf16[1,16,128]{2,1,0:T(8,128)(2,1)S(1)} %bitcast.5, f32[16,512]{1,0:T(8,128)S(1)} %collective-permute-done.refs_1_, ...), custom_call_target="tpu_custom_call" | custom-call | tf_op jit(solution)/shard_map/pallas_call | solution.py:374
  9.7 2.8 %collective-permute-start.1 = (bf16[32,1024]{1,0:T(8,128)(2,1)S(1)}, bf16[32,1024]{1,0:T(8,128)(2,1)S(1)}, u32[]{:S(2)}, u32[]{:S(2)}) collective-permute-start(bf16[32,1024]{1,0:T(8,128)(2,1)S(1)} %get-tuple-element.43), channel_id=1, source_target_pairs={{0,1},{1,0},{2,3},{3,2},{4,5},{5,4},{6,7},{7,6},{8,9},{9,8},{10,11... | collective-permute-start | bytes 196616 | tf_op jit(solution)/shard_map/ppermute | solution.py:412
  12.6 0.0 copy-done
  12.6 0.0 copy-done.1
  12.6 0.0 copy-done.2
  12.6 0.0 copy-done.4
  12.6 0.0 copy-done.5
  12.6 1.0 %shard_map.86 = (f32[128,16,512]{2,1,0:T(8,128)S(1)}, f32[16,512]{1,0:T(8,128)S(1)}, f32[4,136,128]{2,1,0:T(8,128)S(1)}, f32[4,136,128]{2,1,0:T(8,128)S(1)}, f32...) custom-call(bf16[1,128,1024]{2,1,0:T(8,128)(2,1)S(1)} %copy-done.1, ...), custom_call_target="tpu_custom_call" | custom-call | tf_op jit(solution)/shard_map/pallas_call | solution.py:357
  13.6 0.1 collective-permute-start.4
  13.7 1.2 %collective-permute-done.4.refs_1_ = f32[16,512]{1,0:T(8,128)S(1)} collective-permute-done((f32[16,512]{1,0:T(8,128)S(1)}, f32[16,512]{1,0:T(8,128)S(1)}, u32[]{:S(2)}, u32[]{:S(2)}) %collective-permute-start.4) | collective-permute-done | bytes 32800 | tf_op jit(solution)/shard_map/ppermute | solution.py:392
  14.9 4.9 %shard_map.87 = (bf16[32,1152]{1,0:T(8,128)(2,1)S(1)}, bf16[32,1152]{1,0:T(8,128)(2,1)S(1)}, bf16[32,1152]{1,0:T(8,128)(2,1)S(1)}, bf16[32,1152]{1,0:T(8,128)(2,1)S(1)}, f32[32,128]{1,0:T(8,128)}) custom-call(bf16[1,16,128]{2,1,0:T(8,128)(2,1)S(1)} %bitcast.7, f32[16,512]{1,0:T(8,128)S(1)} %collective-permute-done.4.refs_1_, ...), custom_call_target="tpu_custom_call" | custom-call | tf_op jit(solution)/shard_map/pallas_call | solution.py:374
  19.8 0.0 collective-permute-start.5
  19.8 3.0 %collective-permute-start.6 = (bf16[32,1152]{1,0:T(8,128)(2,1)S(1)}, bf16[32,1152]{1,0:T(8,128)(2,1)S(1)}, u32[]{:S(2)}, u32[]{:S(2)}) collective-permute-start(bf16[32,1152]{1,0:T(8,128)(2,1)S(1)} %get-tuple-element.56), channel_id=1, source_target_pairs={{0,2},{1,3},{2,0},{3,1},{4,6},{5,7},{6,4},{7,5},{8,10},{9,11},{10,... | collective-permute-start | bytes 221192 | tf_op jit(solution)/shard_map/ppermute | solution.py:412
  22.8 1.3 %collective-permute-start.7 = (bf16[32,1152]{1,0:T(8,128)(2,1)S(1)}, bf16[32,1152]{1,0:T(8,128)(2,1)S(1)}, u32[]{:S(2)}, u32[]{:S(2)}) collective-permute-start(bf16[32,1152]{1,0:T(8,128)(2,1)S(1)} %get-tuple-element.57), channel_id=1, source_target_pairs={{0,3},{1,2},{2,1},{3,0},{4,7},{5,6},{6,5},{7,4},{8,11},{9,10},{10,... | collective-permute-start | bytes 221192 | tf_op jit(solution)/shard_map/ppermute | solution.py:412
  24.2 1.7 %collective-permute-start.2 = (bf16[32,1024]{1,0:T(8,128)(2,1)S(1)}, bf16[32,1024]{1,0:T(8,128)(2,1)S(1)}, u32[]{:S(2)}, u32[]{:S(2)}) collective-permute-start(bf16[32,1024]{1,0:T(8,128)(2,1)S(1)} %get-tuple-element.44), channel_id=1, source_target_pairs={{0,2},{1,3},{2,0},{3,1},{4,6},{5,7},{6,4},{7,5},{8,10},{9,11},{10,... | collective-permute-start | bytes 196616 | tf_op jit(solution)/shard_map/ppermute | solution.py:412
  25.9 0.0 collective-permute-done.1.refs_1_
  25.9 0.9 %collective-permute-start.3 = (bf16[32,1024]{1,0:T(8,128)(2,1)S(1)}, bf16[32,1024]{1,0:T(8,128)(2,1)S(1)}, u32[]{:S(2)}, u32[]{:S(2)}) collective-permute-start(bf16[32,1024]{1,0:T(8,128)(2,1)S(1)} %get-tuple-element.45), channel_id=1, source_target_pairs={{0,3},{1,2},{2,1},{3,0},{4,7},{5,6},{6,5},{7,4},{8,11},{9,10},{10,... | collective-permute-start | bytes 196616 | tf_op jit(solution)/shard_map/ppermute | solution.py:412
  26.8 8.3 %collective-permute-done.2.refs_2_ = bf16[32,1024]{1,0:T(8,128)(2,1)S(1)} collective-permute-done((bf16[32,1024]{1,0:T(8,128)(2,1)S(1)}, bf16[32,1024]{1,0:T(8,128)(2,1)S(1)}, u32[]{:S(2)}, u32[]{:S(2)}) %collective-permute-start.2) | collective-permute-done | bytes 65568 | tf_op jit(solution)/shard_map/ppermute | solution.py:412
  35.1 0.0 collective-permute-done.3.refs_3_
  35.1 0.0 collective-permute-done.5.refs_5_
  35.1 0.0 collective-permute-done.6.refs_6_
  35.1 0.0 collective-permute-done.7.refs_7_
  35.1 0.8 %shard_map.88 = (bf16[1,32,4096]{2,1,0:T(8,128)(2,1)}, bf16[1,32,4096]{2,1,0:T(8,128)(2,1)}, f32[1,16,32]{2,1,0:T(8,128)}, f32[1,16,32]{2,1,0:T(8,128)}) custom-call(bf16[32,1024]{1,0:T(8,128)(2,1)S(1)} %get-tuple-element.42.refs_0_, bf16[32,1024]{1,0:T(8,128)(2,1)S(1)} %collective-permute-done.1.refs_1_, ...), custom_call_target="tpu_custom_call" | custom-call | tf_op jit(solution)/shard_map/pallas_call | solution.py:414
Async XLA Ops:
  0.6 12.0 %copy-start = (f32[1,128,1024]{2,1,0:T(8,128)S(1)}, f32[1,128,1024]{2,1,0:T(8,128)}, u32[]{:S(2)}) copy-start(f32[1,128,1024]{2,1,0:T(8,128)} %refs_1_.3) | copy-start | bytes 1572868
  0.6 11.9 %copy-start.1 = (bf16[1,128,1024]{2,1,0:T(8,128)(2,1)S(1)}, bf16[1,128,1024]{2,1,0:T(8,128)(2,1)}, u32[]{:S(2)}) copy-start(bf16[1,128,1024]{2,1,0:T(8,128)(2,1)} %refs_0_.3) | copy-start | bytes 786436
  0.7 11.9 %copy-start.2 = (bf16[1,128,1024]{2,1,0:T(8,128)(2,1)S(1)}, bf16[1,128,1024]{2,1,0:T(8,128)(2,1)}, u32[]{:S(2)}) copy-start(bf16[1,128,1024]{2,1,0:T(8,128)(2,1)} %refs_4_.3) | copy-start | bytes 786436
  0.7 11.9 %copy-start.4 = (bf16[1,128,16]{1,2,0:T(8,128)(2,1)S(1)}, bf16[1,128,16]{1,2,0:T(8,128)(2,1)}, u32[]{:S(2)}) copy-start(bf16[1,128,16]{1,2,0:T(8,128)(2,1)} %param.7) | copy-start | bytes 12292
  0.7 11.9 %copy-start.5 = (bf16[1,128,16]{1,2,0:T(8,128)(2,1)S(1)}, bf16[1,128,16]{1,2,0:T(8,128)(2,1)}, u32[]{:S(2)}) copy-start(bf16[1,128,16]{1,2,0:T(8,128)(2,1)} %param.8) | copy-start | bytes 12292
  3.3 1.5 %collective-permute-start = (f32[16,512]{1,0:T(8,128)S(1)}, f32[16,512]{1,0:T(8,128)S(1)}, u32[]{:S(2)}, u32[]{:S(2)}) collective-permute-start(f32[16,512]{1,0:T(8,128)S(1)} %get-tuple-element.33), channel_id=1, source_target_pairs={{0,4},{4,0},{1,5},{5,1},{2,6},{6,2},{3,7},{7,3},{8,12},{12,8},{9,1... | collective-permute-start | bytes 98312 | tf_op jit(solution)/shard_map/ppermute | solution.py:392
  4.8 0.7 %copy-start.3 = (bf16[1,128,16]{1,2,0:T(8,128)(2,1)S(1)}, bf16[1,128,16]{1,2,0:T(8,128)(2,1)}, u32[]{:S(2)}) copy-start(bf16[1,128,16]{1,2,0:T(8,128)(2,1)} %param.7) | copy-start | bytes 12292
  9.7 16.1 %collective-permute-start.1 = (bf16[32,1024]{1,0:T(8,128)(2,1)S(1)}, bf16[32,1024]{1,0:T(8,128)(2,1)S(1)}, u32[]{:S(2)}, u32[]{:S(2)}) collective-permute-start(bf16[32,1024]{1,0:T(8,128)(2,1)S(1)} %get-tuple-element.43), channel_id=1, source_target_pairs={{0,1},{1,0},{2,3},{3,2},{4,5},{5,4},{6,7},{7,6},{8,9},{9,8},{10,11... | collective-permute-start | bytes 196616 | tf_op jit(solution)/shard_map/ppermute | solution.py:412
  13.6 1.3 %collective-permute-start.4 = (f32[16,512]{1,0:T(8,128)S(1)}, f32[16,512]{1,0:T(8,128)S(1)}, u32[]{:S(2)}, u32[]{:S(2)}) collective-permute-start(f32[16,512]{1,0:T(8,128)S(1)} %get-tuple-element.46), channel_id=1, source_target_pairs={{0,4},{4,0},{1,5},{5,1},{2,6},{6,2},{3,7},{7,3},{8,12},{12,8},{9,1... | collective-permute-start | bytes 98312 | tf_op jit(solution)/shard_map/ppermute | solution.py:392
  19.8 15.3 %collective-permute-start.5 = (bf16[32,1152]{1,0:T(8,128)(2,1)S(1)}, bf16[32,1152]{1,0:T(8,128)(2,1)S(1)}, u32[]{:S(2)}, u32[]{:S(2)}) collective-permute-start(bf16[32,1152]{1,0:T(8,128)(2,1)S(1)} %get-tuple-element.55), channel_id=1, source_target_pairs={{0,1},{1,0},{2,3},{3,2},{4,5},{5,4},{6,7},{7,6},{8,9},{9,8},{10,11... | collective-permute-start | bytes 221192 | tf_op jit(solution)/shard_map/ppermute | solution.py:412
  19.8 15.3 %collective-permute-start.6 = (bf16[32,1152]{1,0:T(8,128)(2,1)S(1)}, bf16[32,1152]{1,0:T(8,128)(2,1)S(1)}, u32[]{:S(2)}, u32[]{:S(2)}) collective-permute-start(bf16[32,1152]{1,0:T(8,128)(2,1)S(1)} %get-tuple-element.56), channel_id=1, source_target_pairs={{0,2},{1,3},{2,0},{3,1},{4,6},{5,7},{6,4},{7,5},{8,10},{9,11},{10,... | collective-permute-start | bytes 221192 | tf_op jit(solution)/shard_map/ppermute | solution.py:412
  22.8 12.3 %collective-permute-start.7 = (bf16[32,1152]{1,0:T(8,128)(2,1)S(1)}, bf16[32,1152]{1,0:T(8,128)(2,1)S(1)}, u32[]{:S(2)}, u32[]{:S(2)}) collective-permute-start(bf16[32,1152]{1,0:T(8,128)(2,1)S(1)} %get-tuple-element.57), channel_id=1, source_target_pairs={{0,3},{1,2},{2,1},{3,0},{4,7},{5,6},{6,5},{7,4},{8,11},{9,10},{10,... | collective-permute-start | bytes 221192 | tf_op jit(solution)/shard_map/ppermute | solution.py:412
  24.2 10.9 %collective-permute-start.2 = (bf16[32,1024]{1,0:T(8,128)(2,1)S(1)}, bf16[32,1024]{1,0:T(8,128)(2,1)S(1)}, u32[]{:S(2)}, u32[]{:S(2)}) collective-permute-start(bf16[32,1024]{1,0:T(8,128)(2,1)S(1)} %get-tuple-element.44), channel_id=1, source_target_pairs={{0,2},{1,3},{2,0},{3,1},{4,6},{5,7},{6,4},{7,5},{8,10},{9,11},{10,... | collective-permute-start | bytes 196616 | tf_op jit(solution)/shard_map/ppermute | solution.py:412
  25.9 9.2 %collective-permute-start.3 = (bf16[32,1024]{1,0:T(8,128)(2,1)S(1)}, bf16[32,1024]{1,0:T(8,128)(2,1)S(1)}, u32[]{:S(2)}, u32[]{:S(2)}) collective-permute-start(bf16[32,1024]{1,0:T(8,128)(2,1)S(1)} %get-tuple-element.45), channel_id=1, source_target_pairs={{0,3},{1,2},{2,1},{3,0},{4,7},{5,6},{6,5},{7,4},{8,11},{9,10},{10,... | collective-permute-start | bytes 196616 | tf_op jit(solution)/shard_map/ppermute | solution.py:412

commit v2 on v1

--- a/solution.py
+++ b/solution.py
@@ -11,7 +11,8 @@
 LANES = 128
 SUB = 8
 UNROLL = 8
-CHUNKS = 2
+CHUNKS = 4
+AHEAD = 1
 VMEM_LIMIT = 20 * 1024 * 1024
 
 
@@ -99,18 +100,21 @@
     return product(high) + product(low)
 
 
-def first_kernel(backwards, has_entry, has_tables, *refs):
+def first_kernel(backwards, has_entry, has_tables, has_earlier, *refs):
     refs = list(refs)
     x_ref, rate_ref, key_ref, query_ref, go_ref = refs[:5]
     del refs[:5]
     entry_ref = refs.pop(0) if has_entry else None
     given = [refs.pop(0), refs.pop(0)] if has_tables else None
+    if has_earlier:
+        del refs[0]
     path_ref, end_ref, step_ref, drive_ref, x32_ref, go32_ref, inverse_ref = refs[:7]
-    keys_ref, queries_ref = given or refs[7:]
+    keys_ref, queries_ref = given or refs[7:9]
     states, tokens = key_ref.shape[1:]
     tiles = x_ref.shape[2] // LANES
     key = key_ref[0].astype(jnp.float32)
     if not has_tables:
+        refs[9][...] = key
         spread_columns(key, keys_ref)
         spread_columns(query_ref[0].astype(jnp.float32), queries_ref)
     key_norm = jnp.sum(key * key, axis=0, keepdims=True)
@@ -184,17 +188,16 @@
 
 def second_kernel(onwards_here, last, heads, has_start, has_before, *refs):
     refs = list(refs)
-    key_ref, entry_ref, path_ref, step_ref, drive_ref, x32_ref, go32_ref, inverse_ref = refs[:8]
-    keys_ref, queries_ref = refs[8:10]
-    del refs[:10]
+    entry_ref, path_ref, step_ref, drive_ref, x32_ref, go32_ref, inverse_ref = refs[:7]
+    keys_ref, queries_ref = refs[7:9]
+    del refs[:9]
     start_ref = refs.pop(0) if has_start else None
-    before_ref = refs.pop(0) if has_before else None
-    message_refs = refs[:heads]
-    sums_ref, dot_ref, weighted_ref, key_part_ref, query_part_ref, norm_ref = refs[heads:]
-    states, tokens = key_ref.shape[1:]
+    before = [refs.pop(0) for _ in range(3)] if has_before else None
+    key_ref = refs.pop(0) if last else None
+    piece_refs = refs[:heads]
+    key_part_ref, query_part_ref, norm_ref, dot_ref, weighted_ref = refs[heads : heads + 5]
+    tokens, states = keys_ref.shape[:2]
     tiles = step_ref.shape[0]
-    width = tiles * LANES
-    key = key_ref[0].astype(jnp.float32)
     pair = range(states // SUB)
 
     def path_at(t, h, j):
@@ -231,7 +234,11 @@
                 for h in pair:
                     by_drive, by_decay, by_query = sums[3 * h : 3 * h + 3]
                     at = pl.ds(pl.multiple_of(t * states + h * SUB, SUB), SUB)
-                    key_part_ref[at, :] = by_drive - (2.0 * k[h]) * by_decay
+                    by_key = by_drive - (2.0 * k[h]) * by_decay
+                    if has_before:
+                        by_key = by_key + before[0][at, :]
+                        by_query = by_query + before[1][at, :]
+                    key_part_ref[at, :] = by_key
                     query_part_ref[at, :] = by_query
             return state
 
@@ -258,8 +265,7 @@
     for d in range(heads):
         for r in range(part // rows):
             base = pl.multiple_of((position ^ d) * part + r * rows, rows)
-            to = pl.ds(r * rows, rows)
-            norm_sum = None
+            norm_sum = before[2][pl.ds(base, rows), :] if has_before else None
             for j in range(tiles):
                 dot, weighted = (
                     sum(ref[j, pl.ds(base * SUB + s, rows, stride=SUB), :] for s in range(SUB))
@@ -269,38 +275,38 @@
                     ref[j, pl.ds(base, rows), :] for ref in (step_ref, x32_ref, inverse_ref)
                 )
                 grad_step = x * dot - weighted
-                message_refs[d][to, tile_at(j)] = (step * dot).astype(jnp.bfloat16)
-                message_refs[d][to, tile_at(tiles + j)] = (grad_step * inverse * inverse).astype(
-                    jnp.bfloat16
-                )
+                grad_rate = grad_step * inverse * inverse
+                to = j * part + r * rows
+                piece_refs[d][pl.ds(to, rows), :] = (step * dot).astype(jnp.bfloat16)
+                to += tiles * part
+                piece_refs[d][pl.ds(to, rows), :] = grad_rate.astype(jnp.bfloat16)
                 term = grad_step * step * step
-                norm_sum = term if j == 0 else norm_sum + term
+                norm_sum = term if norm_sum is None else norm_sum + term
             norm_ref[pl.ds(base, rows), :] = norm_sum
+    if not last:
+        return
+
+    key = key_ref[...]
     norm_row = lane_sums(norm_ref[...])[:1]
+    sums_ref = refs[heads + 5]
     for n in range(states):
         at = pl.ds(n, tokens, stride=states)
         sums_ref[n : n + 1, :] = lane_sums(key_part_ref[at, :])[:1]
         sums_ref[states + n : states + n + 1, :] = lane_sums(query_part_ref[at, :])[:1]
     sums_ref[:states] = sums_ref[:states] - 2.0 * key * norm_row
-    if has_before:
-        sums_ref[...] = sums_ref[...] + before_ref[...]
-    if last:
-        quarters = 2 * states // SUB
-        lane = lax.broadcasted_iota(jnp.int32, (SUB, tokens), 1) // part
-        for d in range(heads):
-            shift = (heads - (position ^ d)) * part
-            packed = None
-            for i in range(quarters):
-                turned = pltpu.roll(
-                    sums_ref[SUB * i : SUB * i + SUB], lax.rem(shift + i * part, tokens), 1
-                )
-                packed = turned if packed is None else jnp.where(lane == i, turned, packed)
-            high = packed.astype(jnp.bfloat16).astype(jnp.float32)
-            both = jnp.concatenate([high, packed - high], axis=0).astype(jnp.bfloat16)
-            message_refs[d][:rows, pl.ds(2 * width, LANES)] = both
-            message_refs[d][rows:, pl.ds(2 * width, LANES)] = jnp.zeros(
-                (part - rows, LANES), jnp.bfloat16
+    quarters = 2 * states // SUB
+    lane = lax.broadcasted_iota(jnp.int32, (SUB, tokens), 1) // part
+    for d in range(heads):
+        shift = (heads - (position ^ d)) * part
+        packed = None
+        for i in range(quarters):
+            turned = pltpu.roll(
+                sums_ref[SUB * i : SUB * i + SUB], lax.rem(shift + i * part, tokens), 1
             )
+            packed = turned if packed is None else jnp.where(lane == i, turned, packed)
+        high = packed.astype(jnp.bfloat16).astype(jnp.float32)
+        both = jnp.concatenate([high, packed - high], axis=0).astype(jnp.bfloat16)
+        piece_refs[d][pl.ds(2 * tiles * part, rows), :] = both
 
 
 def gather_kernel(heads, chunks, *refs):
@@ -309,15 +315,18 @@
     channels = in_ref.shape[2] // heads
     width = channels // chunks
     position = lax.axis_index("head")
+    tiles = width // LANES
     total = None
     for c in range(chunks):
         for d in range(heads):
             piece = pieces[c * heads + d]
             at = pl.multiple_of((position ^ d) * channels + c * width, LANES)
-            in_ref[0, :, pl.ds(at, width)] = piece[:, pl.ds(0, width)]
-            rate_ref[0, :, pl.ds(at, width)] = piece[:, pl.ds(width, width)]
+            for j in range(tiles):
+                to = pl.ds(at + j * LANES, LANES)
+                in_ref[0, :, to] = piece[pl.ds(j * part, part), :]
+                rate_ref[0, :, to] = piece[pl.ds((tiles + j) * part, part), :]
             if c == chunks - 1:
-                both = piece[: 2 * SUB, pl.ds(2 * width, LANES)].astype(jnp.float32)
+                both = piece[pl.ds(2 * tiles * part, 2 * SUB), :].astype(jnp.float32)
                 both = both[:SUB] + both[SUB:]
                 total = both if total is None else total + both
     for i in range(states // SUB):
@@ -342,74 +351,89 @@
 
     table = pltpu.VMEM((tokens, states, LANES), f32)
 
-    def first(c, backwards, tables=(), entry=None):
+    def cost(passes):
+        elements = tokens * states * width
+        return pl.CostEstimate(flops=passes * elements, bytes_accessed=4 * elements, transcendentals=0)
+
+    def first(c, backwards, tables=(), entry=None, earlier=None):
         wide = pl.BlockSpec((1, tokens, width), lambda i: (0, 0, c))
         specs = [wide, wide, whole, whole, wide]
         arrays = [inputs, step_rate, key_cols, query_cols, grad_out]
         if c == 0:
             arrays = [pltpu.with_memory_space_constraint(a, pltpu.HBM) for a in arrays]
-        extra = [*(() if entry is None else (entry,)), *tables]
+        for a in (entry, *tables[:2]):
+            if a is not None:
+                specs, arrays = specs + [whole], arrays + [a]
+        if earlier is not None:
+            specs, arrays = specs + [pl.BlockSpec(memory_space=pl.ANY)], arrays + [earlier]
         out_shape = [
             pltpu.VMEM((tokens, states, width), f32),
             jax.ShapeDtypeStruct((states, width), f32),
         ]
-        out_shape += [plane] * 5 + [table] * (0 if tables else 2)
+        out_shape += [plane] * 5
+        if not tables:
+            out_shape += [table] * 2 + [pltpu.VMEM((states, tokens), f32)]
         path, end, *carried = pl.pallas_call(
-            functools.partial(first_kernel, backwards, entry is not None, bool(tables)),
+            functools.partial(
+                first_kernel, backwards, entry is not None, bool(tables), earlier is not None
+            ),
             grid=(1,),
-            in_specs=specs + [whole] * len(extra),
+            in_specs=specs,
             out_specs=[whole] * len(out_shape),
             out_shape=out_shape,
             compiler_params=params,
-        )(*arrays, *extra)
+            cost_estimate=cost(5),
+        )(*arrays)
         return path, end, carried[:5], tuple(tables) or tuple(carried[5:])
 
-    def second(c, onwards_here, entry, carried, start, before):
+    def second(c, onwards_here, entry, carried, tables, start, before):
         last = c == CHUNKS - 1
-        wide_message = 2 * width + (LANES if last else 0)
-        extra = [a for a in (start, before) if a is not None]
+        keys, queries, key = tables
+        extra = [*(() if start is None else (start,)), *before, *((key,) if last else ())]
         parts = pltpu.VMEM((width // LANES, (tokens + 1) * SUB, LANES), f32)
         sums = pltpu.VMEM(((tokens + 1) * states, LANES), f32)
-        piece = jax.ShapeDtypeStruct((part, wide_message), jnp.bfloat16)
-        *pieces, sums = pl.pallas_call(
+        size = 2 * part * width // LANES + (2 * SUB if last else 0)
+        piece = jax.ShapeDtypeStruct((size, LANES), jnp.bfloat16)
+        results = pl.pallas_call(
             functools.partial(
-                second_kernel, onwards_here, last, heads, start is not None, before is not None
+                second_kernel, onwards_here, last, heads, start is not None, bool(before)
             ),
-            in_specs=[whole] * (10 + len(extra)),
-            out_specs=[whole] * (heads + 1),
-            out_shape=[piece] * heads + [pltpu.VMEM((2 * states, tokens), f32)],
-            scratch_shapes=[parts, parts, sums, sums, pltpu.VMEM((tokens, LANES), f32)],
+            in_specs=[whole] * (9 + len(extra)),
+            out_specs=[whole] * (heads + 3),
+            out_shape=[piece] * heads + [sums, sums, pltpu.VMEM((tokens, LANES), f32)],
+            scratch_shapes=[parts, parts] + [pltpu.VMEM((2 * states, tokens), f32)] * last,
             compiler_params=params,
-        )(key_cols, entry, *carried, *extra)
-        return pieces, sums
-
-    work = []
-    if groups == 2:
-        here = None
-        tables = ()
-        for c in range(CHUNKS):
-            path, end, carried, tables = first(c, here, tables)
-            entry = lax.ppermute(end, "ctx", [(0, 1), (1, 0)])
-            work.append((entry, [path, *carried, *tables], None))
-    else:
+            cost_estimate=cost(20),
+        )(entry, *carried, keys, queries, *extra)
+        return results[:heads], results[heads:]
+
+    entries = starts = None
+    here = None
+    if groups != 2:
         here = False
         product, end, back = group_summary(inputs, step_rate, key_rows, query_rows, grad_out)
         unit = (jnp.ones_like(product), jnp.zeros_like(product))
         starts = prefix((product, end), "ctx", unit, False)[1]
         entries = prefix((product, back), "ctx", unit, True)[1]
-        tables = ()
-        for c in range(CHUNKS):
-            at = slice(c * width, (c + 1) * width)
-            path, _, carried, tables = first(c, here, tables, starts[:, at])
-            work.append((entries[:, at], [path, *carried, *tables], starts[:, at]))
-
-    sums = None
-    arrived = []
-    for c, (entry, carried, start) in enumerate(work):
-        pieces, sums = second(c, here, entry, carried, start, sums)
-        arrived.append(pieces[0])
-        for d in range(1, heads):
-            arrived.append(lax.ppermute(pieces[d], "head", [(s, s ^ d) for s in range(heads)]))
+
+    def part_of(array, c):
+        return None if array is None else array[:, c * width : (c + 1) * width]
+
+    tables, before, work, arrived = (), (), [], []
+    for c in range(CHUNKS + AHEAD):
+        if c < CHUNKS:
+            earlier = before[2] if before else None
+            path, end, carried, tables = first(c, here, tables, part_of(starts, c), earlier)
+            entry = part_of(entries, c)
+            if entry is None:
+                entry = lax.ppermute(end, "ctx", [(0, 1), (1, 0)])
+            work.append((entry, [path, *carried], part_of(starts, c)))
+        if c >= AHEAD:
+            entry, carried, start = work[c - AHEAD]
+            pieces, before = second(c - AHEAD, here, entry, carried, tables, start, before)
+            arrived.append(pieces[0])
+            for d in range(1, heads):
+                arrived.append(lax.ppermute(pieces[d], "head", [(s, s ^ d) for s in range(heads)]))
 
     grad_in, grad_rate, grad_key, grad_query = pl.pallas_call(
         functools.partial(gather_kernel, heads, CHUNKS),

time: 36.2 us -> 39.8 us (1.099)
  starting transfers between devices: 10.5 us -> 20.4 us
  waiting for transfers between devices: 10.4 us -> 4.78 us
  local copies, waits for them, and re-layouts: 0.71 us -> 0.02 us
    ppermute x6 -> x12, starting transfers between devices: 9.82 us -> 18.9 us  [shards(): lax.ppermute(pieces[d], 'head', [(s, s ^ d) for s in range(heads)])]
    ppermute x6 -> x12, waiting for transfers between devices: 8.36 us -> 4.77 us  [shards(): lax.ppermute(pieces[d], 'head', [(s, s ^ d) for s in range(heads)])]
    ppermute x2 -> x4, waiting for transfers between devices: 2.05 us -> 0.01 us  [shards(): entry = lax.ppermute(end, 'ctx', [(0, 1), (1, 0)])]
    ppermute x2 -> x4, starting transfers between devices: 0.69 us -> 1.52 us  [shards(): entry = lax.ppermute(end, 'ctx', [(0, 1), (1, 0)])]
    unnamed x12 -> x10, local copies, waits for them, and re-layouts: 0.71 us -> 0.02 us
    pallas_call x2 -> x4, Pallas kernels: 3.61 us -> 3.86 us  [first(): pl.pallas_call(functools.partial(first_kernel, backwards, entry is not No...]
    pallas_call x2 -> x4, Pallas kernels: 9.18 us -> 8.99 us  [second(): pl.pallas_call(functools.partial(second_kernel, onwards_here, last, heads...]
  transfers between devices with their start and end apart: 8 -> 16, of which waited for: 3 -> 2; matrix products, arithmetic and copies ran while one was open for 0% -> 0% of each run, Pallas kernels for 16% -> 27%
where the time goes in v2:
time: 39.8 us; the launch traced here: 39.7 us
  starting transfers between devices  20.4 us (51%)
  Pallas kernels  13.7 us (34%)
  waiting for transfers between devices  4.78 us (12%)
  between operations  0.77 us (2%)
    ppermute x12, starting transfers between devices, shards(): lax.ppermute(pieces[d], 'head', [(s, s ^ d) for s in range(heads)])  18.9 us
    pallas_call x4, Pallas kernels, second(): pl.pallas_call(functools.partial(second_kernel, onwards_here, last, heads...  8.99 us
    ppermute x12, waiting for transfers between devices, shards(): lax.ppermute(pieces[d], 'head', [(s, s ^ d) for s in range(heads)])  4.77 us
    pallas_call x4, Pallas kernels, first(): pl.pallas_call(functools.partial(first_kernel, backwards, entry is not No...  3.86 us
    ppermute x4, starting transfers between devices, shards(): entry = lax.ppermute(end, 'ctx', [(0, 1), (1, 0)])  1.52 us
    pallas_call x1, Pallas kernels, shards(): pl.pallas_call(functools.partial(gather_kernel, heads, CHUNKS), in_specs=...  0.87 us
  transfers between devices with their start and end apart: 16, of which 2 were waited for; matrix products, arithmetic and copies ran while one was open for 0% of the time, Pallas kernels for 27%

profile of v2, /device:TPU:0, one launch (start us, length us, event | category | flops | bytes accessed | tf_op | source)
XLA Modules:
  0.0 39.7 jit_solution(14613711636791401886)
XLA Ops:
  0.6 0.0 copy-start.1
  0.6 0.0 copy-start
  0.7 0.0 copy-start.3
  0.7 0.0 copy-start.4
  0.7 0.0 copy-start.2
  0.7 2.1 %shard_map.84 = (f32[128,16,256]{2,1,0:T(8,128)S(1)}, f32[16,256]{1,0:T(8,128)S(1)}, f32[2,136,128]{2,1,0:T(8,128)S(1)}, f32[2,136,128]{2,1,0:T(8,128)S(1)}, f32...) custom-call(bf16[1,128,1024]{2,1,0:T(8,128)(2,1)} %refs_0_.7, ...), custom_call_target="tpu_custom_call" | custom-call | flops 2621440 | bytes 2097152 | tf_op jit(solution)/shard_map/pallas_call | solution.py:376
  2.8 0.6 %collective-permute-start = (f32[16,256]{1,0:T(8,128)S(1)}, f32[16,256]{1,0:T(8,128)S(1)}, u32[]{:S(2)}, u32[]{:S(2)}) collective-permute-start(f32[16,256]{1,0:T(8,128)S(1)} %get-tuple-element.64), channel_id=1, source_target_pairs={{0,4},{4,0},{1,5},{5,1},{2,6},{6,2},{3,7},{7,3},{8,12},{12,8},{9,1... | collective-permute-start | bytes 49160 | tf_op jit(solution)/shard_map/ppermute | solution.py:429
  3.4 0.0 copy-done
  3.4 0.0 copy-done.4
  3.4 0.6 %shard_map.86 = (f32[128,16,256]{2,1,0:T(8,128)S(1)}, f32[16,256]{1,0:T(8,128)S(1)}, f32[2,136,128]{2,1,0:T(8,128)S(1)}, f32[2,136,128]{2,1,0:T(8,128)S(1)}, f32...) custom-call(bf16[1,128,1024]{2,1,0:T(8,128)(2,1)S(1)} %copy-done.1, ...), custom_call_target="tpu_custom_call" | custom-call | flops 2621440 | bytes 2097152 | tf_op jit(solution)/shard_map/pallas_call | solution.py:376
  4.0 0.2 collective-permute-start.4
  4.3 0.0 collective-permute-done.refs_0_
  4.3 1.7 %shard_map.85 = (bf16[128,128]{1,0:T(8,128)(2,1)S(1)}, bf16[128,128]{1,0:T(8,128)(2,1)S(1)}, bf16[128,128]{1,0:T(8,128)(2,1)S(1)}, bf16[128,128]{1,0:T(8,128)(2,...) custom-call(f32[16,256]{1,0:T(8,128)S(1)} %collective-permute-done.refs_0_, ...), custom_call_target="tpu_custom_call" | custom-call | flops 10485760 | bytes 2097152 | tf_op jit(solution)/shard_map/pallas_call | solution.py:397
  5.9 3.0 %collective-permute-start.1 = (bf16[128,128]{1,0:T(8,128)(2,1)S(1)}, bf16[128,128]{1,0:T(8,128)(2,1)S(1)}, u32[]{:S(2)}, u32[]{:S(2)}) collective-permute-start(bf16[128,128]{1,0:T(8,128)(2,1)S(1)} %get-tuple-element.74), channel_id=1, source_target_pairs={{0,1},{1,0},{2,3},{3,2},{4,5},{5,4},{6,7},{7,6},{8,9},{9,8},{10,11... | collective-permute-start | bytes 98312 | tf_op jit(solution)/shard_map/ppermute | solution.py:436
  8.9 2.6 %collective-permute-start.2 = (bf16[128,128]{1,0:T(8,128)(2,1)S(1)}, bf16[128,128]{1,0:T(8,128)(2,1)S(1)}, u32[]{:S(2)}, u32[]{:S(2)}) collective-permute-start(bf16[128,128]{1,0:T(8,128)(2,1)S(1)} %get-tuple-element.75), channel_id=1, source_target_pairs={{0,2},{1,3},{2,0},{3,1},{4,6},{5,7},{6,4},{7,5},{8,10},{9,11},{10,... | collective-permute-start | bytes 98312 | tf_op jit(solution)/shard_map/ppermute | solution.py:436
  11.5 0.6 %shard_map.88 = (f32[128,16,256]{2,1,0:T(8,128)S(1)}, f32[16,256]{1,0:T(8,128)S(1)}, f32[2,136,128]{2,1,0:T(8,128)S(1)}, f32[2,136,128]{2,1,0:T(8,128)S(1)}, f32...) custom-call(bf16[1,128,1024]{2,1,0:T(8,128)(2,1)S(1)} %copy-done.1, ...), custom_call_target="tpu_custom_call" | custom-call | flops 2621440 | bytes 2097152 | tf_op jit(solution)/shard_map/pallas_call | solution.py:376
  12.1 0.1 collective-permute-start.8
  12.2 0.0 collective-permute-done.4.refs_0_
  12.2 1.7 %shard_map.87 = (bf16[128,128]{1,0:T(8,128)(2,1)S(1)}, bf16[128,128]{1,0:T(8,128)(2,1)S(1)}, bf16[128,128]{1,0:T(8,128)(2,1)S(1)}, bf16[128,128]{1,0:T(8,128)(2,...) custom-call(f32[16,256]{1,0:T(8,128)S(1)} %collective-permute-done.4.refs_0_, ...), custom_call_target="tpu_custom_call" | custom-call | flops 10485760 | bytes 2097152 | tf_op jit(solution)/shard_map/pallas_call | solution.py:397
  13.9 0.6 %shard_map.90 = (f32[128,16,256]{2,1,0:T(8,128)S(1)}, f32[16,256]{1,0:T(8,128)S(1)}, f32[2,136,128]{2,1,0:T(8,128)S(1)}, f32[2,136,128]{2,1,0:T(8,128)S(1)}, f32...) custom-call(bf16[1,128,1024]{2,1,0:T(8,128)(2,1)S(1)} %copy-done.1, ...), custom_call_target="tpu_custom_call" | custom-call | flops 2621440 | bytes 2097152 | tf_op jit(solution)/shard_map/pallas_call | solution.py:376
  14.5 0.6 %collective-permute-start.12 = (f32[16,256]{1,0:T(8,128)S(1)}, f32[16,256]{1,0:T(8,128)S(1)}, u32[]{:S(2)}, u32[]{:S(2)}) collective-permute-start(f32[16,256]{1,0:T(8,128)S(1)} %get-tuple-element.105), channel_id=1, source_target_pairs={{0,4},{4,0},{1,5},{5,1},{2,6},{6,2},{3,7},{7,3},{8,12},{12,8},{9,1... | collective-permute-start | bytes 49160 | tf_op jit(solution)/shard_map/ppermute | solution.py:429
  15.1 0.0 collective-permute-start.3
  15.1 0.0 collective-permute-done.8.refs_0_
  15.1 0.9 %collective-permute-start.5 = (bf16[128,128]{1,0:T(8,128)(2,1)S(1)}, bf16[128,128]{1,0:T(8,128)(2,1)S(1)}, u32[]{:S(2)}, u32[]{:S(2)}) collective-permute-start(bf16[128,128]{1,0:T(8,128)(2,1)S(1)} %get-tuple-element.88), channel_id=1, source_target_pairs={{0,1},{1,0},{2,3},{3,2},{4,5},{5,4},{6,7},{7,6},{8,9},{9,8},{10,11... | collective-permute-start | bytes 98312 | tf_op jit(solution)/shard_map/ppermute | solution.py:436
  16.0 0.0 collective-permute-done.12.refs_0_
  16.0 3.5 %collective-permute-start.6 = (bf16[128,128]{1,0:T(8,128)(2,1)S(1)}, bf16[128,128]{1,0:T(8,128)(2,1)S(1)}, u32[]{:S(2)}, u32[]{:S(2)}) collective-permute-start(bf16[128,128]{1,0:T(8,128)(2,1)S(1)} %get-tuple-element.89), channel_id=1, source_target_pairs={{0,2},{1,3},{2,0},{3,1},{4,6},{5,7},{6,4},{7,5},{8,10},{9,11},{10,... | collective-permute-start | bytes 98312 | tf_op jit(solution)/shard_map/ppermute | solution.py:436
  19.5 1.7 %shard_map.89 = (bf16[128,128]{1,0:T(8,128)(2,1)S(1)}, bf16[128,128]{1,0:T(8,128)(2,1)S(1)}, bf16[128,128]{1,0:T(8,128)(2,1)S(1)}, bf16[128,128]{1,0:T(8,128)(2,...) custom-call(f32[16,256]{1,0:T(8,128)S(1)} %collective-permute-done.8.refs_0_, ...), custom_call_target="tpu_custom_call" | custom-call | flops 10485760 | bytes 2097152 | tf_op jit(solution)/shard_map/pallas_call | solution.py:397
  21.2 0.0 collective-permute-done.1.refs_1_
  21.2 0.1 collective-permute-start.7
  21.3 0.0 collective-permute-done.2.refs_2_
  21.3 0.5 %collective-permute-start.9 = (bf16[128,128]{1,0:T(8,128)(2,1)S(1)}, bf16[128,128]{1,0:T(8,128)(2,1)S(1)}, u32[]{:S(2)}, u32[]{:S(2)}) collective-permute-start(bf16[128,128]{1,0:T(8,128)(2,1)S(1)} %get-tuple-element.102), channel_id=1, source_target_pairs={{0,1},{1,0},{2,3},{3,2},{4,5},{5,4},{6,7},{7,6},{8,9},{9,8},{10,11... | collective-permute-start | bytes 98312 | tf_op jit(solution)/shard_map/ppermute | solution.py:436
  21.8 3.9 %shard_map.91 = (bf16[144,128]{1,0:T(8,128)(2,1)S(1)}, bf16[144,128]{1,0:T(8,128)(2,1)S(1)}, bf16[144,128]{1,0:T(8,128)(2,1)S(1)}, bf16[144,128]{1,0:T(8,128)(2,...) custom-call(f32[16,256]{1,0:T(8,128)S(1)} %collective-permute-done.12.refs_0_, ...), custom_call_target="tpu_custom_call" | custom-call | flops 10485760 | bytes 2097152 | tf_op jit(solution)/shard_map/pallas_call | solution.py:397
  25.7 0.0 collective-permute-done.3.refs_3_
  25.7 1.5 %collective-permute-start.13 = (bf16[144,128]{1,0:T(8,128)(2,1)S(1)}, bf16[144,128]{1,0:T(8,128)(2,1)S(1)}, u32[]{:S(2)}, u32[]{:S(2)}) collective-permute-start(bf16[144,128]{1,0:T(8,128)(2,1)S(1)} %get-tuple-element.117), channel_id=1, source_target_pairs={{0,1},{1,0},{2,3},{3,2},{4,5},{5,4},{6,7},{7,6},{8,9},{9,8},{10,11... | collective-permute-start | bytes 110600 | tf_op jit(solution)/shard_map/ppermute | solution.py:436
  27.3 0.0 collective-permute-done.5.refs_5_
  27.3 2.3 %collective-permute-start.14 = (bf16[144,128]{1,0:T(8,128)(2,1)S(1)}, bf16[144,128]{1,0:T(8,128)(2,1)S(1)}, u32[]{:S(2)}, u32[]{:S(2)}) collective-permute-start(bf16[144,128]{1,0:T(8,128)(2,1)S(1)} %get-tuple-element.118), channel_id=1, source_target_pairs={{0,2},{1,3},{2,0},{3,1},{4,6},{5,7},{6,4},{7,5},{8,10},{9,11},{10,... | collective-permute-start | bytes 110600 | tf_op jit(solution)/shard_map/ppermute | solution.py:436
  29.6 0.0 collective-permute-done.6.refs_6_
  29.6 1.5 %collective-permute-start.15 = (bf16[144,128]{1,0:T(8,128)(2,1)S(1)}, bf16[144,128]{1,0:T(8,128)(2,1)S(1)}, u32[]{:S(2)}, u32[]{:S(2)}) collective-permute-start(bf16[144,128]{1,0:T(8,128)(2,1)S(1)} %get-tuple-element.119), channel_id=1, source_target_pairs={{0,3},{1,2},{2,1},{3,0},{4,7},{5,6},{6,5},{7,4},{8,11},{9,10},{10,... | collective-permute-start | bytes 110600 | tf_op jit(solution)/shard_map/ppermute | solution.py:436
  31.1 0.0 collective-permute-done.7.refs_7_
  31.1 2.0 %collective-permute-start.10 = (bf16[128,128]{1,0:T(8,128)(2,1)S(1)}, bf16[128,128]{1,0:T(8,128)(2,1)S(1)}, u32[]{:S(2)}, u32[]{:S(2)}) collective-permute-start(bf16[128,128]{1,0:T(8,128)(2,1)S(1)} %get-tuple-element.103), channel_id=1, source_target_pairs={{0,2},{1,3},{2,0},{3,1},{4,6},{5,7},{6,4},{7,5},{8,10},{9,11},{10,... | collective-permute-start | bytes 98312 | tf_op jit(solution)/shard_map/ppermute | solution.py:436
  33.1 0.0 collective-permute-done.9.refs_9_
  33.1 1.0 %collective-permute-start.11 = (bf16[128,128]{1,0:T(8,128)(2,1)S(1)}, bf16[128,128]{1,0:T(8,128)(2,1)S(1)}, u32[]{:S(2)}, u32[]{:S(2)}) collective-permute-start(bf16[128,128]{1,0:T(8,128)(2,1)S(1)} %get-tuple-element.104), channel_id=1, source_target_pairs={{0,3},{1,2},{2,1},{3,0},{4,7},{5,6},{6,5},{7,4},{8,11},{9,10},{10,... | collective-permute-start | bytes 98312 | tf_op jit(solution)/shard_map/ppermute | solution.py:436
  34.0 2.4 %collective-permute-done.10.refs_10_ = bf16[128,128]{1,0:T(8,128)(2,1)S(1)} collective-permute-done((bf16[128,128]{1,0:T(8,128)(2,1)S(1)}, bf16[128,128]{1,0:T(8,128)(2,1)S(1)}, u32[]{:S(2)}, u32[]{:S(2)}) %collective-permute-start.10) | collective-permute-done | bytes 32800 | tf_op jit(solution)/shard_map/ppermute | solution.py:436
  36.4 2.3 %collective-permute-done.11.refs_11_ = bf16[128,128]{1,0:T(8,128)(2,1)S(1)} collective-permute-done((bf16[128,128]{1,0:T(8,128)(2,1)S(1)}, bf16[128,128]{1,0:T(8,128)(2,1)S(1)}, u32[]{:S(2)}, u32[]{:S(2)}) %collective-permute-start.11) | collective-permute-done | bytes 32800 | tf_op jit(solution)/shard_map/ppermute | solution.py:436
  38.8 0.0 collective-permute-done.13.refs_13_
  38.8 0.0 collective-permute-done.14.refs_14_
  38.8 0.0 collective-permute-done.15.refs_15_
  38.8 0.9 %shard_map.92 = (bf16[1,32,4096]{2,1,0:T(8,128)(2,1)}, bf16[1,32,4096]{2,1,0:T(8,128)(2,1)}, f32[1,16,32]{2,1,0:T(8,128)}, f32[1,16,32]{2,1,0:T(8,128)}) custom-call(bf16[128,128]{1,0:T(8,128)(2,1)S(1)} %get-tuple-element.73.refs_0_, bf16[128,128]{1,0:T(8,128)(2,1)S(1)} %collective-permute-done.1.refs_1_, ...), custom_call_target="tpu_custom_call" | custom-call | tf_op jit(solution)/shard_map/pallas_call | solution.py:438
  (3 shorter events, 0.0 us)
Async XLA Ops:
  0.6 2.8 %copy-start.1 = (bf16[1,128,1024]{2,1,0:T(8,128)(2,1)S(1)}, bf16[1,128,1024]{2,1,0:T(8,128)(2,1)}, u32[]{:S(2)}) copy-start(bf16[1,128,1024]{2,1,0:T(8,128)(2,1)} %refs_0_.7) | copy-start | bytes 786436
  0.6 2.8 %copy-start = (f32[1,128,1024]{2,1,0:T(8,128)S(1)}, f32[1,128,1024]{2,1,0:T(8,128)}, u32[]{:S(2)}) copy-start(f32[1,128,1024]{2,1,0:T(8,128)} %refs_1_.7) | copy-start | bytes 1572868
  0.7 2.8 %copy-start.3 = (bf16[1,128,16]{1,2,0:T(8,128)(2,1)S(1)}, bf16[1,128,16]{1,2,0:T(8,128)(2,1)}, u32[]{:S(2)}) copy-start(bf16[1,128,16]{1,2,0:T(8,128)(2,1)} %param.7) | copy-start | bytes 12292
  0.7 2.8 %copy-start.4 = (bf16[1,128,16]{1,2,0:T(8,128)(2,1)S(1)}, bf16[1,128,16]{1,2,0:T(8,128)(2,1)}, u32[]{:S(2)}) copy-start(bf16[1,128,16]{1,2,0:T(8,128)(2,1)} %param.8) | copy-start | bytes 12292
  0.7 2.8 %copy-start.2 = (bf16[1,128,1024]{2,1,0:T(8,128)(2,1)S(1)}, bf16[1,128,1024]{2,1,0:T(8,128)(2,1)}, u32[]{:S(2)}) copy-start(bf16[1,128,1024]{2,1,0:T(8,128)(2,1)} %refs_4_.7) | copy-start | bytes 786436
  2.8 1.5 %collective-permute-start = (f32[16,256]{1,0:T(8,128)S(1)}, f32[16,256]{1,0:T(8,128)S(1)}, u32[]{:S(2)}, u32[]{:S(2)}) collective-permute-start(f32[16,256]{1,0:T(8,128)S(1)} %get-tuple-element.64), channel_id=1, source_target_pairs={{0,4},{4,0},{1,5},{5,1},{2,6},{6,2},{3,7},{7,3},{8,12},{12,8},{9,1... | collective-permute-start | bytes 49160 | tf_op jit(solution)/shard_map/ppermute | solution.py:429
  4.0 8.2 %collective-permute-start.4 = (f32[16,256]{1,0:T(8,128)S(1)}, f32[16,256]{1,0:T(8,128)S(1)}, u32[]{:S(2)}, u32[]{:S(2)}) collective-permute-start(f32[16,256]{1,0:T(8,128)S(1)} %get-tuple-element.77), channel_id=1, source_target_pairs={{0,4},{4,0},{1,5},{5,1},{2,6},{6,2},{3,7},{7,3},{8,12},{12,8},{9,1... | collective-permute-start | bytes 49160 | tf_op jit(solution)/shard_map/ppermute | solution.py:429
  5.9 15.2 %collective-permute-start.1 = (bf16[128,128]{1,0:T(8,128)(2,1)S(1)}, bf16[128,128]{1,0:T(8,128)(2,1)S(1)}, u32[]{:S(2)}, u32[]{:S(2)}) collective-permute-start(bf16[128,128]{1,0:T(8,128)(2,1)S(1)} %get-tuple-element.74), channel_id=1, source_target_pairs={{0,1},{1,0},{2,3},{3,2},{4,5},{5,4},{6,7},{7,6},{8,9},{9,8},{10,11... | collective-permute-start | bytes 98312 | tf_op jit(solution)/shard_map/ppermute | solution.py:436
  8.9 12.3 %collective-permute-start.2 = (bf16[128,128]{1,0:T(8,128)(2,1)S(1)}, bf16[128,128]{1,0:T(8,128)(2,1)S(1)}, u32[]{:S(2)}, u32[]{:S(2)}) collective-permute-start(bf16[128,128]{1,0:T(8,128)(2,1)S(1)} %get-tuple-element.75), channel_id=1, source_target_pairs={{0,2},{1,3},{2,0},{3,1},{4,6},{5,7},{6,4},{7,5},{8,10},{9,11},{10,... | collective-permute-start | bytes 98312 | tf_op jit(solution)/shard_map/ppermute | solution.py:436
  12.1 3.0 %collective-permute-start.8 = (f32[16,256]{1,0:T(8,128)S(1)}, f32[16,256]{1,0:T(8,128)S(1)}, u32[]{:S(2)}, u32[]{:S(2)}) collective-permute-start(f32[16,256]{1,0:T(8,128)S(1)} %get-tuple-element.91), channel_id=1, source_target_pairs={{0,4},{4,0},{1,5},{5,1},{2,6},{6,2},{3,7},{7,3},{8,12},{12,8},{9,1... | collective-permute-start | bytes 49160 | tf_op jit(solution)/shard_map/ppermute | solution.py:429
  14.5 1.5 %collective-permute-start.12 = (f32[16,256]{1,0:T(8,128)S(1)}, f32[16,256]{1,0:T(8,128)S(1)}, u32[]{:S(2)}, u32[]{:S(2)}) collective-permute-start(f32[16,256]{1,0:T(8,128)S(1)} %get-tuple-element.105), channel_id=1, source_target_pairs={{0,4},{4,0},{1,5},{5,1},{2,6},{6,2},{3,7},{7,3},{8,12},{12,8},{9,1... | collective-permute-start | bytes 49160 | tf_op jit(solution)/shard_map/ppermute | solution.py:429
  15.1 10.7 %collective-permute-start.3 = (bf16[128,128]{1,0:T(8,128)(2,1)S(1)}, bf16[128,128]{1,0:T(8,128)(2,1)S(1)}, u32[]{:S(2)}, u32[]{:S(2)}) collective-permute-start(bf16[128,128]{1,0:T(8,128)(2,1)S(1)} %get-tuple-element.76), channel_id=1, source_target_pairs={{0,3},{1,2},{2,1},{3,0},{4,7},{5,6},{6,5},{7,4},{8,11},{9,10},{10,... | collective-permute-start | bytes 98312 | tf_op jit(solution)/shard_map/ppermute | solution.py:436
  15.1 12.2 %collective-permute-start.5 = (bf16[128,128]{1,0:T(8,128)(2,1)S(1)}, bf16[128,128]{1,0:T(8,128)(2,1)S(1)}, u32[]{:S(2)}, u32[]{:S(2)}) collective-permute-start(bf16[128,128]{1,0:T(8,128)(2,1)S(1)} %get-tuple-element.88), channel_id=1, source_target_pairs={{0,1},{1,0},{2,3},{3,2},{4,5},{5,4},{6,7},{7,6},{8,9},{9,8},{10,11... | collective-permute-start | bytes 98312 | tf_op jit(solution)/shard_map/ppermute | solution.py:436
  16.0 13.7 %collective-permute-start.6 = (bf16[128,128]{1,0:T(8,128)(2,1)S(1)}, bf16[128,128]{1,0:T(8,128)(2,1)S(1)}, u32[]{:S(2)}, u32[]{:S(2)}) collective-permute-start(bf16[128,128]{1,0:T(8,128)(2,1)S(1)} %get-tuple-element.89), channel_id=1, source_target_pairs={{0,2},{1,3},{2,0},{3,1},{4,6},{5,7},{6,4},{7,5},{8,10},{9,11},{10,... | collective-permute-start | bytes 98312 | tf_op jit(solution)/shard_map/ppermute | solution.py:436
  21.2 9.9 %collective-permute-start.7 = (bf16[128,128]{1,0:T(8,128)(2,1)S(1)}, bf16[128,128]{1,0:T(8,128)(2,1)S(1)}, u32[]{:S(2)}, u32[]{:S(2)}) collective-permute-start(bf16[128,128]{1,0:T(8,128)(2,1)S(1)} %get-tuple-element.90), channel_id=1, source_target_pairs={{0,3},{1,2},{2,1},{3,0},{4,7},{5,6},{6,5},{7,4},{8,11},{9,10},{10,... | collective-permute-start | bytes 98312 | tf_op jit(solution)/shard_map/ppermute | solution.py:436
  21.3 11.8 %collective-permute-start.9 = (bf16[128,128]{1,0:T(8,128)(2,1)S(1)}, bf16[128,128]{1,0:T(8,128)(2,1)S(1)}, u32[]{:S(2)}, u32[]{:S(2)}) collective-permute-start(bf16[128,128]{1,0:T(8,128)(2,1)S(1)} %get-tuple-element.102), channel_id=1, source_target_pairs={{0,1},{1,0},{2,3},{3,2},{4,5},{5,4},{6,7},{7,6},{8,9},{9,8},{10,11... | collective-permute-start | bytes 98312 | tf_op jit(solution)/shard_map/ppermute | solution.py:436
  25.7 13.0 %collective-permute-start.13 = (bf16[144,128]{1,0:T(8,128)(2,1)S(1)}, bf16[144,128]{1,0:T(8,128)(2,1)S(1)}, u32[]{:S(2)}, u32[]{:S(2)}) collective-permute-start(bf16[144,128]{1,0:T(8,128)(2,1)S(1)} %get-tuple-element.117), channel_id=1, source_target_pairs={{0,1},{1,0},{2,3},{3,2},{4,5},{5,4},{6,7},{7,6},{8,9},{9,8},{10,11... | collective-permute-start | bytes 110600 | tf_op jit(solution)/shard_map/ppermute | solution.py:436
  27.3 11.5 %collective-permute-start.14 = (bf16[144,128]{1,0:T(8,128)(2,1)S(1)}, bf16[144,128]{1,0:T(8,128)(2,1)S(1)}, u32[]{:S(2)}, u32[]{:S(2)}) collective-permute-start(bf16[144,128]{1,0:T(8,128)(2,1)S(1)} %get-tuple-element.118), channel_id=1, source_target_pairs={{0,2},{1,3},{2,0},{3,1},{4,6},{5,7},{6,4},{7,5},{8,10},{9,11},{10,... | collective-permute-start | bytes 110600 | tf_op jit(solution)/shard_map/ppermute | solution.py:436
  29.6 9.1 %collective-permute-start.15 = (bf16[144,128]{1,0:T(8,128)(2,1)S(1)}, bf16[144,128]{1,0:T(8,128)(2,1)S(1)}, u32[]{:S(2)}, u32[]{:S(2)}) collective-permute-start(bf16[144,128]{1,0:T(8,128)(2,1)S(1)} %get-tuple-element.119), channel_id=1, source_target_pairs={{0,3},{1,2},{2,1},{3,0},{4,7},{5,6},{6,5},{7,4},{8,11},{9,10},{10,... | collective-permute-start | bytes 110600 | tf_op jit(solution)/shard_map/ppermute | solution.py:436
  31.1 5.3 %collective-permute-start.10 = (bf16[128,128]{1,0:T(8,128)(2,1)S(1)}, bf16[128,128]{1,0:T(8,128)(2,1)S(1)}, u32[]{:S(2)}, u32[]{:S(2)}) collective-permute-start(bf16[128,128]{1,0:T(8,128)(2,1)S(1)} %get-tuple-element.103), channel_id=1, source_target_pairs={{0,2},{1,3},{2,0},{3,1},{4,6},{5,7},{6,4},{7,5},{8,10},{9,11},{10,... | collective-permute-start | bytes 98312 | tf_op jit(solution)/shard_map/ppermute | solution.py:436
  33.1 5.7 %collective-permute-start.11 = (bf16[128,128]{1,0:T(8,128)(2,1)S(1)}, bf16[128,128]{1,0:T(8,128)(2,1)S(1)}, u32[]{:S(2)}, u32[]{:S(2)}) collective-permute-start(bf16[128,128]{1,0:T(8,128)(2,1)S(1)} %get-tuple-element.104), channel_id=1, source_target_pairs={{0,3},{1,2},{2,1},{3,0},{4,7},{5,6},{6,5},{7,4},{8,11},{9,10},{10,... | collective-permute-start | bytes 98312 | tf_op jit(solution)/shard_map/ppermute | solution.py:436

commit v3 on v2

--- a/solution.py
+++ b/solution.py
@@ -11,8 +11,8 @@
 LANES = 128
 SUB = 8
 UNROLL = 8
-CHUNKS = 4
-AHEAD = 1
+FIRST_TILES = 5
+DELAYED = (1,)
 VMEM_LIMIT = 20 * 1024 * 1024
 
 
@@ -88,30 +88,23 @@
 
 
 def lane_sums(values):
-    ones = jnp.ones((SUB, LANES), jnp.bfloat16)
-
-    def product(part):
-        return lax.dot_general(
-            ones, part, (((1,), (1,)), ((), ())), preferred_element_type=jnp.float32
-        )
-
     high = values.astype(jnp.bfloat16)
     low = (values - high.astype(jnp.float32)).astype(jnp.bfloat16)
-    return product(high) + product(low)
-
-
-def first_kernel(backwards, has_entry, has_tables, has_earlier, *refs):
+    both = jnp.concatenate([high, low], axis=1)
+    ones = jnp.ones((2 * LANES, LANES), jnp.bfloat16)
+    return jnp.dot(both, ones, preferred_element_type=jnp.float32)
+
+
+def first_kernel(offset, width, backwards, has_entry, has_tables, *refs):
     refs = list(refs)
     x_ref, rate_ref, key_ref, query_ref, go_ref = refs[:5]
     del refs[:5]
     entry_ref = refs.pop(0) if has_entry else None
     given = [refs.pop(0), refs.pop(0)] if has_tables else None
-    if has_earlier:
-        del refs[0]
     path_ref, end_ref, step_ref, drive_ref, x32_ref, go32_ref, inverse_ref = refs[:7]
     keys_ref, queries_ref = given or refs[7:9]
     states, tokens = key_ref.shape[1:]
-    tiles = x_ref.shape[2] // LANES
+    tiles = width // LANES
     key = key_ref[0].astype(jnp.float32)
     if not has_tables:
         refs[9][...] = key
@@ -120,15 +113,16 @@
     key_norm = jnp.sum(key * key, axis=0, keepdims=True)
     norm = jnp.transpose(jnp.broadcast_to(key_norm, (LANES, tokens)))
     for j in range(tiles):
-        rate = rate_ref[0, :, tile_at(j)]
-        x = x_ref[0, :, tile_at(j)].astype(jnp.float32)
+        at = pl.ds(offset + j * LANES, LANES)
+        rate = rate_ref[0, :, at]
+        x = x_ref[0, :, at].astype(jnp.float32)
         inverse = 1.0 / (1.0 + rate * norm)
         step = rate * inverse
         inverse_ref[j, :tokens] = inverse
         step_ref[j, :tokens] = step
         x32_ref[j, :tokens] = x
         drive_ref[j, :tokens] = step * x
-        go32_ref[j, :tokens] = go_ref[0, :, tile_at(j)].astype(jnp.float32)
+        go32_ref[j, :tokens] = go_ref[0, :, at].astype(jnp.float32)
 
     if has_entry:
         entry = [halves(entry_ref[:, tile_at(j)]) for j in range(tiles)]
@@ -186,14 +180,16 @@
         (if_set if flag else if_not)()
 
 
-def second_kernel(onwards_here, last, heads, has_start, has_before, *refs):
+def second_kernel(onwards_here, last, heads, has_start, *refs):
     refs = list(refs)
     entry_ref, path_ref, step_ref, drive_ref, x32_ref, go32_ref, inverse_ref = refs[:7]
     keys_ref, queries_ref = refs[7:9]
     del refs[:9]
     start_ref = refs.pop(0) if has_start else None
-    before = [refs.pop(0) for _ in range(3)] if has_before else None
+    before = [refs.pop(0) for _ in range(3)] if last else None
     key_ref = refs.pop(0) if last else None
+    if not last:
+        del refs[0]
     piece_refs = refs[:heads]
     key_part_ref, query_part_ref, norm_ref, dot_ref, weighted_ref = refs[heads : heads + 5]
     tokens, states = keys_ref.shape[:2]
@@ -235,7 +231,7 @@
                     by_drive, by_decay, by_query = sums[3 * h : 3 * h + 3]
                     at = pl.ds(pl.multiple_of(t * states + h * SUB, SUB), SUB)
                     by_key = by_drive - (2.0 * k[h]) * by_decay
-                    if has_before:
+                    if last:
                         by_key = by_key + before[0][at, :]
                         by_query = by_query + before[1][at, :]
                     key_part_ref[at, :] = by_key
@@ -262,10 +258,11 @@
     part = tokens // heads
     rows = 2 * SUB
     position = lax.axis_index("head")
+    width = tiles * LANES
     for d in range(heads):
         for r in range(part // rows):
             base = pl.multiple_of((position ^ d) * part + r * rows, rows)
-            norm_sum = before[2][pl.ds(base, rows), :] if has_before else None
+            norm_sum = before[2][pl.ds(base, rows), :] if last else None
             for j in range(tiles):
                 dot, weighted = (
                     sum(ref[j, pl.ds(base * SUB + s, rows, stride=SUB), :] for s in range(SUB))
@@ -276,10 +273,14 @@
                 )
                 grad_step = x * dot - weighted
                 grad_rate = grad_step * inverse * inverse
-                to = j * part + r * rows
-                piece_refs[d][pl.ds(to, rows), :] = (step * dot).astype(jnp.bfloat16)
-                to += tiles * part
-                piece_refs[d][pl.ds(to, rows), :] = grad_rate.astype(jnp.bfloat16)
+                to = j * LANES
+                piece_refs[d][pl.ds(r * rows, rows), pl.ds(to, LANES)] = (step * dot).astype(
+                    jnp.bfloat16
+                )
+                to += width
+                piece_refs[d][pl.ds(r * rows, rows), pl.ds(to, LANES)] = grad_rate.astype(
+                    jnp.bfloat16
+                )
                 term = grad_step * step * step
                 norm_sum = term if norm_sum is None else norm_sum + term
             norm_ref[pl.ds(base, rows), :] = norm_sum
@@ -287,13 +288,24 @@
         return
 
     key = key_ref[...]
-    norm_row = lane_sums(norm_ref[...])[:1]
+    lane = lax.broadcasted_iota(jnp.int32, (tokens, tokens), 1)
+    own_row = lane == lax.broadcasted_iota(jnp.int32, (tokens, tokens), 0)
+    norm_sums = jnp.where(own_row, lane_sums(norm_ref[...]), 0.0)
+    norm_row = jnp.sum(norm_sums, axis=0, keepdims=True)
+    lane = lax.broadcasted_iota(jnp.int32, (states, tokens), 1)
+    totals = []
+    for ref in (key_part_ref, query_part_ref):
+        total = jnp.zeros((states, tokens), jnp.float32)
+        for b in range(tokens // UNROLL):
+            sums = lane_sums(ref[pl.ds(b * UNROLL * states, UNROLL * states), :])
+            for u in range(UNROLL):
+                total = jnp.where(
+                    lane == b * UNROLL + u, sums[u * states : (u + 1) * states], total
+                )
+        totals.append(total)
     sums_ref = refs[heads + 5]
-    for n in range(states):
-        at = pl.ds(n, tokens, stride=states)
-        sums_ref[n : n + 1, :] = lane_sums(key_part_ref[at, :])[:1]
-        sums_ref[states + n : states + n + 1, :] = lane_sums(query_part_ref[at, :])[:1]
-    sums_ref[:states] = sums_ref[:states] - 2.0 * key * norm_row
+    sums_ref[:states] = totals[0] - 2.0 * key * norm_row
+    sums_ref[states:] = totals[1]
     quarters = 2 * states // SUB
     lane = lax.broadcasted_iota(jnp.int32, (SUB, tokens), 1) // part
     for d in range(heads):
@@ -306,33 +318,63 @@
             packed = turned if packed is None else jnp.where(lane == i, turned, packed)
         high = packed.astype(jnp.bfloat16).astype(jnp.float32)
         both = jnp.concatenate([high, packed - high], axis=0).astype(jnp.bfloat16)
-        piece_refs[d][pl.ds(2 * tiles * part, rows), :] = both
-
-
-def gather_kernel(heads, chunks, *refs):
-    pieces, (in_ref, rate_ref, key_ref, query_ref) = refs[:-4], refs[-4:]
+        tail = pl.ds(2 * width, LANES)
+        piece_refs[d][:rows, tail] = both
+        piece_refs[d][rows:, tail] = jnp.zeros((part - rows, LANES), jnp.bfloat16)
+
+
+def place(out_refs, piece, d, offset, width, channels, semaphores):
+    at = pl.multiple_of((lax.axis_index("head") ^ d) * channels + offset, LANES)
+    copies = []
+    for i, out in enumerate(out_refs):
+        copies.append(
+            pltpu.make_async_copy(
+                piece.at[:, pl.ds(i * width, width)],
+                out.at[0, :, pl.ds(at, width)],
+                semaphores.at[i],
+            )
+        )
+        copies[-1].start()
+    return copies
+
+
+def early_kernel(distances, channels, *refs):
+    pieces, out_refs, semaphores = refs[:-3], refs[-3:-1], refs[-1]
+    width = pieces[0].shape[1] // 2
+    copies = []
+    for piece, d in zip(pieces, distances):
+        copies += place(out_refs, piece, d, 0, width, channels, semaphores.at[d])
+    for copy in copies:
+        copy.wait()
+
+
+def late_kernel(heads, distances, channels, *refs):
+    pieces = refs[:heads][::-1]
+    others = refs[heads : heads + len(distances)]
+    *out_refs, key_ref, query_ref, semaphores = refs[heads + len(distances) + 2 :]
     states, part = key_ref.shape[1:]
-    channels = in_ref.shape[2] // heads
-    width = channels // chunks
-    position = lax.axis_index("head")
-    tiles = width // LANES
+    width = (pieces[0].shape[1] - LANES) // 2
+    copies = []
+    for d in range(heads):
+        copies += place(
+            out_refs, pieces[d], d, channels - width, width, channels, semaphores.at[d]
+        )
+    for i, d in enumerate(distances):
+        copies += place(
+            out_refs, others[i], d, 0, channels - width, channels, semaphores.at[heads + i]
+        )
     total = None
-    for c in range(chunks):
-        for d in range(heads):
-            piece = pieces[c * heads + d]
-            at = pl.multiple_of((position ^ d) * channels + c * width, LANES)
-            for j in range(tiles):
-                to = pl.ds(at + j * LANES, LANES)
-                in_ref[0, :, to] = piece[pl.ds(j * part, part), :]
-                rate_ref[0, :, to] = piece[pl.ds((tiles + j) * part, part), :]
-            if c == chunks - 1:
-                both = piece[pl.ds(2 * tiles * part, 2 * SUB), :].astype(jnp.float32)
-                both = both[:SUB] + both[SUB:]
-                total = both if total is None else total + both
+    for d in range(heads):
+        tail = pl.ds(2 * width, LANES)
+        both = pieces[d][: 2 * SUB, tail].astype(jnp.float32)
+        both = both[:SUB] + both[SUB:]
+        total = both if total is None else total + both
     for i in range(states // SUB):
         key_ref[0, SUB * i : SUB * i + SUB] = total[:, i * part : (i + 1) * part]
         at = states // SUB + i
         query_ref[0, SUB * i : SUB * i + SUB] = total[:, at * part : (at + 1) * part]
+    for copy in copies:
+        copy.wait()
 
 
 def shards(inputs, step_rate, key_rows, query_rows, grad_out):
@@ -340,75 +382,77 @@
     states = key_rows.shape[2]
     heads = lax.axis_size("head")
     groups = lax.axis_size("ctx")
-    width = channels // CHUNKS
     part = tokens // heads
+    tiles = channels // LANES
+    first_width = tiles * FIRST_TILES // 8 * LANES
+    widths = (first_width, channels - first_width)
     key_cols = jnp.swapaxes(key_rows, 1, 2)
     query_cols = jnp.swapaxes(query_rows, 1, 2)
     f32 = jnp.float32
+    bf16 = jnp.bfloat16
     params = pltpu.CompilerParams(vmem_limit_bytes=VMEM_LIMIT)
     whole = pl.BlockSpec(memory_space=pltpu.VMEM)
-    plane = pltpu.VMEM((width // LANES, tokens + SUB, LANES), f32)
-
+    anywhere = pl.BlockSpec(memory_space=pl.ANY)
     table = pltpu.VMEM((tokens, states, LANES), f32)
 
-    def cost(passes):
+    def cost(width, passes):
         elements = tokens * states * width
-        return pl.CostEstimate(flops=passes * elements, bytes_accessed=4 * elements, transcendentals=0)
-
-    def first(c, backwards, tables=(), entry=None, earlier=None):
-        wide = pl.BlockSpec((1, tokens, width), lambda i: (0, 0, c))
-        specs = [wide, wide, whole, whole, wide]
+        return pl.CostEstimate(
+            flops=passes * elements, bytes_accessed=4 * elements, transcendentals=0
+        )
+
+    def first(c, backwards, tables=(), entry=None):
+        width = widths[c]
         arrays = [inputs, step_rate, key_cols, query_cols, grad_out]
+        specs = [whole] * 5
         if c == 0:
+            wide = pl.BlockSpec((1, tokens, width), lambda i: (0, 0, 0))
+            specs = [wide, wide, whole, whole, wide]
             arrays = [pltpu.with_memory_space_constraint(a, pltpu.HBM) for a in arrays]
-        for a in (entry, *tables[:2]):
-            if a is not None:
-                specs, arrays = specs + [whole], arrays + [a]
-        if earlier is not None:
-            specs, arrays = specs + [pl.BlockSpec(memory_space=pl.ANY)], arrays + [earlier]
+        extra = [*(() if entry is None else (entry,)), *tables[:2]]
         out_shape = [
             pltpu.VMEM((tokens, states, width), f32),
             jax.ShapeDtypeStruct((states, width), f32),
         ]
-        out_shape += [plane] * 5
+        out_shape += [pltpu.VMEM((width // LANES, tokens + SUB, LANES), f32)] * 5
         if not tables:
             out_shape += [table] * 2 + [pltpu.VMEM((states, tokens), f32)]
         path, end, *carried = pl.pallas_call(
             functools.partial(
-                first_kernel, backwards, entry is not None, bool(tables), earlier is not None
+                first_kernel, sum(widths[:c]), width, backwards, entry is not None, bool(tables)
             ),
             grid=(1,),
-            in_specs=specs,
+            in_specs=specs + [whole] * len(extra),
             out_specs=[whole] * len(out_shape),
             out_shape=out_shape,
             compiler_params=params,
-            cost_estimate=cost(5),
-        )(*arrays)
+            cost_estimate=cost(width, 5),
+        )(*arrays, *extra)
         return path, end, carried[:5], tuple(tables) or tuple(carried[5:])
 
     def second(c, onwards_here, entry, carried, tables, start, before):
-        last = c == CHUNKS - 1
+        width = widths[c]
+        last = c == 1
         keys, queries, key = tables
         extra = [*(() if start is None else (start,)), *before, *((key,) if last else ())]
+        specs = [whole] * (9 + len(extra))
+        if not last:
+            extra, specs = extra + [work[1][1][0]], specs + [anywhere]
         parts = pltpu.VMEM((width // LANES, (tokens + 1) * SUB, LANES), f32)
         sums = pltpu.VMEM(((tokens + 1) * states, LANES), f32)
-        size = 2 * part * width // LANES + (2 * SUB if last else 0)
-        piece = jax.ShapeDtypeStruct((size, LANES), jnp.bfloat16)
+        pieces = [jax.ShapeDtypeStruct((part, 2 * width + LANES * last), bf16)] * heads
         results = pl.pallas_call(
-            functools.partial(
-                second_kernel, onwards_here, last, heads, start is not None, bool(before)
-            ),
-            in_specs=[whole] * (9 + len(extra)),
+            functools.partial(second_kernel, onwards_here, last, heads, start is not None),
+            in_specs=specs,
             out_specs=[whole] * (heads + 3),
-            out_shape=[piece] * heads + [sums, sums, pltpu.VMEM((tokens, LANES), f32)],
+            out_shape=pieces + [sums, sums, pltpu.VMEM((tokens, LANES), f32)],
             scratch_shapes=[parts, parts] + [pltpu.VMEM((2 * states, tokens), f32)] * last,
             compiler_params=params,
-            cost_estimate=cost(20),
+            cost_estimate=cost(width, 20),
         )(entry, *carried, keys, queries, *extra)
         return results[:heads], results[heads:]
 
-    entries = starts = None
-    here = None
+    entries = starts = here = None
     if groups != 2:
         here = False
         product, end, back = group_summary(inputs, step_rate, key_rows, query_rows, grad_out)
@@ -417,36 +461,51 @@
         entries = prefix((product, back), "ctx", unit, True)[1]
 
     def part_of(array, c):
-        return None if array is None else array[:, c * width : (c + 1) * width]
-
-    tables, before, work, arrived = (), (), [], []
-    for c in range(CHUNKS + AHEAD):
-        if c < CHUNKS:
-            earlier = before[2] if before else None
-            path, end, carried, tables = first(c, here, tables, part_of(starts, c), earlier)
-            entry = part_of(entries, c)
-            if entry is None:
-                entry = lax.ppermute(end, "ctx", [(0, 1), (1, 0)])
-            work.append((entry, [path, *carried], part_of(starts, c)))
-        if c >= AHEAD:
-            entry, carried, start = work[c - AHEAD]
-            pieces, before = second(c - AHEAD, here, entry, carried, tables, start, before)
-            arrived.append(pieces[0])
-            for d in range(1, heads):
-                arrived.append(lax.ppermute(pieces[d], "head", [(s, s ^ d) for s in range(heads)]))
-
+        return None if array is None else array[:, sum(widths[:c]) : sum(widths[: c + 1])]
+
+    def send(piece, d):
+        return lax.ppermute(piece, "head", [(s, s ^ d) for s in range(heads)])
+
+    tables, work = (), []
+    for c in range(2):
+        path, end, carried, tables = first(c, here, tables, part_of(starts, c))
+        entry = part_of(entries, c)
+        if entry is None:
+            entry = lax.ppermute(end, "ctx", [(0, 1), (1, 0)])
+        work.append((entry, [path, *carried], part_of(starts, c)))
+
+    def call_second(c, before):
+        entry, carried, start = work[c]
+        return second(c, here, entry, carried, tables, start, before)
+
+    away = list(range(heads - 1, 0, -1))
+    pieces, before = call_second(0, ())
+    arrived = {d: send(pieces[d], d) for d in away}
+    arrived[0] = pieces[0]
+    early = [d for d in range(heads) if d not in DELAYED]
+    pieces, _ = call_second(1, before)
+    late = {d: send(pieces[d], d) for d in away}
+    late[0] = pieces[0]
+
+    out = [jax.ShapeDtypeStruct((1, part, heads * channels), bf16)] * 2
+    outs = pl.pallas_call(
+        functools.partial(early_kernel, early, channels),
+        in_specs=[whole] * len(early),
+        out_specs=[anywhere] * 2,
+        out_shape=out,
+        scratch_shapes=[pltpu.SemaphoreType.DMA((heads, 2))],
+        compiler_params=params,
+    )(*[arrived[d] for d in early])
+    pieces = [late[d] for d in reversed(range(heads))] + [arrived[d] for d in DELAYED]
     grad_in, grad_rate, grad_key, grad_query = pl.pallas_call(
-        functools.partial(gather_kernel, heads, CHUNKS),
-        in_specs=[whole] * len(arrived),
-        out_specs=[whole] * 4,
-        out_shape=[
-            jax.ShapeDtypeStruct((1, part, heads * channels), jnp.bfloat16),
-            jax.ShapeDtypeStruct((1, part, heads * channels), jnp.bfloat16),
-            jax.ShapeDtypeStruct((1, states, part), f32),
-            jax.ShapeDtypeStruct((1, states, part), f32),
-        ],
+        functools.partial(late_kernel, heads, DELAYED, channels),
+        in_specs=[whole] * len(pieces) + [anywhere] * 2,
+        out_specs=[anywhere] * 2 + [whole] * 2,
+        out_shape=out + [jax.ShapeDtypeStruct((1, states, part), f32)] * 2,
+        scratch_shapes=[pltpu.SemaphoreType.DMA((heads + len(DELAYED), 2))],
+        input_output_aliases={len(pieces): 0, len(pieces) + 1: 1},
         compiler_params=params,
-    )(*arrived)
+    )(*pieces, *outs)
     return (grad_in, grad_rate, jnp.swapaxes(grad_key, 1, 2), jnp.swapaxes(grad_query, 1, 2))
 
 

time: 39.8 us -> 28.9 us (0.73)
  starting transfers between devices: 20.4 us -> 10.5 us
  waiting for transfers between devices: 4.78 us -> 3.65 us
    ppermute x12 -> x6, starting transfers between devices: 18.9 us -> 9.79 us  [send(): return lax.ppermute(piece, 'head', [(s, s ^ d) for s in range(heads)])]
    ppermute x12 -> x6, waiting for transfers between devices: 4.77 us -> 3.58 us  [send(): return lax.ppermute(piece, 'head', [(s, s ^ d) for s in range(heads)])]
    pallas_call x5 -> x4, Pallas kernels: 4.73 us -> 5.78 us  [the longest x2 3.63 us: first(): pl.pallas_call(functools.partial(first_kernel, sum(widths[:c]), width, ba...]
    pallas_call x4 -> x2, Pallas kernels: 8.99 us -> 8.1 us  [second(): pl.pallas_call(functools.partial(second_kernel, onwards_here, last, heads...]
    ppermute x4 -> x2, starting transfers between devices: 1.52 us -> 0.7 us  [shards(): entry = lax.ppermute(end, 'ctx', [(0, 1), (1, 0)])]
  transfers between devices with their start and end apart: 16 -> 8, of which waited for: 2 -> 3; matrix products, arithmetic and copies ran while one was open for 0% -> 0% of each run, Pallas kernels for 27% -> 20%
where the time goes in v3:
time: 28.9 us; the launch traced here: 28.7 us
  Pallas kernels  13.9 us (48%)
  starting transfers between devices  10.5 us (36%)
  waiting for transfers between devices  3.65 us (13%)
  between operations  0.71 us (2%)
    ppermute x6, starting transfers between devices, send(): return lax.ppermute(piece, 'head', [(s, s ^ d) for s in range(heads)])  9.79 us
    pallas_call x2, Pallas kernels, second(): pl.pallas_call(functools.partial(second_kernel, onwards_here, last, heads...  8.1 us
    pallas_call x2, Pallas kernels, first(): pl.pallas_call(functools.partial(first_kernel, sum(widths[:c]), width, ba...  3.63 us
    ppermute x6, waiting for transfers between devices, send(): return lax.ppermute(piece, 'head', [(s, s ^ d) for s in range(heads)])  3.58 us
    pallas_call x1, Pallas kernels, shards(): pl.pallas_call(functools.partial(late_kernel, heads, DELAYED, channels),...  1.39 us
    pallas_call x1, Pallas kernels, shards(): pl.pallas_call(functools.partial(early_kernel, early, channels), in_specs...  0.75 us
    ppermute x2, starting transfers between devices, shards(): entry = lax.ppermute(end, 'ctx', [(0, 1), (1, 0)])  0.7 us
  transfers between devices with their start and end apart: 8, of which 3 were waited for; matrix products, arithmetic and copies ran while one was open for 0% of the time, Pallas kernels for 20%

profile of v3, /device:TPU:0, one launch (start us, length us, event | category | flops | bytes accessed | tf_op | source)
XLA Modules:
  0.0 28.7 jit_solution(16077270319758859536)
XLA Ops:
  0.6 0.0 copy-start.2
  0.6 0.0 copy-start
  0.7 0.0 copy-start.1
  0.7 0.0 copy-start.4
  0.7 0.0 copy-start.3
  0.7 2.9 %shard_map.84 = (f32[128,16,640]{2,1,0:T(8,128)S(1)}, f32[16,640]{1,0:T(8,128)S(1)}, f32[5,136,128]{2,1,0:T(8,128)S(1)}, f32[5,136,128]{2,1,0:T(8,128)S(1)}, f32...) custom-call(bf16[1,128,1024]{2,1,0:T(8,128)(2,1)} %refs_0_.3, ...), custom_call_target="tpu_custom_call" | custom-call | flops 6553600 | bytes 5242880 | tf_op jit(solution)/shard_map/pallas_call | solution.py:420
  3.5 0.7 %collective-permute-start.1 = (f32[16,640]{1,0:T(8,128)S(1)}, f32[16,640]{1,0:T(8,128)S(1)}, u32[]{:S(2)}, u32[]{:S(2)}) collective-permute-start(f32[16,640]{1,0:T(8,128)S(1)} %get-tuple-element.47), channel_id=1, source_target_pairs={{0,4},{4,0},{1,5},{5,1},{2,6},{6,2},{3,7},{7,3},{8,12},{12,8},{9,1... | collective-permute-start | bytes 122888 | tf_op jit(solution)/shard_map/ppermute | solution.py:474
  4.2 0.0 copy-done.2
  4.2 0.0 copy-done
  4.2 0.0 copy-done.1
  4.2 0.0 copy-done.4
  4.2 0.0 copy-done.3
  4.3 0.8 %shard_map.85 = (f32[128,16,384]{2,1,0:T(8,128)S(1)}, f32[16,384]{1,0:T(8,128)S(1)}, f32[3,136,128]{2,1,0:T(8,128)S(1)}, f32[3,136,128]{2,1,0:T(8,128)S(1)}, f32...) custom-call(bf16[1,128,1024]{2,1,0:T(8,128)(2,1)S(1)} %copy-done.1, ...), custom_call_target="tpu_custom_call" | custom-call | flops 3932160 | bytes 3145728 | tf_op jit(solution)/shard_map/pallas_call | solution.py:420
  5.0 0.1 collective-permute-done.1.refs_0_
  5.1 3.8 %shard_map.86 = (bf16[32,1280]{1,0:T(8,128)(2,1)S(1)}, bf16[32,1280]{1,0:T(8,128)(2,1)S(1)}, bf16[32,1280]{1,0:T(8,128)(2,1)S(1)}, bf16[32,1280]{1,0:T(8,128)(2,...) custom-call(f32[16,640]{1,0:T(8,128)S(1)} %collective-permute-done.1.refs_0_, ...), custom_call_target="tpu_custom_call" | custom-call | flops 26214400 | bytes 5242880 | tf_op jit(solution)/shard_map/pallas_call | solution.py:444
  9.0 3.8 %collective-permute-start.6 = (bf16[32,1280]{1,0:T(8,128)(2,1)S(1)}, bf16[32,1280]{1,0:T(8,128)(2,1)S(1)}, u32[]{:S(2)}, u32[]{:S(2)}) collective-permute-start(bf16[32,1280]{1,0:T(8,128)(2,1)S(1)} %get-tuple-element.64), channel_id=1, source_target_pairs={{0,2},{1,3},{2,0},{3,1},{4,6},{5,7},{6,4},{7,5},{8,10},{9,11},{10,... | collective-permute-start | bytes 245768 | tf_op jit(solution)/shard_map/ppermute | solution.py:467
  12.8 0.0 collective-permute-start
  12.8 1.3 %collective-permute-start.7 = (bf16[32,1280]{1,0:T(8,128)(2,1)S(1)}, bf16[32,1280]{1,0:T(8,128)(2,1)S(1)}, u32[]{:S(2)}, u32[]{:S(2)}) collective-permute-start(bf16[32,1280]{1,0:T(8,128)(2,1)S(1)} %get-tuple-element.65), channel_id=1, source_target_pairs={{0,3},{1,2},{2,1},{3,0},{4,7},{5,6},{6,5},{7,4},{8,11},{9,10},{10,... | collective-permute-start | bytes 245768 | tf_op jit(solution)/shard_map/ppermute | solution.py:467
  14.1 0.2 collective-permute-start.5
  14.4 0.0 collective-permute-done.refs_0_
  14.4 4.2 %shard_map.87 = (bf16[32,896]{1,0:T(8,128)(2,1)S(1)}, bf16[32,896]{1,0:T(8,128)(2,1)S(1)}, bf16[32,896]{1,0:T(8,128)(2,1)S(1)}, bf16[32,896]{1,0:T(8,128)(2,1)S(...) custom-call(f32[16,384]{1,0:T(8,128)S(1)} %collective-permute-done.refs_0_, ...), custom_call_target="tpu_custom_call" | custom-call | flops 15728640 | bytes 3145728 | tf_op jit(solution)/shard_map/pallas_call | solution.py:444
  18.6 2.9 %collective-permute-start.2 = (bf16[32,896]{1,0:T(8,128)(2,1)S(1)}, bf16[32,896]{1,0:T(8,128)(2,1)S(1)}, u32[]{:S(2)}, u32[]{:S(2)}) collective-permute-start(bf16[32,896]{1,0:T(8,128)(2,1)S(1)} %get-tuple-element.58), channel_id=1, source_target_pairs={{0,3},{1,2},{2,1},{3,0},{4,7},{5,6},{6,5},{7,4},{8,11},{9,10},{10,... | collective-permute-start | bytes 172040 | tf_op jit(solution)/shard_map/ppermute | solution.py:467
  21.5 0.3 %collective-permute-start.3 = (bf16[32,896]{1,0:T(8,128)(2,1)S(1)}, bf16[32,896]{1,0:T(8,128)(2,1)S(1)}, u32[]{:S(2)}, u32[]{:S(2)}) collective-permute-start(bf16[32,896]{1,0:T(8,128)(2,1)S(1)} %get-tuple-element.59), channel_id=1, source_target_pairs={{0,2},{1,3},{2,0},{3,1},{4,6},{5,7},{6,4},{7,5},{8,10},{9,11},{10,... | collective-permute-start | bytes 172040 | tf_op jit(solution)/shard_map/ppermute | solution.py:467
  21.9 0.0 collective-permute-done.6.refs_1_
  21.9 1.1 %collective-permute-start.4 = (bf16[32,896]{1,0:T(8,128)(2,1)S(1)}, bf16[32,896]{1,0:T(8,128)(2,1)S(1)}, u32[]{:S(2)}, u32[]{:S(2)}) collective-permute-start(bf16[32,896]{1,0:T(8,128)(2,1)S(1)} %get-tuple-element.60), channel_id=1, source_target_pairs={{0,1},{1,0},{2,3},{3,2},{4,5},{5,4},{6,7},{7,6},{8,9},{9,8},{10,11... | collective-permute-start | bytes 172040 | tf_op jit(solution)/shard_map/ppermute | solution.py:467
  23.0 0.0 collective-permute-done.7.refs_2_
  23.0 0.8 %shard_map.88 = (bf16[1,32,4096]{2,1,0:T(8,128)(2,1)}, bf16[1,32,4096]{2,1,0:T(8,128)(2,1)}) custom-call(bf16[32,1280]{1,0:T(8,128)(2,1)S(1)} %get-tuple-element.63.refs_0_, bf16[32,1280]{1,0:T(8,128)(2,1)S(1)} %collective-permute-done.6.refs_1_, bf16[32,1280]{1,0:T(8,128)(2,1)S(1)} %collective-permute-done.7.refs_2_), custom_call_target="tpu_custom_call" | custom-call | tf_op jit(solution)/shard_map/pallas_call | solution.py:491
  23.8 1.1 %collective-permute-done.2.refs_0_ = bf16[32,896]{1,0:T(8,128)(2,1)S(1)} collective-permute-done((bf16[32,896]{1,0:T(8,128)(2,1)S(1)}, bf16[32,896]{1,0:T(8,128)(2,1)S(1)}, u32[]{:S(2)}, u32[]{:S(2)}) %collective-permute-start.2) | collective-permute-done | bytes 57376 | tf_op jit(solution)/shard_map/ppermute | solution.py:467
  24.9 2.4 %collective-permute-done.3.refs_1_ = bf16[32,896]{1,0:T(8,128)(2,1)S(1)} collective-permute-done((bf16[32,896]{1,0:T(8,128)(2,1)S(1)}, bf16[32,896]{1,0:T(8,128)(2,1)S(1)}, u32[]{:S(2)}, u32[]{:S(2)}) %collective-permute-start.3) | collective-permute-done | bytes 57376 | tf_op jit(solution)/shard_map/ppermute | solution.py:467
  27.3 0.0 collective-permute-done.4.refs_2_
  27.3 0.0 collective-permute-done.5.refs_4_
  27.3 1.4 %shard_map.89 = (bf16[1,32,4096]{2,1,0:T(8,128)(2,1)}, bf16[1,32,4096]{2,1,0:T(8,128)(2,1)}, f32[1,16,32]{2,1,0:T(8,128)}, f32[1,16,32]{2,1,0:T(8,128)}) custom-call(bf16[32,896]{1,0:T(8,128)(2,1)S(1)} %collective-permute-done.2.refs_0_, bf16[32,896]{1,0:T(8,128)(2,1)S(1)} %collective-permute-done.3.refs_1_, ...), custom_call_target="tpu_custom_call", output_to_operand_aliasing={{0}: (5, {}), {1}: (6, {})} | custom-call | tf_op jit(solution)/shard_map/pallas_call | solution.py:500
Async XLA Ops:
  0.6 3.6 %copy-start.2 = (bf16[1,128,1024]{2,1,0:T(8,128)(2,1)S(1)}, bf16[1,128,1024]{2,1,0:T(8,128)(2,1)}, u32[]{:S(2)}) copy-start(bf16[1,128,1024]{2,1,0:T(8,128)(2,1)} %refs_4_.3) | copy-start | bytes 786436
  0.6 3.6 %copy-start = (f32[1,128,1024]{2,1,0:T(8,128)S(1)}, f32[1,128,1024]{2,1,0:T(8,128)}, u32[]{:S(2)}) copy-start(f32[1,128,1024]{2,1,0:T(8,128)} %refs_1_.3) | copy-start | bytes 1572868
  0.7 3.6 %copy-start.1 = (bf16[1,128,1024]{2,1,0:T(8,128)(2,1)S(1)}, bf16[1,128,1024]{2,1,0:T(8,128)(2,1)}, u32[]{:S(2)}) copy-start(bf16[1,128,1024]{2,1,0:T(8,128)(2,1)} %refs_0_.3) | copy-start | bytes 786436
  0.7 3.6 %copy-start.4 = (bf16[1,128,16]{1,2,0:T(8,128)(2,1)S(1)}, bf16[1,128,16]{1,2,0:T(8,128)(2,1)}, u32[]{:S(2)}) copy-start(bf16[1,128,16]{1,2,0:T(8,128)(2,1)} %param.8) | copy-start | bytes 12292
  0.7 3.6 %copy-start.3 = (bf16[1,128,16]{1,2,0:T(8,128)(2,1)S(1)}, bf16[1,128,16]{1,2,0:T(8,128)(2,1)}, u32[]{:S(2)}) copy-start(bf16[1,128,16]{1,2,0:T(8,128)(2,1)} %param.7) | copy-start | bytes 12292
  3.5 1.6 %collective-permute-start.1 = (f32[16,640]{1,0:T(8,128)S(1)}, f32[16,640]{1,0:T(8,128)S(1)}, u32[]{:S(2)}, u32[]{:S(2)}) collective-permute-start(f32[16,640]{1,0:T(8,128)S(1)} %get-tuple-element.47), channel_id=1, source_target_pairs={{0,4},{4,0},{1,5},{5,1},{2,6},{6,2},{3,7},{7,3},{8,12},{12,8},{9,1... | collective-permute-start | bytes 122888 | tf_op jit(solution)/shard_map/ppermute | solution.py:474
  9.0 12.9 %collective-permute-start.6 = (bf16[32,1280]{1,0:T(8,128)(2,1)S(1)}, bf16[32,1280]{1,0:T(8,128)(2,1)S(1)}, u32[]{:S(2)}, u32[]{:S(2)}) collective-permute-start(bf16[32,1280]{1,0:T(8,128)(2,1)S(1)} %get-tuple-element.64), channel_id=1, source_target_pairs={{0,2},{1,3},{2,0},{3,1},{4,6},{5,7},{6,4},{7,5},{8,10},{9,11},{10,... | collective-permute-start | bytes 245768 | tf_op jit(solution)/shard_map/ppermute | solution.py:467
  12.8 1.6 %collective-permute-start = (f32[16,384]{1,0:T(8,128)S(1)}, f32[16,384]{1,0:T(8,128)S(1)}, u32[]{:S(2)}, u32[]{:S(2)}) collective-permute-start(f32[16,384]{1,0:T(8,128)S(1)} %get-tuple-element.40), channel_id=1, source_target_pairs={{0,4},{4,0},{1,5},{5,1},{2,6},{6,2},{3,7},{7,3},{8,12},{12,8},{9,1... | collective-permute-start | bytes 73736 | tf_op jit(solution)/shard_map/ppermute | solution.py:474
  12.8 10.2 %collective-permute-start.7 = (bf16[32,1280]{1,0:T(8,128)(2,1)S(1)}, bf16[32,1280]{1,0:T(8,128)(2,1)S(1)}, u32[]{:S(2)}, u32[]{:S(2)}) collective-permute-start(bf16[32,1280]{1,0:T(8,128)(2,1)S(1)} %get-tuple-element.65), channel_id=1, source_target_pairs={{0,3},{1,2},{2,1},{3,0},{4,7},{5,6},{6,5},{7,4},{8,11},{9,10},{10,... | collective-permute-start | bytes 245768 | tf_op jit(solution)/shard_map/ppermute | solution.py:467
  14.1 13.2 %collective-permute-start.5 = (bf16[32,1280]{1,0:T(8,128)(2,1)S(1)}, bf16[32,1280]{1,0:T(8,128)(2,1)S(1)}, u32[]{:S(2)}, u32[]{:S(2)}) collective-permute-start(bf16[32,1280]{1,0:T(8,128)(2,1)S(1)} %get-tuple-element.62), channel_id=1, source_target_pairs={{0,1},{1,0},{2,3},{3,2},{4,5},{5,4},{6,7},{7,6},{8,9},{9,8},{10,11... | collective-permute-start | bytes 245768 | tf_op jit(solution)/shard_map/ppermute | solution.py:467
  18.6 6.3 %collective-permute-start.2 = (bf16[32,896]{1,0:T(8,128)(2,1)S(1)}, bf16[32,896]{1,0:T(8,128)(2,1)S(1)}, u32[]{:S(2)}, u32[]{:S(2)}) collective-permute-start(bf16[32,896]{1,0:T(8,128)(2,1)S(1)} %get-tuple-element.58), channel_id=1, source_target_pairs={{0,3},{1,2},{2,1},{3,0},{4,7},{5,6},{6,5},{7,4},{8,11},{9,10},{10,... | collective-permute-start | bytes 172040 | tf_op jit(solution)/shard_map/ppermute | solution.py:467
  21.5 5.8 %collective-permute-start.3 = (bf16[32,896]{1,0:T(8,128)(2,1)S(1)}, bf16[32,896]{1,0:T(8,128)(2,1)S(1)}, u32[]{:S(2)}, u32[]{:S(2)}) collective-permute-start(bf16[32,896]{1,0:T(8,128)(2,1)S(1)} %get-tuple-element.59), channel_id=1, source_target_pairs={{0,2},{1,3},{2,0},{3,1},{4,6},{5,7},{6,4},{7,5},{8,10},{9,11},{10,... | collective-permute-start | bytes 172040 | tf_op jit(solution)/shard_map/ppermute | solution.py:467
  21.9 5.5 %collective-permute-start.4 = (bf16[32,896]{1,0:T(8,128)(2,1)S(1)}, bf16[32,896]{1,0:T(8,128)(2,1)S(1)}, u32[]{:S(2)}, u32[]{:S(2)}) collective-permute-start(bf16[32,896]{1,0:T(8,128)(2,1)S(1)} %get-tuple-element.60), channel_id=1, source_target_pairs={{0,1},{1,0},{2,3},{3,2},{4,5},{5,4},{6,7},{7,6},{8,9},{9,8},{10,11... | collective-permute-start | bytes 172040 | tf_op jit(solution)/shard_map/ppermute | solution.py:467

commit v4 on v3

--- a/solution.py
+++ b/solution.py
@@ -12,7 +12,7 @@
 SUB = 8
 UNROLL = 8
 FIRST_TILES = 5
-DELAYED = (1,)
+EARLY = (0, 2, 3)
 VMEM_LIMIT = 20 * 1024 * 1024
 
 
@@ -105,6 +105,18 @@
     keys_ref, queries_ref = given or refs[7:9]
     states, tokens = key_ref.shape[1:]
     tiles = width // LANES
+    fetched = []
+    if not has_tables:
+        sources = (key_ref, query_ref, rate_ref, x_ref, go_ref)
+        kept, semaphores = refs[10:15], refs[15]
+        for i, (source, to) in enumerate(zip(sources, kept)):
+            if i >= 2:
+                source = source.at[:, :, pl.ds(offset, width)]
+            fetched.append(pltpu.make_async_copy(source, to, semaphores.at[i]))
+            fetched[-1].start()
+        key_ref, query_ref, rate_ref, x_ref, go_ref = kept
+        fetched[0].wait()
+        fetched[1].wait()
     key = key_ref[0].astype(jnp.float32)
     if not has_tables:
         refs[9][...] = key
@@ -112,8 +124,10 @@
         spread_columns(query_ref[0].astype(jnp.float32), queries_ref)
     key_norm = jnp.sum(key * key, axis=0, keepdims=True)
     norm = jnp.transpose(jnp.broadcast_to(key_norm, (LANES, tokens)))
+    for copy in fetched[2:]:
+        copy.wait()
     for j in range(tiles):
-        at = pl.ds(offset + j * LANES, LANES)
+        at = pl.ds((offset if has_tables else 0) + j * LANES, LANES)
         rate = rate_ref[0, :, at]
         x = x_ref[0, :, at].astype(jnp.float32)
         inverse = 1.0 / (1.0 + rate * norm)
@@ -186,11 +200,12 @@
     keys_ref, queries_ref = refs[7:9]
     del refs[:9]
     start_ref = refs.pop(0) if has_start else None
-    before = [refs.pop(0) for _ in range(3)] if last else None
+    before = [refs.pop(0) for _ in range(4)] if last else None
     key_ref = refs.pop(0) if last else None
     if not last:
         del refs[0]
     piece_refs = refs[:heads]
+    passed = [refs.pop(heads), refs.pop(heads)] if last else None
     key_part_ref, query_part_ref, norm_ref, dot_ref, weighted_ref = refs[heads : heads + 5]
     tokens, states = keys_ref.shape[:2]
     tiles = step_ref.shape[0]
@@ -199,66 +214,83 @@
     def path_at(t, h, j):
         return path_ref[t, pl.ds(h * SUB, SUB), tile_at(j)]
 
-    def step_through(back, advance):
+    def step_through(back):
+        order = list(reversed(range(UNROLL))) if back else list(range(UNROLL))
+        work = [(u, j) for u in order for j in range(tiles)]
+
         def block(i, state):
             base = tokens - UNROLL - i * UNROLL if back else i * UNROLL
             state = [list(part) for part in state]
-            for u in reversed(range(UNROLL)) if back else range(UNROLL):
+            if back:
+                top = base + UNROLL - 1
+                held = [[path_at(top, h, j) for h in pair] for j in range(tiles)]
+
+            def load(u, j):
+                rows = [row(ref, j, base + u) for ref in (step_ref, drive_ref, go32_ref)]
+                if not back:
+                    return rows, [path_at(base + u, h, j) for h in pair]
+                earlier = [path_at(jnp.maximum(base + u - 1, 0), h, j) for h in pair]
+                if u == 0:
+                    for h in pair:
+                        start = start_ref[pl.ds(h * SUB, SUB), tile_at(j)] if has_start else 0.0
+                        earlier[h] = jnp.where(base == 0, start, earlier[h])
+                return rows, earlier
+
+            ahead = load(*work[0])
+            for at, (u, j) in enumerate(work):
                 t = base + u
-                k, q = halves(keys_ref[t]), halves(queries_ref[t])
-                k2 = [part * part for part in k]
-                sums = None
-                for j in range(tiles):
-                    step, drive, go = (
-                        row(ref, j, t) for ref in (step_ref, drive_ref, go32_ref)
-                    )
-                    dots, weights, terms = [], [], []
-                    for h in pair:
-                        decay = 1.0 - step * k2[h]
-                        grad, here, previous, state[j][h] = advance(
-                            t, u, h, j, state[j][h], decay, drive, go, k[h], q[h]
-                        )
-                        weight = grad * previous
-                        dots.append(grad * k[h])
-                        weights.append(weight * k2[h])
-                        terms += [grad * drive, weight * step, here * go]
-                    dot_ref[j, pl.ds(pl.multiple_of(t * SUB, SUB), SUB), :] = sum(dots[1:], dots[0])
-                    weighted_ref[j, pl.ds(pl.multiple_of(t * SUB, SUB), SUB), :] = sum(
-                        weights[1:], weights[0]
-                    )
-                    sums = terms if j == 0 else [a + b for a, b in zip(sums, terms)]
+                (step, drive, go), loaded = ahead
+                if j == 0:
+                    k, q = halves(keys_ref[t]), halves(queries_ref[t])
+                    k2 = [part * part for part in k]
+                if at + 1 < len(work):
+                    ahead = load(*work[at + 1])
+                dots, weights, terms = [], [], []
+                for h in pair:
+                    decay = 1.0 - step * k2[h]
+                    if back:
+                        grad = go * q[h] + state[j][h]
+                        here, previous = held[j][h], loaded[h]
+                        held[j][h] = previous
+                        state[j][h] = decay * grad
+                    else:
+                        grad, previous = loaded[h], state[j][h]
+                        here = decay * previous + drive * k[h]
+                        state[j][h] = here
+                    weight = grad * previous
+                    dots.append(grad * k[h])
+                    weights.append(weight * k2[h])
+                    terms += [grad * drive, weight * step, here * go]
+                rows = pl.ds(pl.multiple_of(t * SUB, SUB), SUB)
+                dot_ref[j, rows, :] = sum(dots[1:], dots[0])
+                weighted_ref[j, rows, :] = sum(weights[1:], weights[0])
+                sums = terms if j == 0 else [a + b for a, b in zip(sums, terms)]
+                if j < tiles - 1:
+                    continue
                 for h in pair:
                     by_drive, by_decay, by_query = sums[3 * h : 3 * h + 3]
-                    at = pl.ds(pl.multiple_of(t * states + h * SUB, SUB), SUB)
+                    rows = pl.ds(pl.multiple_of(t * states + h * SUB, SUB), SUB)
                     by_key = by_drive - (2.0 * k[h]) * by_decay
                     if last:
-                        by_key = by_key + before[0][at, :]
-                        by_query = by_query + before[1][at, :]
-                    key_part_ref[at, :] = by_key
-                    query_part_ref[at, :] = by_query
+                        by_key = by_key + before[0][rows, :]
+                        by_query = by_query + before[1][rows, :]
+                    key_part_ref[rows, :] = by_key
+                    query_part_ref[rows, :] = by_query
             return state
 
         entry = [halves(entry_ref[:, tile_at(j)]) for j in range(tiles)]
         lax.fori_loop(0, tokens // UNROLL, block, entry)
 
-    def backwards(t, u, h, j, state, decay, drive, go, k, q):
-        grad = go * q + state
-        earlier = path_at(jnp.maximum(t - 1, 0), h, j)
-        if u == 0:
-            start = start_ref[pl.ds(h * SUB, SUB), tile_at(j)] if has_start else 0.0
-            earlier = jnp.where(t == 0, start, earlier)
-        return grad, path_at(t, h, j), earlier, decay * grad
-
-    def onwards(t, u, h, j, state, decay, drive, go, k, q):
-        here = decay * state + drive * k
-        return path_at(t, h, j), here, state, here
-
-    choose(onwards_here, lambda: step_through(False, onwards), lambda: step_through(True, backwards))
+    choose(onwards_here, lambda: step_through(False), lambda: step_through(True))
 
     part = tokens // heads
     rows = 2 * SUB
     position = lax.axis_index("head")
     width = tiles * LANES
+    if last:
+        half = before[3].shape[1] // 2
+        for i, to in enumerate(passed):
+            to[...] = before[3][:, pl.ds(i * half, half)]
     for d in range(heads):
         for r in range(part // rows):
             base = pl.multiple_of((position ^ d) * part + r * rows, rows)
@@ -273,14 +305,9 @@
                 )
                 grad_step = x * dot - weighted
                 grad_rate = grad_step * inverse * inverse
-                to = j * LANES
-                piece_refs[d][pl.ds(r * rows, rows), pl.ds(to, LANES)] = (step * dot).astype(
-                    jnp.bfloat16
-                )
-                to += width
-                piece_refs[d][pl.ds(r * rows, rows), pl.ds(to, LANES)] = grad_rate.astype(
-                    jnp.bfloat16
-                )
+                to = pl.ds(r * rows, rows)
+                piece_refs[d][to, tile_at(j)] = (step * dot).astype(jnp.bfloat16)
+                piece_refs[d][to, tile_at(tiles + j)] = grad_rate.astype(jnp.bfloat16)
                 term = grad_step * step * step
                 norm_sum = term if norm_sum is None else norm_sum + term
             norm_ref[pl.ds(base, rows), :] = norm_sum
@@ -288,20 +315,15 @@
         return
 
     key = key_ref[...]
-    lane = lax.broadcasted_iota(jnp.int32, (tokens, tokens), 1)
-    own_row = lane == lax.broadcasted_iota(jnp.int32, (tokens, tokens), 0)
-    norm_sums = jnp.where(own_row, lane_sums(norm_ref[...]), 0.0)
-    norm_row = jnp.sum(norm_sums, axis=0, keepdims=True)
+    norm_row = jnp.sum(jnp.transpose(norm_ref[...]), axis=0, keepdims=True)
     lane = lax.broadcasted_iota(jnp.int32, (states, tokens), 1)
     totals = []
     for ref in (key_part_ref, query_part_ref):
         total = jnp.zeros((states, tokens), jnp.float32)
-        for b in range(tokens // UNROLL):
-            sums = lane_sums(ref[pl.ds(b * UNROLL * states, UNROLL * states), :])
-            for u in range(UNROLL):
-                total = jnp.where(
-                    lane == b * UNROLL + u, sums[u * states : (u + 1) * states], total
-                )
+        for base in range(0, tokens, tokens // 2):
+            sums = lane_sums(ref[pl.ds(base * states, tokens // 2 * states), :])
+            for t in range(tokens // 2):
+                total = jnp.where(lane == base + t, sums[t * states : (t + 1) * states], total)
         totals.append(total)
     sums_ref = refs[heads + 5]
     sums_ref[:states] = totals[0] - 2.0 * key * norm_row
@@ -323,45 +345,49 @@
         piece_refs[d][rows:, tail] = jnp.zeros((part - rows, LANES), jnp.bfloat16)
 
 
-def place(out_refs, piece, d, offset, width, channels, semaphores):
-    at = pl.multiple_of((lax.axis_index("head") ^ d) * channels + offset, LANES)
+def place(out_ref, piece, at, d, offset, width, channels, semaphore):
+    to = pl.multiple_of((lax.axis_index("head") ^ d) * channels + offset, LANES)
+    copy = pltpu.make_async_copy(
+        piece.at[:, pl.ds(at, width)], out_ref.at[0, :, pl.ds(to, width)], semaphore
+    )
+    copy.start()
+    return copy
+
+
+def early_kernel(channels, distances, *refs):
+    *pieces, own, in_ref, rate_ref, semaphores = refs
+    first = pieces[0].shape[1] // 2
+    width = channels - first
     copies = []
-    for i, out in enumerate(out_refs):
+    for i, out in enumerate((in_ref, rate_ref)):
         copies.append(
-            pltpu.make_async_copy(
-                piece.at[:, pl.ds(i * width, width)],
-                out.at[0, :, pl.ds(at, width)],
-                semaphores.at[i],
+            place(out, own, i * width, 0, first, width, channels, semaphores.at[len(pieces), i])
+        )
+        for p, d in enumerate(distances):
+            copies.append(
+                place(out, pieces[p], i * first, d, 0, first, channels, semaphores.at[p, i])
             )
-        )
-        copies[-1].start()
-    return copies
-
-
-def early_kernel(distances, channels, *refs):
-    pieces, out_refs, semaphores = refs[:-3], refs[-3:-1], refs[-1]
-    width = pieces[0].shape[1] // 2
-    copies = []
-    for piece, d in zip(pieces, distances):
-        copies += place(out_refs, piece, d, 0, width, channels, semaphores.at[d])
     for copy in copies:
         copy.wait()
 
 
-def late_kernel(heads, distances, channels, *refs):
-    pieces = refs[:heads][::-1]
-    others = refs[heads : heads + len(distances)]
-    *out_refs, key_ref, query_ref, semaphores = refs[heads + len(distances) + 2 :]
+def late_kernel(heads, channels, *refs):
+    pieces, passed = refs[:heads][::-1], refs[heads : heads + 2]
+    *out_refs, key_ref, query_ref, key_kept, query_kept, semaphores = refs[heads + 4 :]
     states, part = key_ref.shape[1:]
     width = (pieces[0].shape[1] - LANES) // 2
     copies = []
-    for d in range(heads):
-        copies += place(
-            out_refs, pieces[d], d, channels - width, width, channels, semaphores.at[d]
-        )
-    for i, d in enumerate(distances):
-        copies += place(
-            out_refs, others[i], d, 0, channels - width, channels, semaphores.at[heads + i]
+    for d in range(1, heads):
+        for i, out in enumerate(out_refs):
+            copies.append(
+                place(
+                    out, pieces[d], i * width, d, channels - width, width, channels,
+                    semaphores.at[d, i],
+                )
+            )
+    for i, out in enumerate(out_refs):
+        copies.append(
+            place(out, passed[i], 0, 1, 0, channels - width, channels, semaphores.at[heads, i])
         )
     total = None
     for d in range(heads):
@@ -370,9 +396,12 @@
         both = both[:SUB] + both[SUB:]
         total = both if total is None else total + both
     for i in range(states // SUB):
-        key_ref[0, SUB * i : SUB * i + SUB] = total[:, i * part : (i + 1) * part]
+        key_kept[0, SUB * i : SUB * i + SUB] = total[:, i * part : (i + 1) * part]
         at = states // SUB + i
-        query_ref[0, SUB * i : SUB * i + SUB] = total[:, at * part : (at + 1) * part]
+        query_kept[0, SUB * i : SUB * i + SUB] = total[:, at * part : (at + 1) * part]
+    for i, (kept, out) in enumerate(((key_kept, key_ref), (query_kept, query_ref))):
+        copies.append(pltpu.make_async_copy(kept, out, semaphores.at[0, i]))
+        copies[-1].start()
     for copy in copies:
         copy.wait()
 
@@ -404,11 +433,13 @@
     def first(c, backwards, tables=(), entry=None):
         width = widths[c]
         arrays = [inputs, step_rate, key_cols, query_cols, grad_out]
-        specs = [whole] * 5
+        specs, scratch = [whole] * 5, []
         if c == 0:
-            wide = pl.BlockSpec((1, tokens, width), lambda i: (0, 0, 0))
-            specs = [wide, wide, whole, whole, wide]
+            specs = [anywhere] * 5
             arrays = [pltpu.with_memory_space_constraint(a, pltpu.HBM) for a in arrays]
+            scratch = [pltpu.VMEM((1, states, tokens), bf16)] * 2
+            scratch += [pltpu.VMEM((1, tokens, width), a.dtype) for a in (step_rate, inputs, grad_out)]
+            scratch += [pltpu.SemaphoreType.DMA((5,))]
         extra = [*(() if entry is None else (entry,)), *tables[:2]]
         out_shape = [
             pltpu.VMEM((tokens, states, width), f32),
@@ -421,10 +452,10 @@
             functools.partial(
                 first_kernel, sum(widths[:c]), width, backwards, entry is not None, bool(tables)
             ),
-            grid=(1,),
             in_specs=specs + [whole] * len(extra),
             out_specs=[whole] * len(out_shape),
             out_shape=out_shape,
+            scratch_shapes=scratch,
             compiler_params=params,
             cost_estimate=cost(width, 5),
         )(*arrays, *extra)
@@ -441,16 +472,18 @@
         parts = pltpu.VMEM((width // LANES, (tokens + 1) * SUB, LANES), f32)
         sums = pltpu.VMEM(((tokens + 1) * states, LANES), f32)
         pieces = [jax.ShapeDtypeStruct((part, 2 * width + LANES * last), bf16)] * heads
+        if last:
+            pieces += [jax.ShapeDtypeStruct((part, channels - width), bf16)] * 2
         results = pl.pallas_call(
             functools.partial(second_kernel, onwards_here, last, heads, start is not None),
             in_specs=specs,
-            out_specs=[whole] * (heads + 3),
+            out_specs=[whole] * (len(pieces) + 3),
             out_shape=pieces + [sums, sums, pltpu.VMEM((tokens, LANES), f32)],
             scratch_shapes=[parts, parts] + [pltpu.VMEM((2 * states, tokens), f32)] * last,
             compiler_params=params,
             cost_estimate=cost(width, 20),
         )(entry, *carried, keys, queries, *extra)
-        return results[:heads], results[heads:]
+        return results[:-3], results[-3:]
 
     entries = starts = here = None
     if groups != 2:
@@ -480,32 +513,30 @@
 
     away = list(range(heads - 1, 0, -1))
     pieces, before = call_second(0, ())
-    arrived = {d: send(pieces[d], d) for d in away}
+    arrived = {d: send(pieces[d], d) for d in away if d != 1}
     arrived[0] = pieces[0]
-    early = [d for d in range(heads) if d not in DELAYED]
-    pieces, _ = call_second(1, before)
-    late = {d: send(pieces[d], d) for d in away}
-    late[0] = pieces[0]
+    *pieces, near_in, near_rate = call_second(1, (*before, pieces[1]))[0]
+    late = [*(send(pieces[d], d) for d in away), pieces[0], send(near_in, 1), send(near_rate, 1)]
 
     out = [jax.ShapeDtypeStruct((1, part, heads * channels), bf16)] * 2
     outs = pl.pallas_call(
-        functools.partial(early_kernel, early, channels),
-        in_specs=[whole] * len(early),
+        functools.partial(early_kernel, channels, EARLY),
+        in_specs=[whole] * heads,
         out_specs=[anywhere] * 2,
         out_shape=out,
         scratch_shapes=[pltpu.SemaphoreType.DMA((heads, 2))],
         compiler_params=params,
-    )(*[arrived[d] for d in early])
-    pieces = [late[d] for d in reversed(range(heads))] + [arrived[d] for d in DELAYED]
+    )(*[arrived[d] for d in EARLY], pieces[0])
+    small = (1, states, part)
     grad_in, grad_rate, grad_key, grad_query = pl.pallas_call(
-        functools.partial(late_kernel, heads, DELAYED, channels),
-        in_specs=[whole] * len(pieces) + [anywhere] * 2,
-        out_specs=[anywhere] * 2 + [whole] * 2,
-        out_shape=out + [jax.ShapeDtypeStruct((1, states, part), f32)] * 2,
-        scratch_shapes=[pltpu.SemaphoreType.DMA((heads + len(DELAYED), 2))],
-        input_output_aliases={len(pieces): 0, len(pieces) + 1: 1},
+        functools.partial(late_kernel, heads, channels),
+        in_specs=[whole] * (heads + 2) + [anywhere] * 2,
+        out_specs=[anywhere] * 4,
+        out_shape=out + [jax.ShapeDtypeStruct(small, f32)] * 2,
+        scratch_shapes=[pltpu.VMEM(small, f32)] * 2 + [pltpu.SemaphoreType.DMA((heads + 1, 2))],
+        input_output_aliases={heads + 2: 0, heads + 3: 1},
         compiler_params=params,
-    )(*pieces, *outs)
+    )(*late, *outs)
     return (grad_in, grad_rate, jnp.swapaxes(grad_key, 1, 2), jnp.swapaxes(grad_query, 1, 2))
 
 

time: 28.9 us -> 30.1 us (1.042)
  starting transfers between devices: 10.5 us -> 12.3 us
  Pallas kernels: 13.9 us -> 13.1 us
    ppermute x6 -> x7, starting transfers between devices: 9.79 us -> 11.6 us  [send(): return lax.ppermute(piece, 'head', [(s, s ^ d) for s in range(heads)])]
    ppermute x2, waiting for transfers between devices: 0.06 us -> 1.25 us  [shards(): entry = lax.ppermute(end, 'ctx', [(0, 1), (1, 0)])]
    ppermute x6 -> x7, waiting for transfers between devices: 3.58 us -> 2.52 us  [send(): return lax.ppermute(piece, 'head', [(s, s ^ d) for s in range(heads)])]
    pallas_call x2, Pallas kernels: 2.15 us -> 1.55 us  [the longest x1 0.79 us: shards(): pl.pallas_call(functools.partial(late_kernel, heads, channels), in_specs=...]
  transfers between devices with their start and end apart: 8 -> 9, of which waited for: 3 -> 4; matrix products, arithmetic and copies ran while one was open for 0% -> 0% of each run, Pallas kernels for 20% -> 20%
where the time goes in v4:
time: 30.1 us; the launch traced here: 29.9 us
  Pallas kernels  13.1 us (44%)
  starting transfers between devices  12.3 us (41%)
  waiting for transfers between devices  3.78 us (13%)
  between operations  0.72 us (2%)
    ppermute x7, starting transfers between devices, send(): return lax.ppermute(piece, 'head', [(s, s ^ d) for s in range(heads)])  11.6 us
    pallas_call x2, Pallas kernels, second(): pl.pallas_call(functools.partial(second_kernel, onwards_here, last, heads...  8.22 us
    pallas_call x2, Pallas kernels, first(): pl.pallas_call(functools.partial(first_kernel, sum(widths[:c]), width, ba...  3.34 us
    ppermute x7, waiting for transfers between devices, send(): return lax.ppermute(piece, 'head', [(s, s ^ d) for s in range(heads)])  2.52 us
    ppermute x2, waiting for transfers between devices, shards(): entry = lax.ppermute(end, 'ctx', [(0, 1), (1, 0)])  1.25 us
    pallas_call x1, Pallas kernels, shards(): pl.pallas_call(functools.partial(late_kernel, heads, channels), in_specs=...  0.79 us
    pallas_call x1, Pallas kernels, shards(): pl.pallas_call(functools.partial(early_kernel, channels, EARLY), in_specs...  0.77 us
    ppermute x2, starting transfers between devices, shards(): entry = lax.ppermute(end, 'ctx', [(0, 1), (1, 0)])  0.7 us
  transfers between devices with their start and end apart: 9, of which 4 were waited for; matrix products, arithmetic and copies ran while one was open for 0% of the time, Pallas kernels for 20%

profile of v4, /device:TPU:0, one launch (start us, length us, event | category | flops | bytes accessed | tf_op | source)
XLA Modules:
  0.0 29.9 jit_solution(4640170488326387258)
XLA Ops:
  0.6 0.0 copy-start.2
  0.6 0.0 copy-start
  0.7 0.0 copy-start.1
  0.7 0.0 copy-start.4
  0.7 0.0 copy-start.3
  0.7 2.6 %shard_map.84 = (f32[128,16,640]{2,1,0:T(8,128)S(1)}, f32[16,640]{1,0:T(8,128)S(1)}, f32[5,136,128]{2,1,0:T(8,128)S(1)}, f32[5,136,128]{2,1,0:T(8,128)S(1)}, f32...) custom-call(bf16[1,128,1024]{2,1,0:T(8,128)(2,1)} %refs_0_.3, ...), custom_call_target="tpu_custom_call" | custom-call | flops 6553600 | bytes 5242880 | tf_op jit(solution)/shard_map/pallas_call | solution.py:451
  3.3 0.7 %collective-permute-start.1 = (f32[16,640]{1,0:T(8,128)S(1)}, f32[16,640]{1,0:T(8,128)S(1)}, u32[]{:S(2)}, u32[]{:S(2)}) collective-permute-start(f32[16,640]{1,0:T(8,128)S(1)} %get-tuple-element.49), channel_id=1, source_target_pairs={{0,4},{4,0},{1,5},{5,1},{2,6},{6,2},{3,7},{7,3},{8,12},{12,8},{9,1... | collective-permute-start | bytes 122888 | tf_op jit(solution)/shard_map/ppermute | solution.py:507
  4.0 0.0 copy-done.2
  4.0 0.0 copy-done
  4.0 0.0 copy-done.1
  4.0 0.0 copy-done.4
  4.0 0.0 copy-done.3
  4.0 0.8 %shard_map.85 = (f32[128,16,384]{2,1,0:T(8,128)S(1)}, f32[16,384]{1,0:T(8,128)S(1)}, f32[3,136,128]{2,1,0:T(8,128)S(1)}, f32[3,136,128]{2,1,0:T(8,128)S(1)}, f32...) custom-call(bf16[1,128,1024]{2,1,0:T(8,128)(2,1)S(1)} %copy-done.1, ...), custom_call_target="tpu_custom_call" | custom-call | flops 3932160 | bytes 3145728 | tf_op jit(solution)/shard_map/pallas_call | solution.py:451
  4.8 0.1 collective-permute-done.1.refs_0_
  4.8 3.9 %shard_map.86 = (bf16[32,1280]{1,0:T(8,128)(2,1)S(1)}, bf16[32,1280]{1,0:T(8,128)(2,1)S(1)}, bf16[32,1280]{1,0:T(8,128)(2,1)S(1)}, bf16[32,1280]{1,0:T(8,128)(2,...) custom-call(f32[16,640]{1,0:T(8,128)S(1)} %collective-permute-done.1.refs_0_, ...), custom_call_target="tpu_custom_call" | custom-call | flops 26214400 | bytes 5242880 | tf_op jit(solution)/shard_map/pallas_call | solution.py:477
  8.7 3.8 %collective-permute-start.7 = (bf16[32,1280]{1,0:T(8,128)(2,1)S(1)}, bf16[32,1280]{1,0:T(8,128)(2,1)S(1)}, u32[]{:S(2)}, u32[]{:S(2)}) collective-permute-start(bf16[32,1280]{1,0:T(8,128)(2,1)S(1)} %get-tuple-element.68), channel_id=1, source_target_pairs={{0,2},{1,3},{2,0},{3,1},{4,6},{5,7},{6,4},{7,5},{8,10},{9,11},{10,... | collective-permute-start | bytes 245768 | tf_op jit(solution)/shard_map/ppermute | solution.py:500
  12.5 1.3 %collective-permute-start.8 = (bf16[32,1280]{1,0:T(8,128)(2,1)S(1)}, bf16[32,1280]{1,0:T(8,128)(2,1)S(1)}, u32[]{:S(2)}, u32[]{:S(2)}) collective-permute-start(bf16[32,1280]{1,0:T(8,128)(2,1)S(1)} %get-tuple-element.69), channel_id=1, source_target_pairs={{0,3},{1,2},{2,1},{3,0},{4,7},{5,6},{6,5},{7,4},{8,11},{9,10},{10,... | collective-permute-start | bytes 245768 | tf_op jit(solution)/shard_map/ppermute | solution.py:500
  13.9 0.0 collective-permute-start
  13.9 1.2 %collective-permute-done.refs_0_ = f32[16,384]{1,0:T(8,128)S(1)} collective-permute-done((f32[16,384]{1,0:T(8,128)S(1)}, f32[16,384]{1,0:T(8,128)S(1)}, u32[]{:S(2)}, u32[]{:S(2)}) %collective-permute-start) | collective-permute-done | bytes 24608 | tf_op jit(solution)/shard_map/ppermute | solution.py:507
  15.0 4.4 %shard_map.87 = (bf16[32,896]{1,0:T(8,128)(2,1)S(1)}, bf16[32,896]{1,0:T(8,128)(2,1)S(1)}, bf16[32,896]{1,0:T(8,128)(2,1)S(1)}, bf16[32,896]{1,0:T(8,128)(2,1)S(...) custom-call(f32[16,384]{1,0:T(8,128)S(1)} %collective-permute-done.r, ...), custom_call_target="tpu_custom_call" | custom-call | flops 15728640 | bytes 3145728 | tf_op jit(solution)/shard_map/pallas_call | solution.py:477
  19.4 2.5 %collective-permute-start.2 = (bf16[32,896]{1,0:T(8,128)(2,1)S(1)}, bf16[32,896]{1,0:T(8,128)(2,1)S(1)}, u32[]{:S(2)}, u32[]{:S(2)}) collective-permute-start(bf16[32,896]{1,0:T(8,128)(2,1)S(1)} %get-tuple-element.61), channel_id=1, source_target_pairs={{0,3},{1,2},{2,1},{3,0},{4,7},{5,6},{6,5},{7,4},{8,11},{9,10},{10,... | collective-permute-start | bytes 172040 | tf_op jit(solution)/shard_map/ppermute | solution.py:500
  21.9 0.0 collective-permute-start.3
  21.9 1.9 %collective-permute-start.4 = (bf16[32,896]{1,0:T(8,128)(2,1)S(1)}, bf16[32,896]{1,0:T(8,128)(2,1)S(1)}, u32[]{:S(2)}, u32[]{:S(2)}) collective-permute-start(bf16[32,896]{1,0:T(8,128)(2,1)S(1)} %get-tuple-element.63), channel_id=1, source_target_pairs={{0,1},{1,0},{2,3},{3,2},{4,5},{5,4},{6,7},{7,6},{8,9},{9,8},{10,11... | collective-permute-start | bytes 172040 | tf_op jit(solution)/shard_map/ppermute | solution.py:500
  23.8 0.0 collective-permute-done.7.refs_1_
  23.8 0.1 collective-permute-start.5
  23.9 0.0 collective-permute-done.8.refs_2_
  23.9 1.9 %collective-permute-start.6 = (bf16[32,640]{1,0:T(8,128)(2,1)S(1)}, bf16[32,640]{1,0:T(8,128)(2,1)S(1)}, u32[]{:S(2)}, u32[]{:S(2)}) collective-permute-start(bf16[32,640]{1,0:T(8,128)(2,1)S(1)} %get-tuple-element.66), channel_id=1, source_target_pairs={{0,1},{1,0},{2,3},{3,2},{4,5},{5,4},{6,7},{7,6},{8,9},{9,8},{10,11... | collective-permute-start | bytes 122888 | tf_op jit(solution)/shard_map/ppermute | solution.py:500
  25.8 0.8 %shard_map.88 = (bf16[1,32,4096]{2,1,0:T(8,128)(2,1)}, bf16[1,32,4096]{2,1,0:T(8,128)(2,1)}) custom-call(bf16[32,1280]{1,0:T(8,128)(2,1)S(1)} %get-tuple-element.67.refs_0_, bf16[32,1280]{1,0:T(8,128)(2,1)S(1)} %collective-permute-done.7.refs_1_, bf16[32,1280]{1,0:T(8,128)(2,1)S(1)} %collective-permute-done.8.refs_2_, ...), custom_call_target="tpu_custom_call" | custom-call | tf_op jit(solution)/shard_map/pallas_call | solution.py:522
  26.6 2.1 %collective-permute-done.5.refs_4_ = bf16[32,640]{1,0:T(8,128)(2,1)S(1)} collective-permute-done((bf16[32,640]{1,0:T(8,128)(2,1)S(1)}, bf16[32,640]{1,0:T(8,128)(2,1)S(1)}, u32[]{:S(2)}, u32[]{:S(2)}) %collective-permute-start.5) | collective-permute-done | bytes 40992 | tf_op jit(solution)/shard_map/ppermute | solution.py:500
  28.7 0.4 %collective-permute-done.6.refs_5_ = bf16[32,640]{1,0:T(8,128)(2,1)S(1)} collective-permute-done((bf16[32,640]{1,0:T(8,128)(2,1)S(1)}, bf16[32,640]{1,0:T(8,128)(2,1)S(1)}, u32[]{:S(2)}, u32[]{:S(2)}) %collective-permute-start.6) | collective-permute-done | bytes 40992 | tf_op jit(solution)/shard_map/ppermute | solution.py:500
  29.1 0.0 collective-permute-done.2.refs_0_
  29.1 0.0 collective-permute-done.3.refs_1_
  29.1 0.0 collective-permute-done.4.refs_2_
  29.1 0.8 %shard_map.89 = (bf16[1,32,4096]{2,1,0:T(8,128)(2,1)}, bf16[1,32,4096]{2,1,0:T(8,128)(2,1)}, f32[1,16,32]{2,1,0:T(8,128)}, f32[1,16,32]{2,1,0:T(8,128)}) custom-call(bf16[32,896]{1,0:T(8,128)(2,1)S(1)} %collective-permute-done.2.refs_0_, bf16[32,896]{1,0:T(8,128)(2,1)S(1)} %collective-permute-done.3.refs_1_, ...), custom_call_target="tpu_custom_call", output_to_operand_aliasing={{0}: (6, {}), {1}: (7, {})} | custom-call | tf_op jit(solution)/shard_map/pallas_call | solution.py:531
Async XLA Ops:
  0.6 3.3 %copy-start.2 = (bf16[1,128,1024]{2,1,0:T(8,128)(2,1)S(1)}, bf16[1,128,1024]{2,1,0:T(8,128)(2,1)}, u32[]{:S(2)}) copy-start(bf16[1,128,1024]{2,1,0:T(8,128)(2,1)} %refs_4_.3) | copy-start | bytes 786436
  0.6 3.3 %copy-start = (f32[1,128,1024]{2,1,0:T(8,128)S(1)}, f32[1,128,1024]{2,1,0:T(8,128)}, u32[]{:S(2)}) copy-start(f32[1,128,1024]{2,1,0:T(8,128)} %refs_1_.3) | copy-start | bytes 1572868
  0.7 3.3 %copy-start.1 = (bf16[1,128,1024]{2,1,0:T(8,128)(2,1)S(1)}, bf16[1,128,1024]{2,1,0:T(8,128)(2,1)}, u32[]{:S(2)}) copy-start(bf16[1,128,1024]{2,1,0:T(8,128)(2,1)} %refs_0_.3) | copy-start | bytes 786436
  0.7 3.3 %copy-start.4 = (bf16[1,128,16]{1,2,0:T(8,128)(2,1)S(1)}, bf16[1,128,16]{1,2,0:T(8,128)(2,1)}, u32[]{:S(2)}) copy-start(bf16[1,128,16]{1,2,0:T(8,128)(2,1)} %param.8) | copy-start | bytes 12292
  0.7 3.3 %copy-start.3 = (bf16[1,128,16]{1,2,0:T(8,128)(2,1)S(1)}, bf16[1,128,16]{1,2,0:T(8,128)(2,1)}, u32[]{:S(2)}) copy-start(bf16[1,128,16]{1,2,0:T(8,128)(2,1)} %param.7) | copy-start | bytes 12292
  3.3 1.6 %collective-permute-start.1 = (f32[16,640]{1,0:T(8,128)S(1)}, f32[16,640]{1,0:T(8,128)S(1)}, u32[]{:S(2)}, u32[]{:S(2)}) collective-permute-start(f32[16,640]{1,0:T(8,128)S(1)} %get-tuple-element.49), channel_id=1, source_target_pairs={{0,4},{4,0},{1,5},{5,1},{2,6},{6,2},{3,7},{7,3},{8,12},{12,8},{9,1... | collective-permute-start | bytes 122888 | tf_op jit(solution)/shard_map/ppermute | solution.py:507
  8.7 15.1 %collective-permute-start.7 = (bf16[32,1280]{1,0:T(8,128)(2,1)S(1)}, bf16[32,1280]{1,0:T(8,128)(2,1)S(1)}, u32[]{:S(2)}, u32[]{:S(2)}) collective-permute-start(bf16[32,1280]{1,0:T(8,128)(2,1)S(1)} %get-tuple-element.68), channel_id=1, source_target_pairs={{0,2},{1,3},{2,0},{3,1},{4,6},{5,7},{6,4},{7,5},{8,10},{9,11},{10,... | collective-permute-start | bytes 245768 | tf_op jit(solution)/shard_map/ppermute | solution.py:500
  12.5 11.4 %collective-permute-start.8 = (bf16[32,1280]{1,0:T(8,128)(2,1)S(1)}, bf16[32,1280]{1,0:T(8,128)(2,1)S(1)}, u32[]{:S(2)}, u32[]{:S(2)}) collective-permute-start(bf16[32,1280]{1,0:T(8,128)(2,1)S(1)} %get-tuple-element.69), channel_id=1, source_target_pairs={{0,3},{1,2},{2,1},{3,0},{4,7},{5,6},{6,5},{7,4},{8,11},{9,10},{10,... | collective-permute-start | bytes 245768 | tf_op jit(solution)/shard_map/ppermute | solution.py:500
  13.9 1.2 %collective-permute-start = (f32[16,384]{1,0:T(8,128)S(1)}, f32[16,384]{1,0:T(8,128)S(1)}, u32[]{:S(2)}, u32[]{:S(2)}) collective-permute-start(f32[16,384]{1,0:T(8,128)S(1)} %get-tuple-element.42), channel_id=1, source_target_pairs={{0,4},{4,0},{1,5},{5,1},{2,6},{6,2},{3,7},{7,3},{8,12},{12,8},{9,1... | collective-permute-start | bytes 73736 | tf_op jit(solution)/shard_map/ppermute | solution.py:507
  19.4 9.7 %collective-permute-start.2 = (bf16[32,896]{1,0:T(8,128)(2,1)S(1)}, bf16[32,896]{1,0:T(8,128)(2,1)S(1)}, u32[]{:S(2)}, u32[]{:S(2)}) collective-permute-start(bf16[32,896]{1,0:T(8,128)(2,1)S(1)} %get-tuple-element.61), channel_id=1, source_target_pairs={{0,3},{1,2},{2,1},{3,0},{4,7},{5,6},{6,5},{7,4},{8,11},{9,10},{10,... | collective-permute-start | bytes 172040 | tf_op jit(solution)/shard_map/ppermute | solution.py:500
  21.9 7.2 %collective-permute-start.3 = (bf16[32,896]{1,0:T(8,128)(2,1)S(1)}, bf16[32,896]{1,0:T(8,128)(2,1)S(1)}, u32[]{:S(2)}, u32[]{:S(2)}) collective-permute-start(bf16[32,896]{1,0:T(8,128)(2,1)S(1)} %get-tuple-element.62), channel_id=1, source_target_pairs={{0,2},{1,3},{2,0},{3,1},{4,6},{5,7},{6,4},{7,5},{8,10},{9,11},{10,... | collective-permute-start | bytes 172040 | tf_op jit(solution)/shard_map/ppermute | solution.py:500
  21.9 7.2 %collective-permute-start.4 = (bf16[32,896]{1,0:T(8,128)(2,1)S(1)}, bf16[32,896]{1,0:T(8,128)(2,1)S(1)}, u32[]{:S(2)}, u32[]{:S(2)}) collective-permute-start(bf16[32,896]{1,0:T(8,128)(2,1)S(1)} %get-tuple-element.63), channel_id=1, source_target_pairs={{0,1},{1,0},{2,3},{3,2},{4,5},{5,4},{6,7},{7,6},{8,9},{9,8},{10,11... | collective-permute-start | bytes 172040 | tf_op jit(solution)/shard_map/ppermute | solution.py:500
  23.8 4.9 %collective-permute-start.5 = (bf16[32,640]{1,0:T(8,128)(2,1)S(1)}, bf16[32,640]{1,0:T(8,128)(2,1)S(1)}, u32[]{:S(2)}, u32[]{:S(2)}) collective-permute-start(bf16[32,640]{1,0:T(8,128)(2,1)S(1)} %get-tuple-element.65), channel_id=1, source_target_pairs={{0,1},{1,0},{2,3},{3,2},{4,5},{5,4},{6,7},{7,6},{8,9},{9,8},{10,11... | collective-permute-start | bytes 122888 | tf_op jit(solution)/shard_map/ppermute | solution.py:500
  23.9 5.2 %collective-permute-start.6 = (bf16[32,640]{1,0:T(8,128)(2,1)S(1)}, bf16[32,640]{1,0:T(8,128)(2,1)S(1)}, u32[]{:S(2)}, u32[]{:S(2)}) collective-permute-start(bf16[32,640]{1,0:T(8,128)(2,1)S(1)} %get-tuple-element.66), channel_id=1, source_target_pairs={{0,1},{1,0},{2,3},{3,2},{4,5},{5,4},{6,7},{7,6},{8,9},{9,8},{10,11... | collective-permute-start | bytes 122888 | tf_op jit(solution)/shard_map/ppermute | solution.py:500

commit v5 on v4

--- a/solution.py
+++ b/solution.py
@@ -12,7 +12,7 @@
 SUB = 8
 UNROLL = 8
 FIRST_TILES = 5
-EARLY = (0, 2, 3)
+EARLY = (0, 2, 3, 1)
 VMEM_LIMIT = 20 * 1024 * 1024
 
 
@@ -83,6 +83,10 @@
     return ref[tile, pl.ds(t, SUB, stride=0), :]
 
 
+def norm_row(ref, t):
+    return ref[pl.ds(t, SUB, stride=0), :]
+
+
 def tile_at(j):
     return pl.ds(j * LANES, LANES)
 
@@ -108,7 +112,7 @@
     fetched = []
     if not has_tables:
         sources = (key_ref, query_ref, rate_ref, x_ref, go_ref)
-        kept, semaphores = refs[10:15], refs[15]
+        kept, semaphores = refs[9:14], refs[14]
         for i, (source, to) in enumerate(zip(sources, kept)):
             if i >= 2:
                 source = source.at[:, :, pl.ds(offset, width)]
@@ -119,7 +123,6 @@
         fetched[1].wait()
     key = key_ref[0].astype(jnp.float32)
     if not has_tables:
-        refs[9][...] = key
         spread_columns(key, keys_ref)
         spread_columns(query_ref[0].astype(jnp.float32), queries_ref)
     key_norm = jnp.sum(key * key, axis=0, keepdims=True)
@@ -200,12 +203,10 @@
     keys_ref, queries_ref = refs[7:9]
     del refs[:9]
     start_ref = refs.pop(0) if has_start else None
-    before = [refs.pop(0) for _ in range(4)] if last else None
-    key_ref = refs.pop(0) if last else None
+    before = [refs.pop(0) for _ in range(3)] if last else None
     if not last:
         del refs[0]
     piece_refs = refs[:heads]
-    passed = [refs.pop(heads), refs.pop(heads)] if last else None
     key_part_ref, query_part_ref, norm_ref, dot_ref, weighted_ref = refs[heads : heads + 5]
     tokens, states = keys_ref.shape[:2]
     tiles = step_ref.shape[0]
@@ -287,10 +288,6 @@
     rows = 2 * SUB
     position = lax.axis_index("head")
     width = tiles * LANES
-    if last:
-        half = before[3].shape[1] // 2
-        for i, to in enumerate(passed):
-            to[...] = before[3][:, pl.ds(i * half, half)]
     for d in range(heads):
         for r in range(part // rows):
             base = pl.multiple_of((position ^ d) * part + r * rows, rows)
@@ -305,39 +302,42 @@
                 )
                 grad_step = x * dot - weighted
                 grad_rate = grad_step * inverse * inverse
-                to = pl.ds(r * rows, rows)
-                piece_refs[d][to, tile_at(j)] = (step * dot).astype(jnp.bfloat16)
-                piece_refs[d][to, tile_at(tiles + j)] = grad_rate.astype(jnp.bfloat16)
+                to = j * LANES
+                piece_refs[d][pl.ds(r * rows, rows), pl.ds(to, LANES)] = (step * dot).astype(
+                    jnp.bfloat16
+                )
+                to += width
+                piece_refs[d][pl.ds(r * rows, rows), pl.ds(to, LANES)] = grad_rate.astype(
+                    jnp.bfloat16
+                )
                 term = grad_step * step * step
                 norm_sum = term if norm_sum is None else norm_sum + term
             norm_ref[pl.ds(base, rows), :] = norm_sum
     if not last:
         return
 
-    key = key_ref[...]
-    norm_row = jnp.sum(jnp.transpose(norm_ref[...]), axis=0, keepdims=True)
-    lane = lax.broadcasted_iota(jnp.int32, (states, tokens), 1)
-    totals = []
-    for ref in (key_part_ref, query_part_ref):
-        total = jnp.zeros((states, tokens), jnp.float32)
-        for base in range(0, tokens, tokens // 2):
-            sums = lane_sums(ref[pl.ds(base * states, tokens // 2 * states), :])
-            for t in range(tokens // 2):
-                total = jnp.where(lane == base + t, sums[t * states : (t + 1) * states], total)
-        totals.append(total)
-    sums_ref = refs[heads + 5]
-    sums_ref[:states] = totals[0] - 2.0 * key * norm_row
-    sums_ref[states:] = totals[1]
-    quarters = 2 * states // SUB
-    lane = lax.broadcasted_iota(jnp.int32, (SUB, tokens), 1) // part
+    tails_ref = refs[heads + 5]
+    lane = lax.broadcasted_iota(jnp.int32, (SUB, LANES), 1)
+    for h in range(heads):
+        packed = jnp.zeros((SUB, LANES), jnp.float32)
+        for i, ref in enumerate((key_part_ref, query_part_ref)):
+            here = range(h * part, (h + 1) * part)
+            values = ref[pl.ds(h * part * states, part * states), :]
+            if i == 0:
+                norms = [
+                    2.0 * keys_ref[t] * jnp.concatenate([norm_row(norm_ref, t)] * len(pair), axis=0)
+                    for t in here
+                ]
+                values = values - jnp.concatenate(norms, axis=0)
+            sums = lane_sums(values)
+            for t in range(part):
+                for half in pair:
+                    at = t * states + half * SUB
+                    to = (i * len(pair) + half) * part + t
+                    packed = jnp.where(lane == to, sums[at : at + SUB], packed)
+        tails_ref[h] = packed
     for d in range(heads):
-        shift = (heads - (position ^ d)) * part
-        packed = None
-        for i in range(quarters):
-            turned = pltpu.roll(
-                sums_ref[SUB * i : SUB * i + SUB], lax.rem(shift + i * part, tokens), 1
-            )
-            packed = turned if packed is None else jnp.where(lane == i, turned, packed)
+        packed = tails_ref[position ^ d]
         high = packed.astype(jnp.bfloat16).astype(jnp.float32)
         both = jnp.concatenate([high, packed - high], axis=0).astype(jnp.bfloat16)
         tail = pl.ds(2 * width, LANES)
@@ -345,49 +345,42 @@
         piece_refs[d][rows:, tail] = jnp.zeros((part - rows, LANES), jnp.bfloat16)
 
 
-def place(out_ref, piece, at, d, offset, width, channels, semaphore):
-    to = pl.multiple_of((lax.axis_index("head") ^ d) * channels + offset, LANES)
-    copy = pltpu.make_async_copy(
-        piece.at[:, pl.ds(at, width)], out_ref.at[0, :, pl.ds(to, width)], semaphore
-    )
-    copy.start()
-    return copy
+def place(out_refs, piece, d, offset, width, channels, semaphores):
+    at = pl.multiple_of((lax.axis_index("head") ^ d) * channels + offset, LANES)
+    copies = []
+    for i, out in enumerate(out_refs):
+        copies.append(
+            pltpu.make_async_copy(
+                piece.at[:, pl.ds(i * width, width)],
+                out.at[0, :, pl.ds(at, width)],
+                semaphores.at[i],
+            )
+        )
+        copies[-1].start()
+    return copies
 
 
 def early_kernel(channels, distances, *refs):
     *pieces, own, in_ref, rate_ref, semaphores = refs
+    out_refs = (in_ref, rate_ref)
     first = pieces[0].shape[1] // 2
     width = channels - first
-    copies = []
-    for i, out in enumerate((in_ref, rate_ref)):
-        copies.append(
-            place(out, own, i * width, 0, first, width, channels, semaphores.at[len(pieces), i])
-        )
-        for p, d in enumerate(distances):
-            copies.append(
-                place(out, pieces[p], i * first, d, 0, first, channels, semaphores.at[p, i])
-            )
+    copies = place(out_refs, own, 0, first, width, channels, semaphores.at[len(pieces)])
+    for i, d in enumerate(distances):
+        copies += place(out_refs, pieces[i], d, 0, first, channels, semaphores.at[i])
     for copy in copies:
         copy.wait()
 
 
 def late_kernel(heads, channels, *refs):
-    pieces, passed = refs[:heads][::-1], refs[heads : heads + 2]
-    *out_refs, key_ref, query_ref, key_kept, query_kept, semaphores = refs[heads + 4 :]
+    pieces = refs[:heads][::-1]
+    *out_refs, key_ref, query_ref, key_kept, query_kept, semaphores = refs[heads + 2 :]
     states, part = key_ref.shape[1:]
     width = (pieces[0].shape[1] - LANES) // 2
     copies = []
     for d in range(1, heads):
-        for i, out in enumerate(out_refs):
-            copies.append(
-                place(
-                    out, pieces[d], i * width, d, channels - width, width, channels,
-                    semaphores.at[d, i],
-                )
-            )
-    for i, out in enumerate(out_refs):
-        copies.append(
-            place(out, passed[i], 0, 1, 0, channels - width, channels, semaphores.at[heads, i])
+        copies += place(
+            out_refs, pieces[d], d, channels - width, width, channels, semaphores.at[d]
         )
     total = None
     for d in range(heads):
@@ -447,7 +440,7 @@
         ]
         out_shape += [pltpu.VMEM((width // LANES, tokens + SUB, LANES), f32)] * 5
         if not tables:
-            out_shape += [table] * 2 + [pltpu.VMEM((states, tokens), f32)]
+            out_shape += [table] * 2
         path, end, *carried = pl.pallas_call(
             functools.partial(
                 first_kernel, sum(widths[:c]), width, backwards, entry is not None, bool(tables)
@@ -464,26 +457,24 @@
     def second(c, onwards_here, entry, carried, tables, start, before):
         width = widths[c]
         last = c == 1
-        keys, queries, key = tables
-        extra = [*(() if start is None else (start,)), *before, *((key,) if last else ())]
+        keys, queries = tables
+        extra = [*(() if start is None else (start,)), *before]
         specs = [whole] * (9 + len(extra))
         if not last:
             extra, specs = extra + [work[1][1][0]], specs + [anywhere]
         parts = pltpu.VMEM((width // LANES, (tokens + 1) * SUB, LANES), f32)
         sums = pltpu.VMEM(((tokens + 1) * states, LANES), f32)
         pieces = [jax.ShapeDtypeStruct((part, 2 * width + LANES * last), bf16)] * heads
-        if last:
-            pieces += [jax.ShapeDtypeStruct((part, channels - width), bf16)] * 2
         results = pl.pallas_call(
             functools.partial(second_kernel, onwards_here, last, heads, start is not None),
             in_specs=specs,
-            out_specs=[whole] * (len(pieces) + 3),
-            out_shape=pieces + [sums, sums, pltpu.VMEM((tokens, LANES), f32)],
-            scratch_shapes=[parts, parts] + [pltpu.VMEM((2 * states, tokens), f32)] * last,
+            out_specs=[whole] * (heads + 3),
+            out_shape=pieces + [sums, sums, pltpu.VMEM((tokens + SUB, LANES), f32)],
+            scratch_shapes=[parts, parts] + [pltpu.VMEM((heads, SUB, LANES), f32)] * last,
             compiler_params=params,
             cost_estimate=cost(width, 20),
         )(entry, *carried, keys, queries, *extra)
-        return results[:-3], results[-3:]
+        return results[:heads], results[heads:]
 
     entries = starts = here = None
     if groups != 2:
@@ -513,28 +504,28 @@
 
     away = list(range(heads - 1, 0, -1))
     pieces, before = call_second(0, ())
-    arrived = {d: send(pieces[d], d) for d in away if d != 1}
+    arrived = {d: send(pieces[d], d) for d in away}
     arrived[0] = pieces[0]
-    *pieces, near_in, near_rate = call_second(1, (*before, pieces[1]))[0]
-    late = [*(send(pieces[d], d) for d in away), pieces[0], send(near_in, 1), send(near_rate, 1)]
+    pieces, _ = call_second(1, before)
+    late = [*(send(pieces[d], d) for d in away), pieces[0]]
 
     out = [jax.ShapeDtypeStruct((1, part, heads * channels), bf16)] * 2
     outs = pl.pallas_call(
         functools.partial(early_kernel, channels, EARLY),
-        in_specs=[whole] * heads,
+        in_specs=[whole] * (heads + 1),
         out_specs=[anywhere] * 2,
         out_shape=out,
-        scratch_shapes=[pltpu.SemaphoreType.DMA((heads, 2))],
+        scratch_shapes=[pltpu.SemaphoreType.DMA((heads + 1, 2))],
         compiler_params=params,
     )(*[arrived[d] for d in EARLY], pieces[0])
     small = (1, states, part)
     grad_in, grad_rate, grad_key, grad_query = pl.pallas_call(
         functools.partial(late_kernel, heads, channels),
-        in_specs=[whole] * (heads + 2) + [anywhere] * 2,
+        in_specs=[whole] * heads + [anywhere] * 2,
         out_specs=[anywhere] * 4,
         out_shape=out + [jax.ShapeDtypeStruct(small, f32)] * 2,
-        scratch_shapes=[pltpu.VMEM(small, f32)] * 2 + [pltpu.SemaphoreType.DMA((heads + 1, 2))],
-        input_output_aliases={heads + 2: 0, heads + 3: 1},
+        scratch_shapes=[pltpu.VMEM(small, f32)] * 2 + [pltpu.SemaphoreType.DMA((heads, 2))],
+        input_output_aliases={heads: 0, heads + 1: 1},
         compiler_params=params,
     )(*late, *outs)
     return (grad_in, grad_rate, jnp.swapaxes(grad_key, 1, 2), jnp.swapaxes(grad_query, 1, 2))

time: 30.1 us -> 27.7 us (0.920)
  starting transfers between devices: 12.3 us -> 10.5 us
    ppermute x7 -> x6, starting transfers between devices: 11.6 us -> 9.78 us  [send(): return lax.ppermute(piece, 'head', [(s, s ^ d) for s in range(heads)])]
    ppermute x2, waiting for transfers between devices: 1.25 us -> 0.06 us  [shards(): entry = lax.ppermute(end, 'ctx', [(0, 1), (1, 0)])]
    ppermute x7 -> x6, waiting for transfers between devices: 2.52 us -> 3.52 us  [send(): return lax.ppermute(piece, 'head', [(s, s ^ d) for s in range(heads)])]
    pallas_call x2, Pallas kernels: 8.22 us -> 7.88 us  [second(): pl.pallas_call(functools.partial(second_kernel, onwards_here, last, heads...]
  transfers between devices with their start and end apart: 9 -> 8, of which waited for: 4 -> 3; matrix products, arithmetic and copies ran while one was open for 0% -> 0% of each run, Pallas kernels for 20% -> 20%
where the time goes in v5:
time: 27.7 us; the launch traced here: 27.6 us
  Pallas kernels  12.8 us (46%)
  starting transfers between devices  10.5 us (38%)
  waiting for transfers between devices  3.58 us (13%)
  between operations  0.72 us (3%)
    ppermute x6, starting transfers between devices, send(): return lax.ppermute(piece, 'head', [(s, s ^ d) for s in range(heads)])  9.78 us
    pallas_call x2, Pallas kernels, second(): pl.pallas_call(functools.partial(second_kernel, onwards_here, last, heads...  7.88 us
    ppermute x6, waiting for transfers between devices, send(): return lax.ppermute(piece, 'head', [(s, s ^ d) for s in range(heads)])  3.52 us
    pallas_call x2, Pallas kernels, first(): pl.pallas_call(functools.partial(first_kernel, sum(widths[:c]), width, ba...  3.34 us
    pallas_call x1, Pallas kernels, shards(): pl.pallas_call(functools.partial(early_kernel, channels, EARLY), in_specs...  0.81 us
    pallas_call x1, Pallas kernels, shards(): pl.pallas_call(functools.partial(late_kernel, heads, channels), in_specs=...  0.75 us
    ppermute x2, starting transfers between devices, shards(): entry = lax.ppermute(end, 'ctx', [(0, 1), (1, 0)])  0.7 us
  transfers between devices with their start and end apart: 8, of which 3 were waited for; matrix products, arithmetic and copies ran while one was open for 0% of the time, Pallas kernels for 20%

profile of v5, /device:TPU:0, one launch (start us, length us, event | category | flops | bytes accessed | tf_op | source)
XLA Modules:
  0.0 27.6 jit_solution(9857449311482955572)
XLA Ops:
  0.6 0.0 copy-start.1
  0.6 0.0 copy-start
  0.7 0.0 copy-start.3
  0.7 0.0 copy-start.4
  0.7 0.0 copy-start.2
  0.7 2.6 %shard_map.84 = (f32[128,16,640]{2,1,0:T(8,128)S(1)}, f32[16,640]{1,0:T(8,128)S(1)}, f32[5,136,128]{2,1,0:T(8,128)S(1)}, f32[5,136,128]{2,1,0:T(8,128)S(1)}, f32...) custom-call(bf16[1,128,1024]{2,1,0:T(8,128)(2,1)} %refs_0_.3, ...), custom_call_target="tpu_custom_call" | custom-call | flops 6553600 | bytes 5242880 | tf_op jit(solution)/shard_map/pallas_call | solution.py:444
  3.3 0.7 %collective-permute-start.1 = (f32[16,640]{1,0:T(8,128)S(1)}, f32[16,640]{1,0:T(8,128)S(1)}, u32[]{:S(2)}, u32[]{:S(2)}) collective-permute-start(f32[16,640]{1,0:T(8,128)S(1)} %get-tuple-element.46), channel_id=1, source_target_pairs={{0,4},{4,0},{1,5},{5,1},{2,6},{6,2},{3,7},{7,3},{8,12},{12,8},{9,1... | collective-permute-start | bytes 122888 | tf_op jit(solution)/shard_map/ppermute | solution.py:498
  4.0 0.0 copy-done.1
  4.0 0.0 copy-done
  4.0 0.0 copy-done.3
  4.0 0.0 copy-done.4
  4.0 0.0 copy-done.2
  4.0 0.8 %shard_map.85 = (f32[128,16,384]{2,1,0:T(8,128)S(1)}, f32[16,384]{1,0:T(8,128)S(1)}, f32[3,136,128]{2,1,0:T(8,128)S(1)}, f32[3,136,128]{2,1,0:T(8,128)S(1)}, f32...) custom-call(bf16[1,128,1024]{2,1,0:T(8,128)(2,1)S(1)} %copy-done.1, ...), custom_call_target="tpu_custom_call" | custom-call | flops 3932160 | bytes 3145728 | tf_op jit(solution)/shard_map/pallas_call | solution.py:444
  4.8 0.1 collective-permute-done.1.refs_0_
  4.8 3.9 %shard_map.86 = (bf16[32,1280]{1,0:T(8,128)(2,1)S(1)}, bf16[32,1280]{1,0:T(8,128)(2,1)S(1)}, bf16[32,1280]{1,0:T(8,128)(2,1)S(1)}, bf16[32,1280]{1,0:T(8,128)(2,...) custom-call(f32[16,640]{1,0:T(8,128)S(1)} %collective-permute-done.1.refs_0_, ...), custom_call_target="tpu_custom_call" | custom-call | flops 26214400 | bytes 5242880 | tf_op jit(solution)/shard_map/pallas_call | solution.py:468
  8.7 3.8 %collective-permute-start.5 = (bf16[32,1280]{1,0:T(8,128)(2,1)S(1)}, bf16[32,1280]{1,0:T(8,128)(2,1)S(1)}, u32[]{:S(2)}, u32[]{:S(2)}) collective-permute-start(bf16[32,1280]{1,0:T(8,128)(2,1)S(1)} %get-tuple-element.61), channel_id=1, source_target_pairs={{0,2},{1,3},{2,0},{3,1},{4,6},{5,7},{6,4},{7,5},{8,10},{9,11},{10,... | collective-permute-start | bytes 245768 | tf_op jit(solution)/shard_map/ppermute | solution.py:491
  12.5 0.0 collective-permute-start
  12.5 1.3 %collective-permute-start.6 = (bf16[32,1280]{1,0:T(8,128)(2,1)S(1)}, bf16[32,1280]{1,0:T(8,128)(2,1)S(1)}, u32[]{:S(2)}, u32[]{:S(2)}) collective-permute-start(bf16[32,1280]{1,0:T(8,128)(2,1)S(1)} %get-tuple-element.62), channel_id=1, source_target_pairs={{0,3},{1,2},{2,1},{3,0},{4,7},{5,6},{6,5},{7,4},{8,11},{9,10},{10,... | collective-permute-start | bytes 245768 | tf_op jit(solution)/shard_map/ppermute | solution.py:491
  13.9 0.2 collective-permute-start.7
  14.1 0.0 collective-permute-done.refs_0_
  14.1 4.0 %shard_map.87 = (bf16[32,896]{1,0:T(8,128)(2,1)S(1)}, bf16[32,896]{1,0:T(8,128)(2,1)S(1)}, bf16[32,896]{1,0:T(8,128)(2,1)S(1)}, bf16[32,896]{1,0:T(8,128)(2,1)S(...) custom-call(f32[16,384]{1,0:T(8,128)S(1)} %collective-permute-done.refs_0_, ...), custom_call_target="tpu_custom_call" | custom-call | flops 15728640 | bytes 3145728 | tf_op jit(solution)/shard_map/pallas_call | solution.py:468
  18.1 2.9 %collective-permute-start.2 = (bf16[32,896]{1,0:T(8,128)(2,1)S(1)}, bf16[32,896]{1,0:T(8,128)(2,1)S(1)}, u32[]{:S(2)}, u32[]{:S(2)}) collective-permute-start(bf16[32,896]{1,0:T(8,128)(2,1)S(1)} %get-tuple-element.56), channel_id=1, source_target_pairs={{0,3},{1,2},{2,1},{3,0},{4,7},{5,6},{6,5},{7,4},{8,11},{9,10},{10,... | collective-permute-start | bytes 172040 | tf_op jit(solution)/shard_map/ppermute | solution.py:491
  21.0 0.3 %collective-permute-start.3 = (bf16[32,896]{1,0:T(8,128)(2,1)S(1)}, bf16[32,896]{1,0:T(8,128)(2,1)S(1)}, u32[]{:S(2)}, u32[]{:S(2)}) collective-permute-start(bf16[32,896]{1,0:T(8,128)(2,1)S(1)} %get-tuple-element.57), channel_id=1, source_target_pairs={{0,2},{1,3},{2,0},{3,1},{4,6},{5,7},{6,4},{7,5},{8,10},{9,11},{10,... | collective-permute-start | bytes 172040 | tf_op jit(solution)/shard_map/ppermute | solution.py:491
  21.4 0.0 collective-permute-done.5.refs_1_
  21.4 1.1 %collective-permute-start.4 = (bf16[32,896]{1,0:T(8,128)(2,1)S(1)}, bf16[32,896]{1,0:T(8,128)(2,1)S(1)}, u32[]{:S(2)}, u32[]{:S(2)}) collective-permute-start(bf16[32,896]{1,0:T(8,128)(2,1)S(1)} %get-tuple-element.58), channel_id=1, source_target_pairs={{0,1},{1,0},{2,3},{3,2},{4,5},{5,4},{6,7},{7,6},{8,9},{9,8},{10,11... | collective-permute-start | bytes 172040 | tf_op jit(solution)/shard_map/ppermute | solution.py:491
  22.5 0.0 collective-permute-done.6.refs_2_
  22.5 0.0 collective-permute-done.7.refs_3_
  22.5 0.8 %shard_map.88 = (bf16[1,32,4096]{2,1,0:T(8,128)(2,1)}, bf16[1,32,4096]{2,1,0:T(8,128)(2,1)}) custom-call(bf16[32,1280]{1,0:T(8,128)(2,1)S(1)} %get-tuple-element.60.refs_0_, bf16[32,1280]{1,0:T(8,128)(2,1)S(1)} %collective-permute-done.5.refs_1_, bf16[32,1280]{1,0:T(8,128)(2,1)S(1)} %collective-permute-done.6.refs_2_, ...), custom_call_target="tpu_custom_call" | custom-call | tf_op jit(solution)/shard_map/pallas_call | solution.py:513
  23.3 1.1 %collective-permute-done.2.refs_0_ = bf16[32,896]{1,0:T(8,128)(2,1)S(1)} collective-permute-done((bf16[32,896]{1,0:T(8,128)(2,1)S(1)}, bf16[32,896]{1,0:T(8,128)(2,1)S(1)}, u32[]{:S(2)}, u32[]{:S(2)}) %collective-permute-start.2) | collective-permute-done | bytes 57376 | tf_op jit(solution)/shard_map/ppermute | solution.py:491
  24.4 2.4 %collective-permute-done.3.refs_1_ = bf16[32,896]{1,0:T(8,128)(2,1)S(1)} collective-permute-done((bf16[32,896]{1,0:T(8,128)(2,1)S(1)}, bf16[32,896]{1,0:T(8,128)(2,1)S(1)}, u32[]{:S(2)}, u32[]{:S(2)}) %collective-permute-start.3) | collective-permute-done | bytes 57376 | tf_op jit(solution)/shard_map/ppermute | solution.py:491
  26.8 0.0 collective-permute-done.4.refs_2_
  26.8 0.7 %shard_map.89 = (bf16[1,32,4096]{2,1,0:T(8,128)(2,1)}, bf16[1,32,4096]{2,1,0:T(8,128)(2,1)}, f32[1,16,32]{2,1,0:T(8,128)}, f32[1,16,32]{2,1,0:T(8,128)}) custom-call(bf16[32,896]{1,0:T(8,128)(2,1)S(1)} %collective-permute-done.2.refs_0_, bf16[32,896]{1,0:T(8,128)(2,1)S(1)} %collective-permute-done.3.refs_1_, ...), custom_call_target="tpu_custom_call", output_to_operand_aliasing={{0}: (4, {}), {1}: (5, {})} | custom-call | tf_op jit(solution)/shard_map/pallas_call | solution.py:522
Async XLA Ops:
  0.6 3.3 %copy-start.1 = (bf16[1,128,1024]{2,1,0:T(8,128)(2,1)S(1)}, bf16[1,128,1024]{2,1,0:T(8,128)(2,1)}, u32[]{:S(2)}) copy-start(bf16[1,128,1024]{2,1,0:T(8,128)(2,1)} %refs_0_.3) | copy-start | bytes 786436
  0.6 3.3 %copy-start = (f32[1,128,1024]{2,1,0:T(8,128)S(1)}, f32[1,128,1024]{2,1,0:T(8,128)}, u32[]{:S(2)}) copy-start(f32[1,128,1024]{2,1,0:T(8,128)} %refs_1_.3) | copy-start | bytes 1572868
  0.7 3.3 %copy-start.3 = (bf16[1,128,16]{1,2,0:T(8,128)(2,1)S(1)}, bf16[1,128,16]{1,2,0:T(8,128)(2,1)}, u32[]{:S(2)}) copy-start(bf16[1,128,16]{1,2,0:T(8,128)(2,1)} %param.7) | copy-start | bytes 12292
  0.7 3.3 %copy-start.4 = (bf16[1,128,16]{1,2,0:T(8,128)(2,1)S(1)}, bf16[1,128,16]{1,2,0:T(8,128)(2,1)}, u32[]{:S(2)}) copy-start(bf16[1,128,16]{1,2,0:T(8,128)(2,1)} %param.8) | copy-start | bytes 12292
  0.7 3.3 %copy-start.2 = (bf16[1,128,1024]{2,1,0:T(8,128)(2,1)S(1)}, bf16[1,128,1024]{2,1,0:T(8,128)(2,1)}, u32[]{:S(2)}) copy-start(bf16[1,128,1024]{2,1,0:T(8,128)(2,1)} %refs_4_.3) | copy-start | bytes 786436
  3.3 1.6 %collective-permute-start.1 = (f32[16,640]{1,0:T(8,128)S(1)}, f32[16,640]{1,0:T(8,128)S(1)}, u32[]{:S(2)}, u32[]{:S(2)}) collective-permute-start(f32[16,640]{1,0:T(8,128)S(1)} %get-tuple-element.46), channel_id=1, source_target_pairs={{0,4},{4,0},{1,5},{5,1},{2,6},{6,2},{3,7},{7,3},{8,12},{12,8},{9,1... | collective-permute-start | bytes 122888 | tf_op jit(solution)/shard_map/ppermute | solution.py:498
  8.7 12.7 %collective-permute-start.5 = (bf16[32,1280]{1,0:T(8,128)(2,1)S(1)}, bf16[32,1280]{1,0:T(8,128)(2,1)S(1)}, u32[]{:S(2)}, u32[]{:S(2)}) collective-permute-start(bf16[32,1280]{1,0:T(8,128)(2,1)S(1)} %get-tuple-element.61), channel_id=1, source_target_pairs={{0,2},{1,3},{2,0},{3,1},{4,6},{5,7},{6,4},{7,5},{8,10},{9,11},{10,... | collective-permute-start | bytes 245768 | tf_op jit(solution)/shard_map/ppermute | solution.py:491
  12.5 1.6 %collective-permute-start = (f32[16,384]{1,0:T(8,128)S(1)}, f32[16,384]{1,0:T(8,128)S(1)}, u32[]{:S(2)}, u32[]{:S(2)}) collective-permute-start(f32[16,384]{1,0:T(8,128)S(1)} %get-tuple-element.39), channel_id=1, source_target_pairs={{0,4},{4,0},{1,5},{5,1},{2,6},{6,2},{3,7},{7,3},{8,12},{12,8},{9,1... | collective-permute-start | bytes 73736 | tf_op jit(solution)/shard_map/ppermute | solution.py:498
  12.5 10.0 %collective-permute-start.6 = (bf16[32,1280]{1,0:T(8,128)(2,1)S(1)}, bf16[32,1280]{1,0:T(8,128)(2,1)S(1)}, u32[]{:S(2)}, u32[]{:S(2)}) collective-permute-start(bf16[32,1280]{1,0:T(8,128)(2,1)S(1)} %get-tuple-element.62), channel_id=1, source_target_pairs={{0,3},{1,2},{2,1},{3,0},{4,7},{5,6},{6,5},{7,4},{8,11},{9,10},{10,... | collective-permute-start | bytes 245768 | tf_op jit(solution)/shard_map/ppermute | solution.py:491
  13.9 8.6 %collective-permute-start.7 = (bf16[32,1280]{1,0:T(8,128)(2,1)S(1)}, bf16[32,1280]{1,0:T(8,128)(2,1)S(1)}, u32[]{:S(2)}, u32[]{:S(2)}) collective-permute-start(bf16[32,1280]{1,0:T(8,128)(2,1)S(1)} %get-tuple-element.63), channel_id=1, source_target_pairs={{0,1},{1,0},{2,3},{3,2},{4,5},{5,4},{6,7},{7,6},{8,9},{9,8},{10,11... | collective-permute-start | bytes 245768 | tf_op jit(solution)/shard_map/ppermute | solution.py:491
  18.1 6.3 %collective-permute-start.2 = (bf16[32,896]{1,0:T(8,128)(2,1)S(1)}, bf16[32,896]{1,0:T(8,128)(2,1)S(1)}, u32[]{:S(2)}, u32[]{:S(2)}) collective-permute-start(bf16[32,896]{1,0:T(8,128)(2,1)S(1)} %get-tuple-element.56), channel_id=1, source_target_pairs={{0,3},{1,2},{2,1},{3,0},{4,7},{5,6},{6,5},{7,4},{8,11},{9,10},{10,... | collective-permute-start | bytes 172040 | tf_op jit(solution)/shard_map/ppermute | solution.py:491
  21.0 5.8 %collective-permute-start.3 = (bf16[32,896]{1,0:T(8,128)(2,1)S(1)}, bf16[32,896]{1,0:T(8,128)(2,1)S(1)}, u32[]{:S(2)}, u32[]{:S(2)}) collective-permute-start(bf16[32,896]{1,0:T(8,128)(2,1)S(1)} %get-tuple-element.57), channel_id=1, source_target_pairs={{0,2},{1,3},{2,0},{3,1},{4,6},{5,7},{6,4},{7,5},{8,10},{9,11},{10,... | collective-permute-start | bytes 172040 | tf_op jit(solution)/shard_map/ppermute | solution.py:491
  21.4 5.5 %collective-permute-start.4 = (bf16[32,896]{1,0:T(8,128)(2,1)S(1)}, bf16[32,896]{1,0:T(8,128)(2,1)S(1)}, u32[]{:S(2)}, u32[]{:S(2)}) collective-permute-start(bf16[32,896]{1,0:T(8,128)(2,1)S(1)} %get-tuple-element.58), channel_id=1, source_target_pairs={{0,1},{1,0},{2,3},{3,2},{4,5},{5,4},{6,7},{7,6},{8,9},{9,8},{10,11... | collective-permute-start | bytes 172040 | tf_op jit(solution)/shard_map/ppermute | solution.py:491

commit v6 on v5

--- a/solution.py
+++ b/solution.py
@@ -11,7 +11,7 @@
 LANES = 128
 SUB = 8
 UNROLL = 8
-FIRST_TILES = 5
+FIRST_TILES = 6
 EARLY = (0, 2, 3, 1)
 VMEM_LIMIT = 20 * 1024 * 1024
 

time: 27.7 us -> 28.8 us (1.040)
  waiting for transfers between devices: 3.58 us -> 4.36 us
  Pallas kernels: 12.8 us -> 13.1 us
    ppermute x2, waiting for transfers between devices: 0.06 us -> 1.44 us  [shards(): entry = lax.ppermute(end, 'ctx', [(0, 1), (1, 0)])]
    ppermute x6, waiting for transfers between devices: 3.52 us -> 2.92 us  [send(): return lax.ppermute(piece, 'head', [(s, s ^ d) for s in range(heads)])]
    pallas_call x2, Pallas kernels: 7.88 us -> 8.2 us  [second(): pl.pallas_call(functools.partial(second_kernel, onwards_here, last, heads...]
  transfers between devices with their start and end apart: 8 -> 8, of which waited for: 3 -> 4; matrix products, arithmetic and copies ran while one was open for 0% -> 0% of each run, Pallas kernels for 20% -> 16%
where the time goes in v6:
time: 28.8 us; the launch traced here: 28.7 us
  Pallas kernels  13.1 us (45%)
  starting transfers between devices  10.5 us (36%)
  waiting for transfers between devices  4.36 us (15%)
  between operations  0.72 us (2%)
    ppermute x6, starting transfers between devices, send(): return lax.ppermute(piece, 'head', [(s, s ^ d) for s in range(heads)])  9.65 us
    pallas_call x2, Pallas kernels, second(): pl.pallas_call(functools.partial(second_kernel, onwards_here, last, heads...  8.2 us
    pallas_call x2, Pallas kernels, first(): pl.pallas_call(functools.partial(first_kernel, sum(widths[:c]), width, ba...  3.31 us
    ppermute x6, waiting for transfers between devices, send(): return lax.ppermute(piece, 'head', [(s, s ^ d) for s in range(heads)])  2.92 us
    ppermute x2, waiting for transfers between devices, shards(): entry = lax.ppermute(end, 'ctx', [(0, 1), (1, 0)])  1.44 us
    ppermute x2, starting transfers between devices, shards(): entry = lax.ppermute(end, 'ctx', [(0, 1), (1, 0)])  0.84 us
    pallas_call x1, Pallas kernels, shards(): pl.pallas_call(functools.partial(early_kernel, channels, EARLY), in_specs...  0.83 us
    pallas_call x1, Pallas kernels, shards(): pl.pallas_call(functools.partial(late_kernel, heads, channels), in_specs=...  0.75 us
  transfers between devices with their start and end apart: 8, of which 4 were waited for; matrix products, arithmetic and copies ran while one was open for 0% of the time, Pallas kernels for 16%

profile of v6, /device:TPU:0, one launch (start us, length us, event | category | flops | bytes accessed | tf_op | source)
XLA Modules:
  0.0 28.7 jit_solution(4121118725488830333)
XLA Ops:
  0.6 0.0 copy-start.1
  0.6 0.0 copy-start
  0.7 0.0 copy-start.3
  0.7 0.0 copy-start.4
  0.7 0.0 copy-start.2
  0.7 2.7 %shard_map.84 = (f32[128,16,768]{2,1,0:T(8,128)S(1)}, f32[16,768]{1,0:T(8,128)S(1)}, f32[6,136,128]{2,1,0:T(8,128)S(1)}, f32[6,136,128]{2,1,0:T(8,128)S(1)}, f32...) custom-call(bf16[1,128,1024]{2,1,0:T(8,128)(2,1)} %refs_0_.3, ...), custom_call_target="tpu_custom_call" | custom-call | flops 7864320 | bytes 6291456 | tf_op jit(solution)/shard_map/pallas_call | solution.py:444
  3.4 0.8 %collective-permute-start.1 = (f32[16,768]{1,0:T(8,128)S(1)}, f32[16,768]{1,0:T(8,128)S(1)}, u32[]{:S(2)}, u32[]{:S(2)}) collective-permute-start(f32[16,768]{1,0:T(8,128)S(1)} %get-tuple-element.46), channel_id=1, source_target_pairs={{0,4},{4,0},{1,5},{5,1},{2,6},{6,2},{3,7},{7,3},{8,12},{12,8},{9,1... | collective-permute-start | bytes 147464 | tf_op jit(solution)/shard_map/ppermute | solution.py:498
  4.2 0.0 copy-done.1
  4.2 0.0 copy-done
  4.3 0.0 copy-done.3
  4.3 0.0 copy-done.4
  4.3 0.0 copy-done.2
  4.3 0.6 %shard_map.85 = (f32[128,16,256]{2,1,0:T(8,128)S(1)}, f32[16,256]{1,0:T(8,128)S(1)}, f32[2,136,128]{2,1,0:T(8,128)S(1)}, f32[2,136,128]{2,1,0:T(8,128)S(1)}, f32...) custom-call(bf16[1,128,1024]{2,1,0:T(8,128)(2,1)S(1)} %copy-done.1, ...), custom_call_target="tpu_custom_call" | custom-call | flops 2621440 | bytes 2097152 | tf_op jit(solution)/shard_map/pallas_call | solution.py:444
  4.9 0.3 collective-permute-done.1.refs_0_
  5.1 4.9 %shard_map.86 = (bf16[32,1536]{1,0:T(8,128)(2,1)S(1)}, bf16[32,1536]{1,0:T(8,128)(2,1)S(1)}, bf16[32,1536]{1,0:T(8,128)(2,1)S(1)}, bf16[32,1536]{1,0:T(8,128)(2,...) custom-call(f32[16,768]{1,0:T(8,128)S(1)} %collective-permute-done.1.refs_0_, ...), custom_call_target="tpu_custom_call" | custom-call | flops 31457280 | bytes 6291456 | tf_op jit(solution)/shard_map/pallas_call | solution.py:468
  10.1 3.7 %collective-permute-start.5 = (bf16[32,1536]{1,0:T(8,128)(2,1)S(1)}, bf16[32,1536]{1,0:T(8,128)(2,1)S(1)}, u32[]{:S(2)}, u32[]{:S(2)}) collective-permute-start(bf16[32,1536]{1,0:T(8,128)(2,1)S(1)} %get-tuple-element.61), channel_id=1, source_target_pairs={{0,2},{1,3},{2,0},{3,1},{4,6},{5,7},{6,4},{7,5},{8,10},{9,11},{10,... | collective-permute-start | bytes 294920 | tf_op jit(solution)/shard_map/ppermute | solution.py:491
  13.7 1.3 %collective-permute-start.6 = (bf16[32,1536]{1,0:T(8,128)(2,1)S(1)}, bf16[32,1536]{1,0:T(8,128)(2,1)S(1)}, u32[]{:S(2)}, u32[]{:S(2)}) collective-permute-start(bf16[32,1536]{1,0:T(8,128)(2,1)S(1)} %get-tuple-element.62), channel_id=1, source_target_pairs={{0,3},{1,2},{2,1},{3,0},{4,7},{5,6},{6,5},{7,4},{8,11},{9,10},{10,... | collective-permute-start | bytes 294920 | tf_op jit(solution)/shard_map/ppermute | solution.py:491
  15.1 0.2 collective-permute-start.7
  15.3 0.0 collective-permute-start
  15.3 1.2 %collective-permute-done.refs_0_ = f32[16,256]{1,0:T(8,128)S(1)} collective-permute-done((f32[16,256]{1,0:T(8,128)S(1)}, f32[16,256]{1,0:T(8,128)S(1)}, u32[]{:S(2)}, u32[]{:S(2)}) %collective-permute-start) | collective-permute-done | bytes 16416 | tf_op jit(solution)/shard_map/ppermute | solution.py:498
  16.5 3.3 %shard_map.87 = (bf16[32,640]{1,0:T(8,128)(2,1)S(1)}, bf16[32,640]{1,0:T(8,128)(2,1)S(1)}, bf16[32,640]{1,0:T(8,128)(2,1)S(1)}, bf16[32,640]{1,0:T(8,128)(2,1)S(...) custom-call(f32[16,256]{1,0:T(8,128)S(1)} %collective-permute-done.refs_0_, ...), custom_call_target="tpu_custom_call" | custom-call | flops 10485760 | bytes 2097152 | tf_op jit(solution)/shard_map/pallas_call | solution.py:468
  19.8 2.9 %collective-permute-start.2 = (bf16[32,640]{1,0:T(8,128)(2,1)S(1)}, bf16[32,640]{1,0:T(8,128)(2,1)S(1)}, u32[]{:S(2)}, u32[]{:S(2)}) collective-permute-start(bf16[32,640]{1,0:T(8,128)(2,1)S(1)} %get-tuple-element.56), channel_id=1, source_target_pairs={{0,3},{1,2},{2,1},{3,0},{4,7},{5,6},{6,5},{7,4},{8,11},{9,10},{10,... | collective-permute-start | bytes 122888 | tf_op jit(solution)/shard_map/ppermute | solution.py:491
  22.7 0.3 %collective-permute-start.3 = (bf16[32,640]{1,0:T(8,128)(2,1)S(1)}, bf16[32,640]{1,0:T(8,128)(2,1)S(1)}, u32[]{:S(2)}, u32[]{:S(2)}) collective-permute-start(bf16[32,640]{1,0:T(8,128)(2,1)S(1)} %get-tuple-element.57), channel_id=1, source_target_pairs={{0,2},{1,3},{2,0},{3,1},{4,6},{5,7},{6,4},{7,5},{8,10},{9,11},{10,... | collective-permute-start | bytes 122888 | tf_op jit(solution)/shard_map/ppermute | solution.py:491
  23.0 0.0 collective-permute-done.5.refs_1_
  23.0 1.1 %collective-permute-start.4 = (bf16[32,640]{1,0:T(8,128)(2,1)S(1)}, bf16[32,640]{1,0:T(8,128)(2,1)S(1)}, u32[]{:S(2)}, u32[]{:S(2)}) collective-permute-start(bf16[32,640]{1,0:T(8,128)(2,1)S(1)} %get-tuple-element.58), channel_id=1, source_target_pairs={{0,1},{1,0},{2,3},{3,2},{4,5},{5,4},{6,7},{7,6},{8,9},{9,8},{10,11... | collective-permute-start | bytes 122888 | tf_op jit(solution)/shard_map/ppermute | solution.py:491
  24.2 0.0 collective-permute-done.6.refs_2_
  24.2 0.0 collective-permute-done.7.refs_3_
  24.2 0.8 %shard_map.88 = (bf16[1,32,4096]{2,1,0:T(8,128)(2,1)}, bf16[1,32,4096]{2,1,0:T(8,128)(2,1)}) custom-call(bf16[32,1536]{1,0:T(8,128)(2,1)S(1)} %get-tuple-element.60.refs_0_, bf16[32,1536]{1,0:T(8,128)(2,1)S(1)} %collective-permute-done.5.refs_1_, bf16[32,1536]{1,0:T(8,128)(2,1)S(1)} %collective-permute-done.6.refs_2_, ...), custom_call_target="tpu_custom_call" | custom-call | tf_op jit(solution)/shard_map/pallas_call | solution.py:513
  25.0 0.6 %collective-permute-done.2.refs_0_ = bf16[32,640]{1,0:T(8,128)(2,1)S(1)} collective-permute-done((bf16[32,640]{1,0:T(8,128)(2,1)S(1)}, bf16[32,640]{1,0:T(8,128)(2,1)S(1)}, u32[]{:S(2)}, u32[]{:S(2)}) %collective-permute-start.2) | collective-permute-done | bytes 40992 | tf_op jit(solution)/shard_map/ppermute | solution.py:491
  25.6 2.3 %collective-permute-done.3.refs_1_ = bf16[32,640]{1,0:T(8,128)(2,1)S(1)} collective-permute-done((bf16[32,640]{1,0:T(8,128)(2,1)S(1)}, bf16[32,640]{1,0:T(8,128)(2,1)S(1)}, u32[]{:S(2)}, u32[]{:S(2)}) %collective-permute-start.3) | collective-permute-done | bytes 40992 | tf_op jit(solution)/shard_map/ppermute | solution.py:491
  27.9 0.0 collective-permute-done.4.refs_2_
  27.9 0.7 %shard_map.89 = (bf16[1,32,4096]{2,1,0:T(8,128)(2,1)}, bf16[1,32,4096]{2,1,0:T(8,128)(2,1)}, f32[1,16,32]{2,1,0:T(8,128)}, f32[1,16,32]{2,1,0:T(8,128)}) custom-call(bf16[32,640]{1,0:T(8,128)(2,1)S(1)} %collective-permute-done.2.refs_0_, bf16[32,640]{1,0:T(8,128)(2,1)S(1)} %collective-permute-done.3.refs_1_, ...), custom_call_target="tpu_custom_call", output_to_operand_aliasing={{0}: (4, {}), {1}: (5, {})} | custom-call | tf_op jit(solution)/shard_map/pallas_call | solution.py:522
Async XLA Ops:
  0.6 3.6 %copy-start.1 = (bf16[1,128,1024]{2,1,0:T(8,128)(2,1)S(1)}, bf16[1,128,1024]{2,1,0:T(8,128)(2,1)}, u32[]{:S(2)}) copy-start(bf16[1,128,1024]{2,1,0:T(8,128)(2,1)} %refs_0_.3) | copy-start | bytes 786436
  0.6 3.6 %copy-start = (f32[1,128,1024]{2,1,0:T(8,128)S(1)}, f32[1,128,1024]{2,1,0:T(8,128)}, u32[]{:S(2)}) copy-start(f32[1,128,1024]{2,1,0:T(8,128)} %refs_1_.3) | copy-start | bytes 1572868
  0.7 3.6 %copy-start.3 = (bf16[1,128,16]{1,2,0:T(8,128)(2,1)S(1)}, bf16[1,128,16]{1,2,0:T(8,128)(2,1)}, u32[]{:S(2)}) copy-start(bf16[1,128,16]{1,2,0:T(8,128)(2,1)} %param.7) | copy-start | bytes 12292
  0.7 3.6 %copy-start.4 = (bf16[1,128,16]{1,2,0:T(8,128)(2,1)S(1)}, bf16[1,128,16]{1,2,0:T(8,128)(2,1)}, u32[]{:S(2)}) copy-start(bf16[1,128,16]{1,2,0:T(8,128)(2,1)} %param.8) | copy-start | bytes 12292
  0.7 3.6 %copy-start.2 = (bf16[1,128,1024]{2,1,0:T(8,128)(2,1)S(1)}, bf16[1,128,1024]{2,1,0:T(8,128)(2,1)}, u32[]{:S(2)}) copy-start(bf16[1,128,1024]{2,1,0:T(8,128)(2,1)} %refs_4_.3) | copy-start | bytes 786436
  3.4 1.7 %collective-permute-start.1 = (f32[16,768]{1,0:T(8,128)S(1)}, f32[16,768]{1,0:T(8,128)S(1)}, u32[]{:S(2)}, u32[]{:S(2)}) collective-permute-start(f32[16,768]{1,0:T(8,128)S(1)} %get-tuple-element.46), channel_id=1, source_target_pairs={{0,4},{4,0},{1,5},{5,1},{2,6},{6,2},{3,7},{7,3},{8,12},{12,8},{9,1... | collective-permute-start | bytes 147464 | tf_op jit(solution)/shard_map/ppermute | solution.py:498
  10.1 13.0 %collective-permute-start.5 = (bf16[32,1536]{1,0:T(8,128)(2,1)S(1)}, bf16[32,1536]{1,0:T(8,128)(2,1)S(1)}, u32[]{:S(2)}, u32[]{:S(2)}) collective-permute-start(bf16[32,1536]{1,0:T(8,128)(2,1)S(1)} %get-tuple-element.61), channel_id=1, source_target_pairs={{0,2},{1,3},{2,0},{3,1},{4,6},{5,7},{6,4},{7,5},{8,10},{9,11},{10,... | collective-permute-start | bytes 294920 | tf_op jit(solution)/shard_map/ppermute | solution.py:491
  13.7 10.4 %collective-permute-start.6 = (bf16[32,1536]{1,0:T(8,128)(2,1)S(1)}, bf16[32,1536]{1,0:T(8,128)(2,1)S(1)}, u32[]{:S(2)}, u32[]{:S(2)}) collective-permute-start(bf16[32,1536]{1,0:T(8,128)(2,1)S(1)} %get-tuple-element.62), channel_id=1, source_target_pairs={{0,3},{1,2},{2,1},{3,0},{4,7},{5,6},{6,5},{7,4},{8,11},{9,10},{10,... | collective-permute-start | bytes 294920 | tf_op jit(solution)/shard_map/ppermute | solution.py:491
  15.1 9.1 %collective-permute-start.7 = (bf16[32,1536]{1,0:T(8,128)(2,1)S(1)}, bf16[32,1536]{1,0:T(8,128)(2,1)S(1)}, u32[]{:S(2)}, u32[]{:S(2)}) collective-permute-start(bf16[32,1536]{1,0:T(8,128)(2,1)S(1)} %get-tuple-element.63), channel_id=1, source_target_pairs={{0,1},{1,0},{2,3},{3,2},{4,5},{5,4},{6,7},{7,6},{8,9},{9,8},{10,11... | collective-permute-start | bytes 294920 | tf_op jit(solution)/shard_map/ppermute | solution.py:491
  15.3 1.2 %collective-permute-start = (f32[16,256]{1,0:T(8,128)S(1)}, f32[16,256]{1,0:T(8,128)S(1)}, u32[]{:S(2)}, u32[]{:S(2)}) collective-permute-start(f32[16,256]{1,0:T(8,128)S(1)} %get-tuple-element.39), channel_id=1, source_target_pairs={{0,4},{4,0},{1,5},{5,1},{2,6},{6,2},{3,7},{7,3},{8,12},{12,8},{9,1... | collective-permute-start | bytes 49160 | tf_op jit(solution)/shard_map/ppermute | solution.py:498
  19.8 5.8 %collective-permute-start.2 = (bf16[32,640]{1,0:T(8,128)(2,1)S(1)}, bf16[32,640]{1,0:T(8,128)(2,1)S(1)}, u32[]{:S(2)}, u32[]{:S(2)}) collective-permute-start(bf16[32,640]{1,0:T(8,128)(2,1)S(1)} %get-tuple-element.56), channel_id=1, source_target_pairs={{0,3},{1,2},{2,1},{3,0},{4,7},{5,6},{6,5},{7,4},{8,11},{9,10},{10,... | collective-permute-start | bytes 122888 | tf_op jit(solution)/shard_map/ppermute | solution.py:491
  22.7 5.2 %collective-permute-start.3 = (bf16[32,640]{1,0:T(8,128)(2,1)S(1)}, bf16[32,640]{1,0:T(8,128)(2,1)S(1)}, u32[]{:S(2)}, u32[]{:S(2)}) collective-permute-start(bf16[32,640]{1,0:T(8,128)(2,1)S(1)} %get-tuple-element.57), channel_id=1, source_target_pairs={{0,2},{1,3},{2,0},{3,1},{4,6},{5,7},{6,4},{7,5},{8,10},{9,11},{10,... | collective-permute-start | bytes 122888 | tf_op jit(solution)/shard_map/ppermute | solution.py:491
  23.0 4.9 %collective-permute-start.4 = (bf16[32,640]{1,0:T(8,128)(2,1)S(1)}, bf16[32,640]{1,0:T(8,128)(2,1)S(1)}, u32[]{:S(2)}, u32[]{:S(2)}) collective-permute-start(bf16[32,640]{1,0:T(8,128)(2,1)S(1)} %get-tuple-element.58), channel_id=1, source_target_pairs={{0,1},{1,0},{2,3},{3,2},{4,5},{5,4},{6,7},{7,6},{8,9},{9,8},{10,11... | collective-permute-start | bytes 122888 | tf_op jit(solution)/shard_map/ppermute | solution.py:491
